TPU v7x, 32 devices: a whole 2x2x4 slice. The times are simulated.
32 devices in a mesh: dom: 16 (over z, y, x), grp: 2 (over core).
Axes of the slice: x: 2, y: 2, z: 4, core: 2. Of those that a mesh axis runs over, the one named last changes fastest.
Arguments:
- source: float32 [512, 64, 128], P('dom', 'grp'), may hold values from -48 to 48
- conductivity: float32 [512, 64, 128], P('dom', 'grp'), may hold values from 0.3 to 3
- absorption: float32 [512, 64, 128], P('dom', 'grp'), may hold values from 0.1 to 2
- brick_mask: int32 [64, 8, 16], P('dom', 'grp'), may hold values 0 or 1
Outputs:
- fine_iterate: float32 [512, 64, 128], P('dom', 'grp')
- fine_residual: float32 [512, 64, 128], P('dom', 'grp')
- mid_iterate: float32 [256, 32, 64], P('dom', 'grp')
- coarse_iterate: float32 [128, 16, 32], P('dom', 'grp')
All inputs are finite; a program needn't handle non-finite values. No bound on the sum of `brick_mask` on one device may be relied on, other than what follows from the above.
Results may differ from a plain program's by a relative error of at most 0.00002.
Values sent between devices are 32-bit elements; how exact they have to be, the bound alone decides.
No kernel may reach another device: no remote copies, remote signals or barrier semaphores. Data moves between devices by JAX's collectives and lax.ppermute only.
A program may use at most 192 MiB of HBM per device.

v0:
```python
import jax
import jax.numpy as jnp
from jax import lax
from jax.sharding import PartitionSpec as P

DEGREE = 4
COARSE_DEGREE = 6


step_scale = 4.0
smooth_low = 0.3
smooth_high = 2.0
coarse_low = 0.05


def extended_2(array, sides, width):
    for axis, dim in sides:
        devices, length = (lax.axis_size(axis), array.shape[dim])
        up = [(i, (i + 1) % devices) for i in range(devices - 1)]
        down = [(j, i) for i, j in up]
        last = lax.slice_in_dim(array, length - width, length, axis=dim)
        leading = lax.slice_in_dim(array, 0, width, axis=dim)
        before = lax.ppermute(last, axis, up)
        after = lax.ppermute(leading, axis, down)
        array = jnp.concatenate([before, array, after], axis=dim)
    return array


def refine_mask(brick_flags):
    values = brick_flags.astype(jnp.float32)
    values = jnp.repeat(values, 8, axis=0)
    values = jnp.repeat(values, 8, axis=1)
    return jnp.repeat(values, 8, axis=2)


def six_views(padded):
    return [
        padded[2:, 1:-1, 1:-1],
        padded[:-2, 1:-1, 1:-1],
        padded[1:-1, 2:, 1:-1],
        padded[1:-1, :-2, 1:-1],
        padded[1:-1, 1:-1, 2:],
        padded[1:-1, 1:-1, :-2],
    ]


def coefficients(kappa_pad, filled_pad, absorb_cells, factor):
    kappa_mid = kappa_pad[1:-1, 1:-1, 1:-1]
    weights = []
    summed = jnp.zeros_like(kappa_mid)
    counted = jnp.zeros_like(kappa_mid)
    for neighbour_kappa, neighbour_filled in zip(six_views(kappa_pad), six_views(filled_pad)):
        weight = factor * 0.5 * (kappa_mid + neighbour_kappa) * neighbour_filled
        weights.append(weight)
        summed = summed + weight
        counted = counted + neighbour_filled
    diagonal = 1.0 + summed + factor * absorb_cells * (6.0 - counted)
    return (weights, diagonal)


def apply_padded(field_pad, weights, diagonal, filled):
    center = field_pad[1:-1, 1:-1, 1:-1]
    neighbours = six_views(field_pad)
    coupled = weights[0] * neighbours[0]
    for index in range(1, 6):
        coupled = coupled + weights[index] * neighbours[index]
    return filled * (diagonal * center - coupled) + (1.0 - filled) * center


def chebyshev(source_term, diagonal, degree, lowest, highest, operate, keep_residual):
    middle = (highest + lowest) / 2.0
    spread = (highest - lowest) / 2.0
    relative = middle / spread
    factor_prev = 1.0 / relative
    inverse = 1.0 / diagonal
    update = inverse * source_term / middle
    iterate = update
    residual = source_term
    for sweep_index in range(degree):
        if sweep_index > 0:
            factor_next = 1.0 / (2.0 * relative - factor_prev)
            update = factor_next * factor_prev * update + 2.0 * factor_next / spread * (
                inverse * residual
            )
            iterate = iterate + update
            factor_prev = factor_next
        if sweep_index < degree - 1 or keep_residual:
            residual = residual - operate(update)
    return (iterate, residual)


def coarsen(fields):
    shape_in = fields.shape
    blocks = fields.reshape(shape_in[0] // 2, 2, shape_in[1] // 2, 2, shape_in[2] // 2, 2)
    return jnp.mean(blocks, axis=(1, 3, 5))


def pad_depth(fields):
    return jnp.pad(fields, [(0, 0)] * (fields.ndim - 1) + [(1, 1)])


def margin_solve(extended, factor, degree, lowest, keep_residual, width):
    ext_pad = jnp.pad(extended, ((0, 0), (1, 1), (1, 1), (1, 1)))
    ext_filled = extended[3]
    weights, diagonal = coefficients(ext_pad[1], ext_pad[3], extended[2], factor)

    def operate(vector):
        return apply_padded(jnp.pad(vector, 1), weights, diagonal, ext_filled)

    long_iterate, long_residual = chebyshev(
        extended[0], diagonal, degree, lowest, smooth_high, operate, keep_residual
    )
    return (
        long_iterate[width:-width, width:-width, :],
        long_residual[width:-width, width:-width, :],
    )


def body(source, conductivity, absorption, brick_mask):
    filled = refine_mask(brick_mask)
    masked = source * filled
    coef_pad = pad_depth(extended_2(jnp.stack([conductivity, filled]), (("dom", 1), ("grp", 2)), 1))
    fine_weights, fine_diagonal = coefficients(coef_pad[0], coef_pad[1], absorption, step_scale)

    def fine_operate(vector):
        padded = pad_depth(extended_2(vector, (("dom", 0), ("grp", 1)), 1))
        return apply_padded(padded, fine_weights, fine_diagonal, filled)

    fine_iterate, fine_residual = chebyshev(
        masked, fine_diagonal, DEGREE, smooth_low, smooth_high, fine_operate, True
    )
    mid_kappa = coarsen(conductivity)
    mid_absorb = coarsen(absorption)
    mid_filled = coarsen(filled)
    mid_source = coarsen(fine_residual)
    coarse_kappa = coarsen(mid_kappa)
    coarse_absorb = coarsen(mid_absorb)
    coarse_filled = coarsen(mid_filled)
    coarse_factor = step_scale / 16.0
    mid_width = DEGREE + 1
    mid_ext = extended_2(
        jnp.stack([mid_source, mid_kappa, mid_absorb, mid_filled]),
        (("dom", 1), ("grp", 2)),
        mid_width,
    )
    mid_iterate, mid_residual = margin_solve(
        mid_ext, step_scale / 4.0, DEGREE, smooth_low, True, mid_width
    )
    coarse_width = COARSE_DEGREE
    coarse_ext = extended_2(
        jnp.stack([coarsen(mid_residual), coarse_kappa, coarse_absorb, coarse_filled]),
        (("dom", 1), ("grp", 2)),
        coarse_width,
    )
    coarse_iterate = margin_solve(
        coarse_ext, coarse_factor, COARSE_DEGREE, coarse_low, False, coarse_width
    )[0]
    return (fine_iterate, fine_residual, mid_iterate, coarse_iterate)


def solution(mesh):
    return jax.shard_map(
        body,
        mesh=mesh,
        in_specs=(
            P("dom", "grp", None),
            P("dom", "grp", None),
            P("dom", "grp", None),
            P("dom", "grp", None),
        ),
        out_specs=(
            P("dom", "grp", None),
            P("dom", "grp", None),
            P("dom", "grp", None),
            P("dom", "grp", None),
        ),
        check_vma=False,
    )
```

profile of v0, /device:TPU:19, one launch (start us, length us, event | category | flops | bytes accessed | tf_op | source)
XLA Modules:
  0.0 332.0 jit_solution(16223984009827309389)
XLA Ops:
  1.6 2.5 broadcast_bitcast_fusion
  4.1 2.2 copy.165
  6.4 3.1 collective-permute-start
  9.5 2.2 collective-permute-start.1
  11.7 3.4 %collective-permute-done.1 = f32[2,1,32,128]{3,2,1,0:T(8,128)S(1)} collective-permute-done((f32[2,1,32,128]{3,2,1,0:T(8,128)S(1)}, f32[2,1,32,128]{3,2,1,0:T(8,128)S(1)}, u32[]{:S(2)}, u32[]{:S(2)}) %collective-permute-start.1) | collective-permute-done | bytes 32800 | tf_op jit(solution)/shard_map/ppermute | solution.py:24
  15.1 4.0 %collective-permute-start.3 = (f32[2,34,1,128]{3,0,2,1:T(2,128)S(1)}, f32[2,34,1,128]{3,0,2,1:T(2,128)S(1)}, u32[]{:S(2)}, u32[]{:S(2)}) collective-permute-start(f32[2,34,1,128]{3,0,2,1:T(2,128)S(1)} %copy.178), channel_id=1, source_target_pairs={{1,0},{3,2},{5,4},{7,6},{9,8},{11,10},{13,12},{15,14},{17,16},{19,... | collective-permute-start | bytes 104456 | tf_op jit(solution)/shard_map/ppermute | solution.py:24
  19.2 1.3 collective-permute-start.2
  20.5 2.2 copy.170
  22.8 2.5 select_maximum_fusion
  26.5 1.6 multiply_multiply_fusion
  28.1 2.2 collective-permute-start.5
  30.3 3.1 collective-permute-start.4
  33.4 3.0 collective-permute-done.4
  36.4 1.3 collective-permute-start.7
  37.7 4.2 %collective-permute-start.6 = (f32[34,1,128]{2,1,0:T(1,128)S(1)}, f32[34,1,128]{2,1,0:T(1,128)S(1)}, u32[]{:S(2)}, u32[]{:S(2)}) collective-permute-start(f32[34,1,128]{2,1,0:T(1,128)S(1)} %get-tuple-element.85), channel_id=1, source_target_pairs={{1,0},{3,2},{5,4},{7,6},{9,8},{11,10},{13,12},{15,14},{17,16},{19,... | collective-permute-start | bytes 52232 | tf_op jit(solution)/shard_map/ppermute | solution.py:24
  43.3 1.7 multiply_add_fusion.2
  45.0 3.6 %collective-permute-start.9 = (f32[1,32,128]{2,1,0:T(8,128)S(1)}, f32[1,32,128]{2,1,0:T(8,128)S(1)}, u32[]{:S(2)}, u32[]{:S(2)}) collective-permute-start(f32[1,32,128]{2,1,0:T(8,128)S(1)} %get-tuple-element.92), channel_id=1, source_target_pairs={{0,2},{2,4},{4,6},{6,8},{8,10},{10,12},{12,14},{14,16},{16,18},{18... | collective-permute-start | bytes 49160 | tf_op jit(solution)/shard_map/ppermute | solution.py:23
  48.6 1.9 collective-permute-start.8
  50.6 3.4 %collective-permute-done.8 = f32[1,32,128]{2,1,0:T(8,128)S(1)} collective-permute-done((f32[1,32,128]{2,1,0:T(8,128)S(1)}, f32[1,32,128]{2,1,0:T(8,128)S(1)}, u32[]{:S(2)}, u32[]{:S(2)}) %collective-permute-start.8) | collective-permute-done | bytes 16416 | tf_op jit(solution)/shard_map/ppermute | solution.py:24
  54.1 1.3 collective-permute-start.11
  55.4 3.7 %collective-permute-start.10 = (f32[34,1,128]{2,1,0:T(1,128)S(1)}, f32[34,1,128]{2,1,0:T(1,128)S(1)}, u32[]{:S(2)}, u32[]{:S(2)}) collective-permute-start(f32[34,1,128]{2,1,0:T(1,128)S(1)} %get-tuple-element.83), channel_id=1, source_target_pairs={{1,0},{3,2},{5,4},{7,6},{9,8},{11,10},{13,12},{15,14},{17,16},{19,... | collective-permute-start | bytes 52232 | tf_op jit(solution)/shard_map/ppermute | solution.py:24
  59.1 4.6 %broadcast_in_dim.18 = f32[32,32,16,4]{3,2,1,0:T(8,128)} broadcast(f32[32,32,16]{2,1,0:T(8,128)S(1)} %copy-done.24), dimensions={0,1,2} | broadcast | bytes 327680 | tf_op jit(solution)/shard_map/broadcast_in_dim | solution.py:33
  63.7 6.7 %broadcast_in_dim.19 = f32[16,2,16,2,64]{4,3,2,1,0:T(2,128)S(1)} reshape(f32[32,32,16,4]{3,2,1,0:T(8,128)} %broadcast_in_dim.18) | data formatting | bytes 524288 | tf_op jit(solution)/shard_map/broadcast_in_dim | solution.py:33
  73.2 2.5 collective-permute-start.13
  75.7 2.9 collective-permute-start.12
  79.4 35.6 %reshape.121 = f32[16,2,16,2,64,2]{5,4,3,2,1,0:T(8,128)} reshape(f32[32,32,128]{2,1,0:T(8,128)} %param.6) | data formatting | bytes 1048576 | tf_op jit(solution)/shard_map/reshape | solution.py:94
  115.0 12.2 %reduce_sum.74 = f32[16,16,64]{2,1,0:T(8,128)S(1)} reduce(f32[16,2,16,2,64,2]{5,4,3,2,1,0:T(8,128)} %reshape.121, f32[]{:T(128)} %constant.27.clone.1), dimensions={1,3,5}, to_apply=%region_2.3 | reduce | flops 114688 | bytes 589828 | tf_op jit(solution)/shard_map/reduce_sum | solution.py:95
  127.9 1.3 collective-permute-start.15
  129.2 4.2 %collective-permute-start.14 = (f32[34,1,128]{2,1,0:T(1,128)}, f32[34,1,128]{2,1,0:T(1,128)}, u32[]{:S(2)}, u32[]{:S(2)}) collective-permute-start(f32[34,1,128]{2,1,0:T(1,128)} %get-tuple-element.81), channel_id=1, source_target_pairs={{1,0},{3,2},{5,4},{7,6},{9,8},{11,10},{13,12},{15,14},{17,16},{19,... | collective-permute-start | bytes 52232 | tf_op jit(solution)/shard_map/ppermute | solution.py:24
  133.4 1.6 broadcast_multiply_fusion
  135.0 35.6 %reshape.120 = f32[16,2,16,2,64,2]{5,4,3,2,1,0:T(8,128)} reshape(f32[32,32,128]{2,1,0:T(8,128)} %param.5) | data formatting | bytes 1048576 | tf_op jit(solution)/shard_map/reshape | solution.py:94
  170.6 12.9 %reduce_sum.73 = f32[16,16,64]{2,1,0:T(8,128)} reduce(f32[16,2,16,2,64,2]{5,4,3,2,1,0:T(8,128)} %reshape.120, f32[]{:T(128)} %constant.27.clone.1), dimensions={1,3,5}, to_apply=%region_1.2 | reduce | flops 114688 | bytes 589828 | tf_op jit(solution)/shard_map/reduce_sum | solution.py:95
  183.5 1.4 select_maximum_fusion.9
  185.0 4.5 %multiply_add_fusion = (f32[32,32,128]{2,1,0:T(8,128)S(1)}, f32[32,32,128]{2,1,0:T(8,128)}) fusion(f32[32,32,128]{2,1,0:T(8,128)S(1)} %multiply_add_fusion.1, f32[32,32,128]{2,1,0:T(8,128)S(1)} %get-tuple-element.55, f32[32,32,128]{2,1,0:T(8,128)S(1)} %copy.170, f32[32,32,128]{2,1,0:T(8,128)} %copy-done.12, f32[34,34,130]{2,1,0:T(8,128)S(1)} %select_maximum_fusion.9, ...), kind=kLoop, calls=%fused_computation.149 | loop fusion | flops 7340032 | bytes 9048064 | tf_op jit(solution)/shard_map/add | solution.py:82
  191.0 3.4 %collective-permute-start.17 = (f32[1,32,128]{2,1,0:T(8,128)}, f32[1,32,128]{2,1,0:T(8,128)S(1)}, u32[]{:S(2)}, u32[]{:S(2)}) collective-permute-start(f32[1,32,128]{2,1,0:T(8,128)} %get-tuple-element.88), channel_id=1, source_target_pairs={{0,2},{2,4},{4,6},{6,8},{8,10},{10,12},{12,14},{14,16},{16,18},{18... | collective-permute-start | bytes 49160 | tf_op jit(solution)/shard_map/ppermute | solution.py:23
  194.4 1.9 collective-permute-start.16
  196.4 5.7 %div.89 = f32[8,2,8,2,32,2]{5,4,3,2,1,0:T(8,128)} reshape(f32[16,16,64]{2,1,0:T(8,128)S(1)} %get-tuple-element.107) | data formatting | bytes 131072 | tf_op jit(solution)/shard_map/div | solution.py:95
  202.1 3.2 reduce_sum.77
  205.4 1.3 pad_maximum_fusion.47
  206.7 1.3 collective-permute-start.19
  208.0 4.2 %collective-permute-start.18 = (f32[34,1,128]{2,1,0:T(1,128)}, f32[34,1,128]{2,1,0:T(1,128)}, u32[]{:S(2)}, u32[]{:S(2)}) collective-permute-start(f32[34,1,128]{2,1,0:T(1,128)} %get-tuple-element.79), channel_id=1, source_target_pairs={{1,0},{3,2},{5,4},{7,6},{9,8},{11,10},{13,12},{15,14},{17,16},{19,... | collective-permute-start | bytes 52232 | tf_op jit(solution)/shard_map/ppermute | solution.py:24
  212.2 1.4 multiply_bitcast_fusion.3
  213.6 6.5 %div.95 = f32[8,2,8,2,32,2]{5,4,3,2,1,0:T(8,128)} reshape(f32[16,16,64]{2,1,0:T(8,128)} %get-tuple-element.111) | data formatting | bytes 131072 | tf_op jit(solution)/shard_map/div | solution.py:95
  220.1 3.2 reduce_sum.79
  223.3 1.8 select_maximum_fusion.5
  225.1 4.3 %fusion.6 = f32[32,32,128]{2,1,0:T(8,128)} fusion(f32[32,32,128]{2,1,0:T(8,128)} %get-tuple-element.51, f32[32,32,128]{2,1,0:T(8,128)S(1)} %copy.170, f32[32,32,128]{2,1,0:T(8,128)} %copy-done.12, f32[34,34,130]{2,1,0:T(8,128)S(1)} %select_maximum_fusion.5, f32[32,32,128]{2,1,0:T(8,128)S(1)} %copy-done.11, f32[32,32,128]{2,1,0:T(8,128)S(1)} %copy-done.7, ...), kind=kLoop, calls=%fused_computation.43 | loop fusion | flops 3407872 | bytes 6883328 | tf_op jit(solution)/shard_map/sub | solution.py:88
  229.4 35.6 %reshape.119 = f32[16,2,16,2,64,2]{5,4,3,2,1,0:T(8,128)} reshape(f32[32,32,128]{2,1,0:T(8,128)} %fusion.6) | data formatting | bytes 1048576 | tf_op jit(solution)/shard_map/reshape | solution.py:94
  265.0 12.3 %reduce_sum.72 = f32[16,16,64]{2,1,0:T(8,128)S(1)} reduce(f32[16,2,16,2,64,2]{5,4,3,2,1,0:T(8,128)} %reshape.119, f32[]{:T(128)} %constant.27.clone.1), dimensions={1,3,5}, to_apply=%region_0.1 | reduce | flops 114688 | bytes 589828 | tf_op jit(solution)/shard_map/reduce_sum | solution.py:95
  277.3 4.3 %collective-permute-start.20 = (f32[4,5,16,64]{3,2,1,0:T(8,128)S(1)}, f32[4,5,16,64]{3,2,1,0:T(8,128)S(1)}, u32[]{:S(2)}, u32[]{:S(2)}) collective-permute-start(f32[4,5,16,64]{3,2,1,0:T(8,128)S(1)} %get-tuple-element.86), channel_id=1, source_target_pairs={{0,2},{2,4},{4,6},{6,8},{8,10},{10,12},{12,14},{14,16},{16,18},{18... | collective-permute-start | bytes 245768 | tf_op jit(solution)/shard_map/ppermute | solution.py:23
  281.6 2.1 collective-permute-start.21
  283.8 5.7 %div.92 = f32[8,2,8,2,32,2]{5,4,3,2,1,0:T(8,128)} reshape(f32[16,16,64]{2,1,0:T(8,128)S(1)} %copy-done.29) | data formatting | bytes 131072 | tf_op jit(solution)/shard_map/div | solution.py:95
  289.5 2.6 reduce_sum.78
  292.2 1.3 collective-permute-start.22
  293.5 3.3 %collective-permute-start.23 = (f32[4,26,5,64]{3,2,1,0:T(8,128)S(1)}, f32[4,26,5,64]{3,2,1,0:T(8,128)S(1)}, u32[]{:S(2)}, u32[]{:S(2)}) collective-permute-start(f32[4,26,5,64]{3,2,1,0:T(8,128)S(1)} %get-tuple-element.77), channel_id=1, source_target_pairs={{1,0},{3,2},{5,4},{7,6},{9,8},{11,10},{13,12},{15,14},{17,16},{19,... | collective-permute-start | bytes 399368 | tf_op jit(solution)/shard_map/ppermute | solution.py:24
  296.9 1.1 collective-permute-done.23
  298.6 1.3 fusion.105
  303.3 5.7 %reshape.122 = f32[8,2,8,2,32,2]{5,4,3,2,1,0:T(8,128)} reshape(f32[16,16,64]{2,1,0:T(8,128)S(1)} %get-tuple-element.96) | data formatting | bytes 131072 | tf_op jit(solution)/shard_map/reshape | solution.py:94
  309.0 2.6 reduce_sum.76
  311.7 4.2 %collective-permute-start.24 = (f32[4,6,8,32]{3,2,1,0:T(8,128)S(1)}, f32[4,6,8,32]{3,2,1,0:T(8,128)S(1)}, u32[]{:S(2)}, u32[]{:S(2)}) collective-permute-start(f32[4,6,8,32]{3,2,1,0:T(8,128)S(1)} %get-tuple-element.105), channel_id=1, source_target_pairs={{0,2},{2,4},{4,6},{6,8},{8,10},{10,12},{12,14},{14,16},{16,18},{18... | collective-permute-start | bytes 73736 | tf_op jit(solution)/shard_map/ppermute | solution.py:23
  315.9 3.0 collective-permute-start.25
  319.8 2.3 collective-permute-done.25
  322.2 1.3 collective-permute-start.26
  323.5 3.7 %collective-permute-start.27 = (f32[4,20,6,32]{3,2,1,0:T(8,128)S(1)}, f32[4,20,6,32]{3,2,1,0:T(8,128)S(1)}, u32[]{:S(2)}, u32[]{:S(2)}) collective-permute-start(f32[4,20,6,32]{3,2,1,0:T(8,128)S(1)} %get-tuple-element.102), channel_id=1, source_target_pairs={{1,0},{3,2},{5,4},{7,6},{9,8},{11,10},{13,12},{15,14},{17,16},{19,... | collective-permute-start | bytes 184328 | tf_op jit(solution)/shard_map/ppermute | solution.py:24
  327.3 1.1 add_add_fusion
  (158 shorter events, 18.3 us)
Async XLA Ops:
  1.4 2.7 copy-start.23
  4.1 2.2 copy-start.17
  6.4 5.3 %collective-permute-start = (f32[2,1,32,128]{3,2,1,0:T(8,128)S(1)}, f32[2,1,32,128]{3,2,1,0:T(8,128)S(1)}, u32[]{:S(2)}, u32[]{:S(2)}) collective-permute-start(f32[2,1,32,128]{3,2,1,0:T(8,128)S(1)} %get-tuple-element.72), channel_id=1, source_target_pairs={{0,2},{2,4},{4,6},{6,8},{8,10},{10,12},{12,14},{14,16},{16,18},{18... | collective-permute-start | bytes 98312 | tf_op jit(solution)/shard_map/ppermute | solution.py:23
  9.5 5.6 %collective-permute-start.1 = (f32[2,1,32,128]{3,2,1,0:T(8,128)S(1)}, f32[2,1,32,128]{3,2,1,0:T(8,128)S(1)}, u32[]{:S(2)}, u32[]{:S(2)}) collective-permute-start(f32[2,1,32,128]{3,2,1,0:T(8,128)S(1)} %get-tuple-element.73), channel_id=1, source_target_pairs={{2,0},{4,2},{6,4},{8,6},{10,8},{12,10},{14,12},{16,14},{18,16},{20... | collective-permute-start | bytes 98312 | tf_op jit(solution)/shard_map/ppermute | solution.py:24
  15.1 7.5 %collective-permute-start.3 = (f32[2,34,1,128]{3,0,2,1:T(2,128)S(1)}, f32[2,34,1,128]{3,0,2,1:T(2,128)S(1)}, u32[]{:S(2)}, u32[]{:S(2)}) collective-permute-start(f32[2,34,1,128]{3,0,2,1:T(2,128)S(1)} %copy.178), channel_id=1, source_target_pairs={{1,0},{3,2},{5,4},{7,6},{9,8},{11,10},{13,12},{15,14},{17,16},{19,... | collective-permute-start | bytes 104456 | tf_op jit(solution)/shard_map/ppermute | solution.py:24
  19.2 3.5 %collective-permute-start.2 = (f32[2,34,1,128]{3,0,2,1:T(2,128)S(1)}, f32[2,34,1,128]{3,0,2,1:T(2,128)S(1)}, u32[]{:S(2)}, u32[]{:S(2)}) collective-permute-start(f32[2,34,1,128]{3,0,2,1:T(2,128)S(1)} %copy.177), channel_id=1, source_target_pairs={{0,1},{2,3},{4,5},{6,7},{8,9},{10,11},{12,13},{14,15},{16,17},{18,... | collective-permute-start | bytes 104456 | tf_op jit(solution)/shard_map/ppermute | solution.py:23
  28.0 16.9 %copy-start = (f32[32,32,128]{2,1,0:T(8,128)}, f32[32,32,128]{2,1,0:T(8,128)S(1)}, u32[]{:S(2)}) copy-start(f32[32,32,128]{2,1,0:T(8,128)S(1)} %get-tuple-element.58) | copy-start | bytes 1572868
  28.1 16.9 %copy-start.4 = (f32[32,32,128]{2,1,0:T(8,128)}, f32[32,32,128]{2,1,0:T(8,128)S(1)}, u32[]{:S(2)}) copy-start(f32[32,32,128]{2,1,0:T(8,128)S(1)} %get-tuple-element.59) | copy-start | bytes 1572868
  28.1 16.9 %copy-start.8 = (f32[32,32,128]{2,1,0:T(8,128)}, f32[32,32,128]{2,1,0:T(8,128)S(1)}, u32[]{:S(2)}) copy-start(f32[32,32,128]{2,1,0:T(8,128)S(1)} %get-tuple-element.60) | copy-start | bytes 1572868
  28.1 16.9 %copy-start.12 = (f32[32,32,128]{2,1,0:T(8,128)}, f32[32,32,128]{2,1,0:T(8,128)S(1)}, u32[]{:S(2)}) copy-start(f32[32,32,128]{2,1,0:T(8,128)S(1)} %get-tuple-element.61) | copy-start | bytes 1572868
  28.1 16.9 %copy-start.20 = (f32[32,32,128]{2,1,0:T(8,128)}, f32[32,32,128]{2,1,0:T(8,128)S(1)}, u32[]{:S(2)}) copy-start(f32[32,32,128]{2,1,0:T(8,128)S(1)} %get-tuple-element.62) | copy-start | bytes 1572868
  28.1 5.3 %collective-permute-start.5 = (f32[1,32,128]{2,1,0:T(8,128)S(1)}, f32[1,32,128]{2,1,0:T(8,128)S(1)}, u32[]{:S(2)}, u32[]{:S(2)}) collective-permute-start(f32[1,32,128]{2,1,0:T(8,128)S(1)} %get-tuple-element.94), channel_id=1, source_target_pairs={{0,2},{2,4},{4,6},{6,8},{8,10},{10,12},{12,14},{14,16},{16,18},{18... | collective-permute-start | bytes 49160 | tf_op jit(solution)/shard_map/ppermute | solution.py:23
  30.3 6.0 %collective-permute-start.4 = (f32[1,32,128]{2,1,0:T(8,128)S(1)}, f32[1,32,128]{2,1,0:T(8,128)S(1)}, u32[]{:S(2)}, u32[]{:S(2)}) collective-permute-start(f32[1,32,128]{2,1,0:T(8,128)S(1)} %get-tuple-element.95), channel_id=1, source_target_pairs={{2,0},{4,2},{6,4},{8,6},{10,8},{12,10},{14,12},{16,14},{18,16},{20... | collective-permute-start | bytes 49160 | tf_op jit(solution)/shard_map/ppermute | solution.py:24
  36.4 5.5 %collective-permute-start.7 = (f32[34,1,128]{2,1,0:T(1,128)S(1)}, f32[34,1,128]{2,1,0:T(1,128)S(1)}, u32[]{:S(2)}, u32[]{:S(2)}) collective-permute-start(f32[34,1,128]{2,1,0:T(1,128)S(1)} %get-tuple-element.84), channel_id=1, source_target_pairs={{0,1},{2,3},{4,5},{6,7},{8,9},{10,11},{12,13},{14,15},{16,17},{18,... | collective-permute-start | bytes 52232 | tf_op jit(solution)/shard_map/ppermute | solution.py:23
  37.7 5.0 %collective-permute-start.6 = (f32[34,1,128]{2,1,0:T(1,128)S(1)}, f32[34,1,128]{2,1,0:T(1,128)S(1)}, u32[]{:S(2)}, u32[]{:S(2)}) collective-permute-start(f32[34,1,128]{2,1,0:T(1,128)S(1)} %get-tuple-element.85), channel_id=1, source_target_pairs={{1,0},{3,2},{5,4},{7,6},{9,8},{11,10},{13,12},{15,14},{17,16},{19,... | collective-permute-start | bytes 52232 | tf_op jit(solution)/shard_map/ppermute | solution.py:24
  43.3 15.8 %copy-start.24 = (f32[32,32,16]{2,1,0:T(8,128)S(1)}, f32[32,32,16]{2,1,0:T(8,128)}, u32[]{:S(2)}) copy-start(f32[32,32,16]{2,1,0:T(8,128)} %copy-done.23) | copy-start | bytes 196612
  45.0 5.6 %collective-permute-start.9 = (f32[1,32,128]{2,1,0:T(8,128)S(1)}, f32[1,32,128]{2,1,0:T(8,128)S(1)}, u32[]{:S(2)}, u32[]{:S(2)}) collective-permute-start(f32[1,32,128]{2,1,0:T(8,128)S(1)} %get-tuple-element.92), channel_id=1, source_target_pairs={{0,2},{2,4},{4,6},{6,8},{8,10},{10,12},{12,14},{14,16},{16,18},{18... | collective-permute-start | bytes 49160 | tf_op jit(solution)/shard_map/ppermute | solution.py:23
  48.6 5.4 %collective-permute-start.8 = (f32[1,32,128]{2,1,0:T(8,128)S(1)}, f32[1,32,128]{2,1,0:T(8,128)S(1)}, u32[]{:S(2)}, u32[]{:S(2)}) collective-permute-start(f32[1,32,128]{2,1,0:T(8,128)S(1)} %get-tuple-element.93), channel_id=1, source_target_pairs={{2,0},{4,2},{6,4},{8,6},{10,8},{12,10},{14,12},{16,14},{18,16},{20... | collective-permute-start | bytes 49160 | tf_op jit(solution)/shard_map/ppermute | solution.py:24
  54.0 17.1 %copy-start.30 = (f32[1,32,128]{2,1,0:T(8,128)}, f32[1,32,128]{2,1,0:T(8,128)S(1)}, u32[]{:S(2)}) copy-start(f32[1,32,128]{2,1,0:T(8,128)S(1)} %collective-permute-done.8) | copy-start | bytes 49156
  54.1 16.4 %collective-permute-start.11 = (f32[34,1,128]{2,1,0:T(1,128)S(1)}, f32[34,1,128]{2,1,0:T(1,128)S(1)}, u32[]{:S(2)}, u32[]{:S(2)}) collective-permute-start(f32[34,1,128]{2,1,0:T(1,128)S(1)} %get-tuple-element.82), channel_id=1, source_target_pairs={{0,1},{2,3},{4,5},{6,7},{8,9},{10,11},{12,13},{14,15},{16,17},{18,... | collective-permute-start | bytes 52232 | tf_op jit(solution)/shard_map/ppermute | solution.py:23
  55.4 15.1 %collective-permute-start.10 = (f32[34,1,128]{2,1,0:T(1,128)S(1)}, f32[34,1,128]{2,1,0:T(1,128)S(1)}, u32[]{:S(2)}, u32[]{:S(2)}) collective-permute-start(f32[34,1,128]{2,1,0:T(1,128)S(1)} %get-tuple-element.83), channel_id=1, source_target_pairs={{1,0},{3,2},{5,4},{7,6},{9,8},{11,10},{13,12},{15,14},{17,16},{19,... | collective-permute-start | bytes 52232 | tf_op jit(solution)/shard_map/ppermute | solution.py:24
  70.4 1.4 copy-start.9
  70.4 1.5 copy-start.13
  70.4 1.8 copy-start.18
  70.5 2.7 copy-start.32
  70.5 2.7 copy-start.34
  71.1 2.1 copy-start.14
  73.2 54.0 %collective-permute-start.13 = (f32[1,32,128]{2,1,0:T(8,128)S(1)}, f32[1,32,128]{2,1,0:T(8,128)S(1)}, u32[]{:S(2)}, u32[]{:S(2)}) collective-permute-start(f32[1,32,128]{2,1,0:T(8,128)S(1)} %get-tuple-element.90), channel_id=1, source_target_pairs={{0,2},{2,4},{4,6},{6,8},{8,10},{10,12},{12,14},{14,16},{16,18},{18... | collective-permute-start | bytes 49160 | tf_op jit(solution)/shard_map/ppermute | solution.py:23
  75.7 51.5 %collective-permute-start.12 = (f32[1,32,128]{2,1,0:T(8,128)S(1)}, f32[1,32,128]{2,1,0:T(8,128)S(1)}, u32[]{:S(2)}, u32[]{:S(2)}) collective-permute-start(f32[1,32,128]{2,1,0:T(8,128)S(1)} %get-tuple-element.91), channel_id=1, source_target_pairs={{2,0},{4,2},{6,4},{8,6},{10,8},{12,10},{14,12},{16,14},{18,16},{20... | collective-permute-start | bytes 49160 | tf_op jit(solution)/shard_map/ppermute | solution.py:24
  127.2 2.0 copy-start.36
  127.2 2.0 copy-start.38
  127.9 55.6 %collective-permute-start.15 = (f32[34,1,128]{2,1,0:T(1,128)}, f32[34,1,128]{2,1,0:T(1,128)}, u32[]{:S(2)}, u32[]{:S(2)}) collective-permute-start(f32[34,1,128]{2,1,0:T(1,128)} %get-tuple-element.80), channel_id=1, source_target_pairs={{0,1},{2,3},{4,5},{6,7},{8,9},{10,11},{12,13},{14,15},{16,17},{18,... | collective-permute-start | bytes 52232 | tf_op jit(solution)/shard_map/ppermute | solution.py:23
  129.2 54.3 %collective-permute-start.14 = (f32[34,1,128]{2,1,0:T(1,128)}, f32[34,1,128]{2,1,0:T(1,128)}, u32[]{:S(2)}, u32[]{:S(2)}) collective-permute-start(f32[34,1,128]{2,1,0:T(1,128)} %get-tuple-element.81), channel_id=1, source_target_pairs={{1,0},{3,2},{5,4},{7,6},{9,8},{11,10},{13,12},{15,14},{17,16},{19,... | collective-permute-start | bytes 52232 | tf_op jit(solution)/shard_map/ppermute | solution.py:24
  170.6 12.9 %copy-start.37 = (f32[1,32,128]{2,1,0:T(8,128)S(1)}, f32[1,32,128]{2,1,0:T(8,128)}, u32[]{:S(2)}) copy-start(f32[1,32,128]{2,1,0:T(8,128)} %copy-done.36) | copy-start | bytes 49156
  170.6 12.9 %copy-start.39 = (f32[1,32,128]{2,1,0:T(8,128)S(1)}, f32[1,32,128]{2,1,0:T(8,128)}, u32[]{:S(2)}) copy-start(f32[1,32,128]{2,1,0:T(8,128)} %copy-done.38) | copy-start | bytes 49156
  183.5 1.5 copy-start.2
  183.5 1.5 copy-start.6
  183.5 1.5 copy-start.10
  183.5 1.5 copy-start.31
  183.5 1.5 copy-start.33
  183.5 1.5 copy-start.35
  185.0 11.4 %copy-start.26 = (f32[16,16,64]{2,1,0:T(8,128)S(1)}, f32[16,16,64]{2,1,0:T(8,128)}, u32[]{:S(2)}) copy-start(f32[16,16,64]{2,1,0:T(8,128)} %reduce_sum.73) | copy-start | bytes 196612
  191.0 14.3 %collective-permute-start.17 = (f32[1,32,128]{2,1,0:T(8,128)}, f32[1,32,128]{2,1,0:T(8,128)S(1)}, u32[]{:S(2)}, u32[]{:S(2)}) collective-permute-start(f32[1,32,128]{2,1,0:T(8,128)} %get-tuple-element.88), channel_id=1, source_target_pairs={{0,2},{2,4},{4,6},{6,8},{8,10},{10,12},{12,14},{14,16},{16,18},{18... | collective-permute-start | bytes 49160 | tf_op jit(solution)/shard_map/ppermute | solution.py:23
  194.4 10.9 %collective-permute-start.16 = (f32[1,32,128]{2,1,0:T(8,128)}, f32[1,32,128]{2,1,0:T(8,128)}, u32[]{:S(2)}, u32[]{:S(2)}) collective-permute-start(f32[1,32,128]{2,1,0:T(8,128)} %get-tuple-element.89), channel_id=1, source_target_pairs={{2,0},{4,2},{6,4},{8,6},{10,8},{12,10},{14,12},{16,14},{18,16},{20... | collective-permute-start | bytes 49160 | tf_op jit(solution)/shard_map/ppermute | solution.py:24
  202.1 3.2 copy-start.16
  206.7 16.6 %collective-permute-start.19 = (f32[34,1,128]{2,1,0:T(1,128)}, f32[34,1,128]{2,1,0:T(1,128)}, u32[]{:S(2)}, u32[]{:S(2)}) collective-permute-start(f32[34,1,128]{2,1,0:T(1,128)} %get-tuple-element.78), channel_id=1, source_target_pairs={{0,1},{2,3},{4,5},{6,7},{8,9},{10,11},{12,13},{14,15},{16,17},{18,... | collective-permute-start | bytes 52232 | tf_op jit(solution)/shard_map/ppermute | solution.py:23
  208.0 15.3 %collective-permute-start.18 = (f32[34,1,128]{2,1,0:T(1,128)}, f32[34,1,128]{2,1,0:T(1,128)}, u32[]{:S(2)}, u32[]{:S(2)}) collective-permute-start(f32[34,1,128]{2,1,0:T(1,128)} %get-tuple-element.79), channel_id=1, source_target_pairs={{1,0},{3,2},{5,4},{7,6},{9,8},{11,10},{13,12},{15,14},{17,16},{19,... | collective-permute-start | bytes 52232 | tf_op jit(solution)/shard_map/ppermute | solution.py:24
  223.2 1.8 copy-start.3
  223.3 1.8 copy-start.7
  223.3 1.8 copy-start.11
  265.0 18.8 %copy-start.40 = (f32[8,8,32]{2,1,0:T(8,128)S(1)}, f32[8,8,32]{2,1,0:T(8,128)}, u32[]{:S(2)}) copy-start(f32[8,8,32]{2,1,0:T(8,128)} %reduce_sum.79) | copy-start | bytes 24580
  265.0 18.8 %copy-start.29 = (f32[16,16,64]{2,1,0:T(8,128)S(1)}, f32[16,16,64]{2,1,0:T(8,128)}, u32[]{:S(2)}) copy-start(f32[16,16,64]{2,1,0:T(8,128)} %get-tuple-element.114) | copy-start | bytes 196612
  277.3 14.7 %collective-permute-start.20 = (f32[4,5,16,64]{3,2,1,0:T(8,128)S(1)}, f32[4,5,16,64]{3,2,1,0:T(8,128)S(1)}, u32[]{:S(2)}, u32[]{:S(2)}) collective-permute-start(f32[4,5,16,64]{3,2,1,0:T(8,128)S(1)} %get-tuple-element.86), channel_id=1, source_target_pairs={{0,2},{2,4},{4,6},{6,8},{8,10},{10,12},{12,14},{14,16},{16,18},{18... | collective-permute-start | bytes 245768 | tf_op jit(solution)/shard_map/ppermute | solution.py:23
  281.6 10.5 %collective-permute-start.21 = (f32[4,5,16,64]{3,2,1,0:T(8,128)S(1)}, f32[4,5,16,64]{3,2,1,0:T(8,128)S(1)}, u32[]{:S(2)}, u32[]{:S(2)}) collective-permute-start(f32[4,5,16,64]{3,2,1,0:T(8,128)S(1)} %get-tuple-element.87), channel_id=1, source_target_pairs={{2,0},{4,2},{6,4},{8,6},{10,8},{12,10},{14,12},{16,14},{18,16},{20... | collective-permute-start | bytes 245768 | tf_op jit(solution)/shard_map/ppermute | solution.py:24
  292.2 4.7 %collective-permute-start.22 = (f32[4,26,5,64]{3,2,1,0:T(8,128)S(1)}, f32[4,26,5,64]{3,2,1,0:T(8,128)S(1)}, u32[]{:S(2)}, u32[]{:S(2)}) collective-permute-start(f32[4,26,5,64]{3,2,1,0:T(8,128)S(1)} %get-tuple-element.76), channel_id=1, source_target_pairs={{0,1},{2,3},{4,5},{6,7},{8,9},{10,11},{12,13},{14,15},{16,17},{18,... | collective-permute-start | bytes 399368 | tf_op jit(solution)/shard_map/ppermute | solution.py:23
  293.5 4.4 %collective-permute-start.23 = (f32[4,26,5,64]{3,2,1,0:T(8,128)S(1)}, f32[4,26,5,64]{3,2,1,0:T(8,128)S(1)}, u32[]{:S(2)}, u32[]{:S(2)}) collective-permute-start(f32[4,26,5,64]{3,2,1,0:T(8,128)S(1)} %get-tuple-element.77), channel_id=1, source_target_pairs={{1,0},{3,2},{5,4},{7,6},{9,8},{11,10},{13,12},{15,14},{17,16},{19,... | collective-permute-start | bytes 399368 | tf_op jit(solution)/shard_map/ppermute | solution.py:24
  309.0 2.6 copy-start.27
  311.6 15.7 %copy-start.19 = (f32[32,32,128]{2,1,0:T(8,128)S(1)}, f32[32,32,128]{2,1,0:T(8,128)}, u32[]{:S(2)}) copy-start(f32[32,32,128]{2,1,0:T(8,128)} %get-tuple-element.53) | copy-start | bytes 1572868
  311.6 15.7 %copy-start.21 = (f32[32,32,128]{2,1,0:T(8,128)S(1)}, f32[32,32,128]{2,1,0:T(8,128)}, u32[]{:S(2)}) copy-start(f32[32,32,128]{2,1,0:T(8,128)} %copy-done.20) | copy-start | bytes 1572868
  311.6 15.7 %copy-start.22 = (f32[32,32,128]{2,1,0:T(8,128)S(1)}, f32[32,32,128]{2,1,0:T(8,128)}, u32[]{:S(2)}) copy-start(f32[32,32,128]{2,1,0:T(8,128)} %get-tuple-element.51) | copy-start | bytes 1572868
  311.7 8.2 %collective-permute-start.24 = (f32[4,6,8,32]{3,2,1,0:T(8,128)S(1)}, f32[4,6,8,32]{3,2,1,0:T(8,128)S(1)}, u32[]{:S(2)}, u32[]{:S(2)}) collective-permute-start(f32[4,6,8,32]{3,2,1,0:T(8,128)S(1)} %get-tuple-element.105), channel_id=1, source_target_pairs={{0,2},{2,4},{4,6},{6,8},{8,10},{10,12},{12,14},{14,16},{16,18},{18... | collective-permute-start | bytes 73736 | tf_op jit(solution)/shard_map/ppermute | solution.py:23
  315.9 6.3 %collective-permute-start.25 = (f32[4,6,8,32]{3,2,1,0:T(8,128)S(1)}, f32[4,6,8,32]{3,2,1,0:T(8,128)S(1)}, u32[]{:S(2)}, u32[]{:S(2)}) collective-permute-start(f32[4,6,8,32]{3,2,1,0:T(8,128)S(1)} %get-tuple-element.106), channel_id=1, source_target_pairs={{2,0},{4,2},{6,4},{8,6},{10,8},{12,10},{14,12},{16,14},{18,16},{20... | collective-permute-start | bytes 73736 | tf_op jit(solution)/shard_map/ppermute | solution.py:24
  322.2 6.2 %collective-permute-start.26 = (f32[4,20,6,32]{3,2,1,0:T(8,128)S(1)}, f32[4,20,6,32]{3,2,1,0:T(8,128)S(1)}, u32[]{:S(2)}, u32[]{:S(2)}) collective-permute-start(f32[4,20,6,32]{3,2,1,0:T(8,128)S(1)} %get-tuple-element.101), channel_id=1, source_target_pairs={{0,1},{2,3},{4,5},{6,7},{8,9},{10,11},{12,13},{14,15},{16,17},{18,... | collective-permute-start | bytes 184328 | tf_op jit(solution)/shard_map/ppermute | solution.py:23
  323.5 5.0 %collective-permute-start.27 = (f32[4,20,6,32]{3,2,1,0:T(8,128)S(1)}, f32[4,20,6,32]{3,2,1,0:T(8,128)S(1)}, u32[]{:S(2)}, u32[]{:S(2)}) collective-permute-start(f32[4,20,6,32]{3,2,1,0:T(8,128)S(1)} %get-tuple-element.102), channel_id=1, source_target_pairs={{1,0},{3,2},{5,4},{7,6},{9,8},{11,10},{13,12},{15,14},{17,16},{19,... | collective-permute-start | bytes 184328 | tf_op jit(solution)/shard_map/ppermute | solution.py:24
  (5 other events, 5.3 us)
where the time goes:
time: 337 us; the launch traced here: 332 us
  local copies, waits for them, and re-layouts  153 us (45%)
  other arithmetic  84.9 us (25%)
  starting transfers between devices  76.9 us (23%)
  waiting for transfers between devices  15 us (4%)
    reshape x4, local copies, waits for them, and re-layouts, coarsen(): fields.reshape(shape_in[0] // 2, 2, shape_in[1] // 2, 2, shape_in[2] // 2...  112 us
    reduce_sum x8, other arithmetic, coarsen(): return jnp.mean(blocks, axis=(1, 3, 5))  49.6 us
    ppermute x14, starting transfers between devices, extended_2(): after = lax.ppermute(leading, axis, down)  44.5 us
    ppermute x14, starting transfers between devices, extended_2(): before = lax.ppermute(last, axis, up)  32.4 us
    div x3, local copies, waits for them, and re-layouts, coarsen(): return jnp.mean(blocks, axis=(1, 3, 5))  17.9 us
    ppermute x14, waiting for transfers between devices, extended_2(): after = lax.ppermute(leading, axis, down)  14 us
    broadcast_in_dim x3, local copies, waits for them, and re-layouts, refine_mask(): return jnp.repeat(values, 8, axis=2)  11.3 us
    add x10, other arithmetic, chebyshev(): factor_next * factor_prev * update  10.5 us
  transfers between devices with their start and end apart: 28, of which 8 were waited for; matrix products, arithmetic and copies ran while one was open for 43% of the time, Pallas kernels for 0%

commit v1 on v0

v1 whole, which is shorter than its diff:
```python
import functools

import jax
import jax.numpy as jnp
from jax import lax
from jax.experimental import pallas as pl
from jax.experimental.pallas import tpu as pltpu
from jax.sharding import PartitionSpec as P

DEGREE = 4
COARSE_DEGREE = 6

STEP_SCALE = 4.0
SMOOTH_LOW = 0.3
SMOOTH_HIGH = 2.0
COARSE_LOW = 0.05

BRICK = 8
TILE = 8
VMEM_BYTES = 48 * 1024 * 1024


def chebyshev_constants(degree, lowest, highest):
    middle = (highest + lowest) / 2.0
    spread = (highest - lowest) / 2.0
    relative = middle / spread
    previous = 1.0 / relative
    steps = []
    for _ in range(degree - 1):
        following = 1.0 / (2.0 * relative - previous)
        steps.append((following * previous, 2.0 * following / spread))
        previous = following
    return 1.0 / middle, steps


def lane_index(shape):
    return lax.broadcasted_iota(jnp.int32, shape, len(shape) - 1)


def ahead(value, axis, step=1):
    return pltpu.roll(value, value.shape[axis] - step, axis)


def behind(value, axis, step=1):
    return pltpu.roll(value, step, axis)


def positive(value):
    return jnp.where(value > 0.0, 1.0, 0.0)


def rows_loop(start, stop, body, unroll=2):
    lax.fori_loop(start, stop, lambda i, c: (body(i), c)[1], 0, unroll=unroll)


def level_setup(lo, hi, zstep, factor, g_ref, a_ref, wx_ref, wy_ref, wz_ref, inv_ref, d_ref):
    half = 0.5 * factor

    def weight_x(i):
        here, there = g_ref[i], g_ref[i + 1]
        wx_ref[i] = jnp.where((here > 0.0) & (there > 0.0), half * (here + there), 0.0)

    weight_x(lo - 1)

    def row(i):
        weight_x(i)
        here = g_ref[i]
        lanes = lane_index(here.shape)
        inside = here > 0.0
        there_y = ahead(here, 0)
        there_z = ahead(here, 1, zstep)
        wy = jnp.where(inside & (there_y > 0.0), half * (here + there_y), 0.0)
        wz = jnp.where(inside & (there_z > 0.0) & (lanes < here.shape[1] - zstep), half * (here + there_z), 0.0)
        wy_ref[i] = wy
        wz_ref[i] = wz
        faces = [wx_ref[i], wx_ref[i - 1], wy, behind(wy, 0), wz, behind(wz, 1, zstep)]
        summed = faces[0]
        counted = positive(faces[0])
        for face in faces[1:]:
            summed = summed + face
            counted = counted + positive(face)
        diagonal = 1.0 + summed + factor * a_ref[i] * (6.0 - counted)
        d_ref[i] = diagonal
        inv_ref[i] = jnp.where(inside, 1.0 / diagonal, 0.0)

    rows_loop(lo, hi, row)


def level_sweeps(base, size, reach, degree, lowest, keep, zstep, b_ref, inv_ref, wx_ref, wy_ref, wz_ref, e_ref, u_refs):
    first, steps = chebyshev_constants(degree, lowest, SMOOTH_HIGH)
    passes = degree if keep else degree - 1

    def start(i):
        e = inv_ref[i] * b_ref[i]
        e_ref[i] = e
        u_refs[0][i] = e * first

    width = reach + passes
    rows_loop(base - width, base + size + width, start)
    for k in range(passes):
        old = u_refs[k]

        def row(i, k=k, old=old):
            u = old[i]
            wy = wy_ref[i]
            wz = wz_ref[i]
            coupled = wx_ref[i] * old[i + 1] + wx_ref[i - 1] * old[i - 1]
            coupled = coupled + (wy * ahead(u, 0) + behind(wy * u, 0))
            coupled = coupled + (wz * ahead(u, 1, zstep) + behind(wz * u, 1, zstep))
            e = e_ref[i] - u + inv_ref[i] * coupled
            e_ref[i] = e
            if k + 1 < degree:
                u_refs[k + 1][i] = steps[k][0] * u + steps[k][1] * e

        width = reach + passes - 1 - k
        rows_loop(base - width, base + size + width, row)


def coarsen_rows(one, two, pair_ref, zstep):
    pair_ref[...] = one + two
    half = pair_ref.shape[0] // 2
    summed = pair_ref[pl.ds(0, half, 2), :] + pair_ref[pl.ds(1, half, 2), :]
    return (summed + ahead(summed, 1, zstep)) * 0.125


def pack_two(one, two):
    return jnp.where(lane_index(one.shape) % 2 == 0, one, behind(two, 1))


def unpack_two(packed):
    even = lane_index(packed.shape) % 2 == 0
    return jnp.where(even, packed, 0.0), jnp.where(even, ahead(packed, 1), 0.0)


def pack_kernel(slots, src_ref, kap_ref, ab_ref, brick_ref, g_ref, a_out, b_out, q_ref, *rest):
    y_outs, pair_ref = rest[:slots], rest[slots]
    nx, ny, nz = src_ref.shape
    lower, upper = DEGREE, DEGREE + 1
    nbz = brick_ref.shape[2]
    spread = jnp.where(
        lax.broadcasted_iota(jnp.int32, (nbz, nz), 1) // BRICK == lax.broadcasted_iota(jnp.int32, (nbz, nz), 0), 1.0, 0.0
    )
    for bx in range(nx // BRICK):
        lines = jnp.dot(brick_ref[bx].astype(jnp.float32), spread, preferred_element_type=jnp.float32)
        mask = jnp.concatenate(
            [jnp.broadcast_to(lines[by : by + 1], (BRICK, nz)) for by in range(ny // BRICK)], axis=0
        )
        for x in range(bx * BRICK, (bx + 1) * BRICK):
            g_ref[x] = kap_ref[x] * mask

    def packed_pair(ref, j):
        cells = [coarsen_rows(ref[4 * j + 2 * t], ref[4 * j + 2 * t + 1], pair_ref.at[t], 1) for t in range(2)]
        return pack_two(*cells)

    def quad(j):
        q_ref[0, j] = packed_pair(g_ref, j)
        q_ref[1, j] = packed_pair(ab_ref, j)

    rows_loop(0, nx // 4, quad, unroll=True)

    even = lax.axis_index("dom") % 2 == 0
    for out, up in ((a_out, even), (b_out, jnp.logical_not(even))):
        four = jnp.where(up, nx - lower, 0)
        five = jnp.where(up, nx - upper, 0)
        for j in range(lower):
            out[j] = src_ref[four + j]
            out[lower + j] = ab_ref[four + j]
        for j in range(upper):
            out[2 * lower + j] = g_ref[five + j]

    core = lax.axis_index("grp")
    for slot, out in enumerate(y_outs):
        up = core == 0 if slots == 1 else slot == 1
        at = pl.multiple_of(jnp.where(up, ny - TILE, 0), TILE)
        for x in range(nx):
            out[0, x] = src_ref[x, pl.ds(at, TILE), :]
            out[1, x] = ab_ref[x, pl.ds(at, TILE), :]
            out[2, x] = g_ref[x, pl.ds(at, TILE), :]


def slot_is_upper(slots, slot):
    return lax.axis_index("grp") == 0 if slots == 1 else slot == 0


def keep_near(value, is_upper, reach):
    rows = lax.broadcasted_iota(jnp.int32, value.shape, 0)
    size = value.shape[0]
    low = jnp.where(is_upper, 0, size - reach)
    high = jnp.where(is_upper, reach, size)
    return jnp.where((rows >= low) & (rows < high), value, 0.0)


def fine_kernel(slots, src_ref, ab_ref, g_in, ra_ref, rb_ref, *rest):
    y_refs, ya_refs, yb_refs = rest[:slots], rest[slots : 2 * slots], rest[2 * slots : 3 * slots]
    it_out, res_out, s_out = rest[3 * slots : 3 * slots + 3]
    b_ref, a_ref, g_ref, wx, wy, wz, inv, d_ref, e_ref, u0, u1, u2, u3, pair_ref = rest[3 * slots + 3 :]
    nx, ny, nz = src_ref.shape
    lower, upper = DEGREE, DEGREE + 1
    base = upper

    def own(i):
        b_ref[base + i, :ny] = src_ref[i]
        a_ref[base + i, :ny] = ab_ref[i]
        g_ref[base + i, :ny] = g_in[i]
        for slot, y_ref in enumerate(y_refs):
            at = slice(ny + slot * TILE, ny + (slot + 1) * TILE)
            b_ref[base + i, at] = y_ref[0, i]
            a_ref[base + i, at] = y_ref[1, i]
            g_ref[base + i, at] = keep_near(y_ref[2, i], slot_is_upper(slots, slot), upper)

    rows_loop(0, nx, own)

    even = lax.axis_index("dom") % 2 == 0
    for r_ref, y_list, is_above in ((ra_ref, ya_refs, even), (rb_ref, yb_refs, jnp.logical_not(even))):
        four = jnp.where(is_above, base + nx, base - lower)
        five = jnp.where(is_above, base + nx, base - upper)
        for j in range(lower):
            b_ref[four + j, :ny] = r_ref[j]
            a_ref[four + j, :ny] = r_ref[lower + j]
        for j in range(upper):
            g_ref[five + j, :ny] = r_ref[2 * lower + j]
        for slot, y_ref in enumerate(y_list):
            at = slice(ny + slot * TILE, ny + (slot + 1) * TILE)
            is_upper = slot_is_upper(slots, slot)
            part = pl.ds(pl.multiple_of(jnp.where(is_upper, 0, ny - TILE), TILE), TILE)
            for j in range(lower):
                b_ref[four + j, at] = y_ref[j, part, :]
                a_ref[four + j, at] = y_ref[lower + j, part, :]
            for j in range(upper):
                g_ref[five + j, at] = keep_near(y_ref[2 * lower + j, part, :], is_upper, upper)

    level_setup(base - lower, base + nx + lower, 1, STEP_SCALE, g_ref, a_ref, wx, wy, wz, inv, d_ref)
    u_refs = (u0, u1, u2, u3)
    level_sweeps(base, nx, 0, DEGREE, SMOOTH_LOW, True, 1, b_ref, inv, wx, wy, wz, e_ref, u_refs)

    def finish(i):
        total = u_refs[0][base + i, :ny]
        for u_ref in u_refs[1:]:
            total = total + u_ref[base + i, :ny]
        it_out[i] = total
        res_out[i] = d_ref[base + i, :ny] * e_ref[base + i, :ny]

    rows_loop(0, nx, finish)

    def quad(j):
        cells = [
            coarsen_rows(res_out[4 * j + 2 * t], res_out[4 * j + 2 * t + 1], pair_ref.at[t], 1) for t in range(2)
        ]
        s_out[j] = pack_two(*cells)

    rows_loop(0, nx // 4, quad, unroll=True)


def compact(value, step):
    nz = value.shape[-1]
    shape = (nz, nz // step)
    pick = jnp.where(
        lax.broadcasted_iota(jnp.int32, shape, 0) == step * lax.broadcasted_iota(jnp.int32, shape, 1), 1.0, 0.0
    )
    return jnp.dot(value, pick, preferred_element_type=jnp.float32, precision=lax.Precision.HIGHEST)


def coarse_kernel(slots, *refs):
    parts = 3 * (1 + slots)
    q_refs, s_refs = refs[:parts], refs[parts : 2 * parts]
    mid_out, coarse_out = refs[2 * parts : 2 * parts + 2]
    scratch = refs[2 * parts + 2 :]
    b_ref, a_ref, g_ref, wx, wy, wz, inv, d_ref, e_ref, u0, u1, u2, u3 = scratch[:13]
    cb, ca, cg, cwx, cwy, cwz, cinv, cd, ce, v0, v1, v2, v3, v4, v5 = scratch[13:28]
    pair_ref = scratch[28]
    packed, ny, nz = s_refs[0].shape
    nx = 2 * packed
    base = nx
    even = lax.axis_index("dom") % 2 == 0

    for part in range(3):
        start = base if part == 0 else jnp.where(even if part == 1 else jnp.logical_not(even), 2 * nx, 0)
        for slot in range(1 + slots):
            q_ref, s_ref = q_refs[part * (1 + slots) + slot], s_refs[part * (1 + slots) + slot]
            at = slice(slot * ny, (slot + 1) * ny)

            def place(j, q_ref=q_ref, s_ref=s_ref, at=at, start=start, slot=slot):
                g_rows, a_rows, b_rows = unpack_two(q_ref[0, j]), unpack_two(q_ref[1, j]), unpack_two(s_ref[j])
                for t in range(2):
                    g_row = g_rows[t]
                    if slot:
                        g_row = keep_near(g_row, slot_is_upper(slots, slot - 1), ny - 1)
                    g_ref[start + 2 * j + t, at] = g_row
                    a_ref[start + 2 * j + t, at] = a_rows[t]
                    b_ref[start + 2 * j + t, at] = b_rows[t]

            rows_loop(0, packed, place)

    reach = 2 * (COARSE_DEGREE - 1)
    width = reach + DEGREE
    u_refs = (u0, u1, u2, u3)
    level_setup(base - width, base + nx + width, 2, STEP_SCALE / 4.0, g_ref, a_ref, wx, wy, wz, inv, d_ref)
    level_sweeps(base, nx, reach, DEGREE, SMOOTH_LOW, True, 2, b_ref, inv, wx, wy, wz, e_ref, u_refs)

    total = u0[base : base + nx, :ny]
    for u_ref in u_refs[1:]:
        total = total + u_ref[base : base + nx, :ny]
    mid_out[...] = compact(total.reshape(nx * ny, nz), 2).reshape(nx, ny, nz // 2)

    half, cny = nx // 2, ny // 2
    cbase = COARSE_DEGREE
    offset = base - 2 * cbase

    def coefficients(i):
        row = offset + 2 * i
        g0, g1 = g_ref[row], g_ref[row + 1]
        whole = coarsen_rows(positive(g0), positive(g1), pair_ref, 2) > 0.75
        first = lane_index(whole.shape) % 4 == 0
        cg[i] = jnp.where(whole & first, coarsen_rows(g0, g1, pair_ref, 2), 0.0)
        ca[i] = coarsen_rows(a_ref[row], a_ref[row + 1], pair_ref, 2)

    rows_loop(0, half + 2 * cbase, coefficients)

    def source(i):
        row = offset + 2 * i
        cb[i] = coarsen_rows(d_ref[row] * e_ref[row], d_ref[row + 1] * e_ref[row + 1], pair_ref, 2)

    rows_loop(1, half + 2 * cbase - 1, source)

    v_refs = (v0, v1, v2, v3, v4, v5)
    level_setup(1, half + 2 * cbase - 1, 4, STEP_SCALE / 16.0, cg, ca, cwx, cwy, cwz, cinv, cd)
    level_sweeps(cbase, half, 0, COARSE_DEGREE, COARSE_LOW, False, 4, cb, cinv, cwx, cwy, cwz, ce, v_refs)
    total = v0[cbase : cbase + half, :cny]
    for v_ref in v_refs[1:]:
        total = total + v_ref[cbase : cbase + half, :cny]
    coarse_out[...] = compact(total.reshape(half * cny, nz), 4).reshape(half, cny, nz // 4)


def call(kernel, ins, outs, scratch):
    whole = pl.BlockSpec(memory_space=pltpu.VMEM)
    return pl.pallas_call(
        kernel,
        out_shape=[jax.ShapeDtypeStruct(shape, jnp.float32) for shape in outs],
        in_specs=[whole] * len(ins),
        out_specs=[whole] * len(outs),
        scratch_shapes=[pltpu.VMEM(shape, jnp.float32) for shape in scratch],
        compiler_params=pltpu.CompilerParams(vmem_limit_bytes=VMEM_BYTES),
    )(*ins)


def body(source, conductivity, absorption, brick_mask):
    doms, grps = lax.axis_size("dom"), lax.axis_size("grp")
    slots = min(grps - 1, 2)
    nx, ny, nz = source.shape
    lower, upper = DEGREE, DEGREE + 1

    def pairing(first):
        pairs = [(i, i + 1) for i in range(first, doms - 1, 2)]
        return pairs + [(j, i) for i, j in pairs]

    def swap_even(array):
        return lax.ppermute(array, "dom", pairing(0))

    def swap_odd(array):
        return lax.ppermute(array, "dom", pairing(1))

    downward = [(i + 1, i) for i in range(grps - 1)]
    upward = [(i, i + 1) for i in range(grps - 1)]

    def along_grp(arrays):
        if slots == 0:
            return []
        if slots == 1:
            return [lax.ppermute(arrays[0], "grp", downward + upward)]
        return [lax.ppermute(arrays[0], "grp", downward), lax.ppermute(arrays[-1], "grp", upward)]

    payload = (2 * lower + upper, ny, nz)
    packed = nx // 4
    outs = [source.shape, payload, payload, (2, packed, ny // 2, nz)] + [(3, nx, TILE, nz)] * slots
    g, to_even, to_odd, coeffs, *edges = call(
        functools.partial(pack_kernel, slots),
        (source, conductivity, absorption, brick_mask),
        outs,
        [(2, ny, nz)],
    )
    from_even, from_odd = swap_even(to_even), swap_odd(to_odd)
    beside = along_grp(edges)
    beside_even, beside_odd = along_grp([from_even]), along_grp([from_odd])
    coeff_parts = [coeffs, swap_even(coeffs), swap_odd(coeffs)]

    wide = (nx + 2 * upper, ny + slots * TILE, nz)
    fine_iterate, fine_residual, mid_source = call(
        functools.partial(fine_kernel, slots),
        (source, absorption, g, from_even, from_odd, *beside, *beside_even, *beside_odd),
        [source.shape, source.shape, (packed, ny // 2, nz)],
        [wide] * 13 + [(2, ny, nz)],
    )

    source_parts = [mid_source, swap_even(mid_source), swap_odd(mid_source)]
    q_ins, s_ins = [], []
    for q_part, s_part in zip(coeff_parts, source_parts):
        q_ins += [q_part] + along_grp([q_part])
        s_ins += [s_part] + along_grp([s_part])
    mid_y = (1 + slots) * ny // 2
    mid_wide = (3 * nx // 2, mid_y, nz)
    coarse_wide = (nx // 4 + 2 * COARSE_DEGREE, mid_y // 2, nz)
    mid_iterate, coarse_iterate = call(
        functools.partial(coarse_kernel, slots),
        (*q_ins, *s_ins),
        [(nx // 2, ny // 2, nz // 2), (nx // 4, ny // 4, nz // 4)],
        [mid_wide] * 13 + [coarse_wide] * 15 + [(mid_y, nz)],
    )
    return (fine_iterate, fine_residual, mid_iterate, coarse_iterate)


def solution(mesh):
    spec = P("dom", "grp", None)
    return jax.shard_map(body, mesh=mesh, in_specs=(spec,) * 4, out_specs=(spec,) * 4, check_vma=False)
```

time: 337 us -> 70.5 us (0.21); the launches traced: 332 us -> 69.8 us
  local copies, waits for them, and re-layouts: 153 us -> 3.82 us
  other arithmetic: 84.9 us -> 0 us
  starting transfers between devices: 76.9 us -> 24.8 us
  Pallas kernels: 0 us -> 32.3 us
  waiting for transfers between devices: 15 us -> 8.18 us
    reshape x8 -> x0, local copies, waits for them, and re-layouts: 117 us -> none  [the longest x4 112 us: coarsen(): fields.reshape(shape_in[0] // 2, 2, shape_in[1] // 2, 2, shape_in[2] // 2...]
    ppermute x28 -> x15, starting transfers between devices: 76.9 us -> 24.8 us  [the longest x9 13.1 us: along_grp(): return [lax.ppermute(arrays[0], 'grp', downward + upward)]]
    reduce_sum x8 -> x0, other arithmetic: 49.6 us -> none  [coarsen(): return jnp.mean(blocks, axis=(1, 3, 5))]
    pallas_call x0 -> x3, Pallas kernels: none -> 32.3 us  [call(): pl.pallas_call(kernel, out_shape=[jax.ShapeDtypeStruct(shape, jnp.float32...]
    div x3 -> x0, local copies, waits for them, and re-layouts: 17.9 us -> none  [coarsen(): return jnp.mean(blocks, axis=(1, 3, 5))]
    add x13 -> x0, other arithmetic: 12.8 us -> none  [the longest x10 10.5 us: chebyshev(): factor_next * factor_prev * update]
    broadcast_in_dim x4 -> x0, local copies, waits for them, and re-layouts: 11.3 us -> none  [the longest x3 11.3 us: refine_mask(): return jnp.repeat(values, 8, axis=2)]
    concatenate x13 -> x0, other arithmetic: 9.45 us -> none  [extended_2(): array = jnp.concatenate([before, array, after], axis=dim)]
  transfers between devices with their start and end apart: 28 -> 15, of which waited for: 8 -> 5; matrix products, arithmetic and copies ran while one was open for 43% -> 0% of each run, Pallas kernels for 0% -> 17%
where the time goes in v1:
time: 70.5 us; the launch traced here: 69.8 us
  Pallas kernels  32.3 us (46%)
  starting transfers between devices  24.8 us (35%)
  waiting for transfers between devices  8.18 us (12%)
  local copies, waits for them, and re-layouts  3.82 us (5%)
  between operations  0.72 us (1%)
    pallas_call x3, Pallas kernels, call(): pl.pallas_call(kernel, out_shape=[jax.ShapeDtypeStruct(shape, jnp.float32...  32.3 us
    ppermute x9, starting transfers between devices, along_grp(): return [lax.ppermute(arrays[0], 'grp', downward + upward)]  13.1 us
    ppermute x3, starting transfers between devices, swap_odd(): return lax.ppermute(array, 'dom', pairing(1))  9.06 us
    ppermute x3, waiting for transfers between devices, swap_odd(): return lax.ppermute(array, 'dom', pairing(1))  4.5 us
    unnamed x10, local copies, waits for them, and re-layouts  3.82 us
    ppermute x3, waiting for transfers between devices, swap_even(): return lax.ppermute(array, 'dom', pairing(0))  2.78 us
    ppermute x3, starting transfers between devices, swap_even(): return lax.ppermute(array, 'dom', pairing(0))  2.69 us
  transfers between devices with their start and end apart: 15, of which 5 were waited for; matrix products, arithmetic and copies ran while one was open for 0% of the time, Pallas kernels for 17%

profile of v1, /device:TPU:19, one launch (start us, length us, event | category | flops | bytes accessed | tf_op | source)
XLA Modules:
  0.0 69.8 jit_solution(15474498634293634948)
XLA Ops:
  0.6 0.0 copy-start
  0.6 1.0 %copy-done = f32[32,32,128]{2,1,0:T(8,128)S(1)} copy-done((f32[32,32,128]{2,1,0:T(8,128)S(1)}, f32[32,32,128]{2,1,0:T(8,128)}, u32[]{:S(2)}) %copy-start) | copy-done | bytes 524312
  1.7 0.0 copy-start.1
  1.7 1.0 %copy-done.1 = f32[32,32,128]{2,1,0:T(8,128)S(1)} copy-done((f32[32,32,128]{2,1,0:T(8,128)S(1)}, f32[32,32,128]{2,1,0:T(8,128)}, u32[]{:S(2)}) %copy-start.1) | copy-done | bytes 524312
  2.7 0.0 copy-start.3
  2.7 1.0 %copy-done.3 = f32[32,32,128]{2,1,0:T(8,128)S(1)} copy-done((f32[32,32,128]{2,1,0:T(8,128)S(1)}, f32[32,32,128]{2,1,0:T(8,128)}, u32[]{:S(2)}) %copy-start.3) | copy-done | bytes 524312
  3.8 0.0 copy-start.4
  3.8 0.7 copy-done.4
  4.5 0.0 copy-start.2
  4.5 0.5 shard_map.75
  4.9 0.3 collective-permute-start
  5.2 4.1 %collective-permute-start.1 = (f32[13,32,128]{2,1,0:T(8,128)S(1)}, f32[13,32,128]{2,1,0:T(8,128)S(1)}, u32[]{:S(2)}, u32[]{:S(2)}) collective-permute-start(f32[13,32,128]{2,1,0:T(8,128)S(1)} %get-tuple-element.16), channel_id=1, source_target_pairs={{2,4},{6,8},{10,12},{14,16},{18,20},{22,24},{26,28},{4,2},{8,6},{1... | collective-permute-start | bytes 638984 | tf_op jit(solution)/shard_map/ppermute | solution.py:360
  9.3 1.3 %collective-permute-start.2 = (f32[3,32,8,128]{3,2,1,0:T(8,128)S(1)}, f32[3,32,8,128]{3,2,1,0:T(8,128)S(1)}, u32[]{:S(2)}, u32[]{:S(2)}) collective-permute-start(f32[3,32,8,128]{3,2,1,0:T(8,128)S(1)} %get-tuple-element.17), channel_id=1, source_target_pairs={{1,0},{0,1},{3,2},{2,3},{5,4},{4,5},{7,6},{6,7},{9,8},{8,9},{11,10... | collective-permute-start | bytes 1179656 | tf_op jit(solution)/shard_map/ppermute | solution.py:369
  10.6 0.5 collective-permute-done.ra_ref
  11.1 6.1 %collective-permute-start.3 = (f32[13,32,128]{2,1,0:T(8,128)S(1)}, f32[13,32,128]{2,1,0:T(8,128)S(1)}, u32[]{:S(2)}, u32[]{:S(2)}) collective-permute-start(f32[13,32,128]{2,1,0:T(8,128)S(1)} %collective-permute-done.ra_ref), channel_id=1, source_target_pairs={{1,0},{0,1},{3,2},{2,3},{5,4},{4,5},{7,6},{6,7},{9,8},{8,9},{11,10... | collective-permute-start | bytes 638984 | tf_op jit(solution)/shard_map/ppermute | solution.py:369
  17.2 0.0 collective-permute-done.1.rb_ref
  17.2 1.0 %collective-permute-start.4 = (f32[13,32,128]{2,1,0:T(8,128)S(1)}, f32[13,32,128]{2,1,0:T(8,128)S(1)}, u32[]{:S(2)}, u32[]{:S(2)}) collective-permute-start(f32[13,32,128]{2,1,0:T(8,128)S(1)} %collective-permute-done.1.rb_ref), channel_id=1, source_target_pairs={{1,0},{0,1},{3,2},{2,3},{5,4},{4,5},{7,6},{6,7},{9,8},{8,9},{11,10... | collective-permute-start | bytes 638984 | tf_op jit(solution)/shard_map/ppermute | solution.py:369
  18.2 0.0 collective-permute-start.6
  18.2 2.8 %collective-permute-start.8 = (f32[2,8,16,128]{3,2,1,0:T(8,128)S(1)}, f32[2,8,16,128]{3,2,1,0:T(8,128)S(1)}, u32[]{:S(2)}, u32[]{:S(2)}) collective-permute-start(f32[2,8,16,128]{3,2,1,0:T(8,128)S(1)} %get-tuple-element.20.refs_0_), channel_id=1, source_target_pairs={{2,4},{6,8},{10,12},{14,16},{18,20},{22,24},{26,28},{4,2},{8,6},{1... | collective-permute-start | bytes 393224 | tf_op jit(solution)/shard_map/ppermute | solution.py:360
  21.0 2.3 %collective-permute-done.6.refs_2_ = f32[2,8,16,128]{3,2,1,0:T(8,128)S(1)} collective-permute-done((f32[2,8,16,128]{3,2,1,0:T(8,128)S(1)}, f32[2,8,16,128]{3,2,1,0:T(8,128)S(1)}, u32[]{:S(2)}, u32[]{:S(2)}) %collective-permute-start.6) | collective-permute-done | bytes 131104 | tf_op jit(solution)/shard_map/ppermute | solution.py:357
  23.3 0.8 %collective-permute-start.5 = (f32[2,8,16,128]{3,2,1,0:T(8,128)S(1)}, f32[2,8,16,128]{3,2,1,0:T(8,128)S(1)}, u32[]{:S(2)}, u32[]{:S(2)}) collective-permute-start(f32[2,8,16,128]{3,2,1,0:T(8,128)S(1)} %get-tuple-element.20.refs_0_), channel_id=1, source_target_pairs={{1,0},{0,1},{3,2},{2,3},{5,4},{4,5},{7,6},{6,7},{9,8},{8,9},{11,10... | collective-permute-start | bytes 393224 | tf_op jit(solution)/shard_map/ppermute | solution.py:369
  24.1 2.0 %collective-permute-done.8.refs_4_ = f32[2,8,16,128]{3,2,1,0:T(8,128)S(1)} collective-permute-done((f32[2,8,16,128]{3,2,1,0:T(8,128)S(1)}, f32[2,8,16,128]{3,2,1,0:T(8,128)S(1)}, u32[]{:S(2)}, u32[]{:S(2)}) %collective-permute-start.8) | collective-permute-done | bytes 131104 | tf_op jit(solution)/shard_map/ppermute | solution.py:360
  26.1 0.8 %collective-permute-start.7 = (f32[2,8,16,128]{3,2,1,0:T(8,128)S(1)}, f32[2,8,16,128]{3,2,1,0:T(8,128)S(1)}, u32[]{:S(2)}, u32[]{:S(2)}) collective-permute-start(f32[2,8,16,128]{3,2,1,0:T(8,128)S(1)} %collective-permute-done.6.refs_2_), channel_id=1, source_target_pairs={{1,0},{0,1},{3,2},{2,3},{5,4},{4,5},{7,6},{6,7},{9,8},{8,9},{11,10... | collective-permute-start | bytes 393224 | tf_op jit(solution)/shard_map/ppermute | solution.py:369
  26.9 0.0 collective-permute-done.2.rest_0_
  26.9 0.0 collective-permute-start.9
  26.9 0.0 collective-permute-done.3.rest_1_
  26.9 0.0 collective-permute-done.4.rest_2_
  26.9 0.0 copy-done.2
  26.9 12.0 %shard_map.76 = (f32[32,32,128]{2,1,0:T(8,128)}, f32[32,32,128]{2,1,0:T(8,128)}, f32[8,16,128]{2,1,0:T(8,128)S(1)}) custom-call(f32[32,32,128]{2,1,0:T(8,128)S(1)} %copy-done, f32[32,32,128]{2,1,0:T(8,128)S(1)} %copy-done.2, f32[32,32,128]{2,1,0:T(8,128)S(1)} %get-tuple-element.14.g_in, f32[13,32,128]{2,1,0:T(8,128)S(1)} %collective-permute-done.ra_ref, ...), custom_call_target="tpu_custom_call" | custom-call | tf_op jit(solution)/shard_map/pallas_call | solution.py:336
  38.9 2.4 %collective-permute-start.11 = (f32[8,16,128]{2,1,0:T(8,128)S(1)}, f32[8,16,128]{2,1,0:T(8,128)S(1)}, u32[]{:S(2)}, u32[]{:S(2)}) collective-permute-start(f32[8,16,128]{2,1,0:T(8,128)S(1)} %get-tuple-element.21.refs_6_), channel_id=1, source_target_pairs={{0,2},{4,6},{8,10},{12,14},{16,18},{20,22},{24,26},{28,30},{2,0},{... | collective-permute-start | bytes 196616 | tf_op jit(solution)/shard_map/ppermute | solution.py:357
  41.2 2.2 %collective-permute-start.13 = (f32[8,16,128]{2,1,0:T(8,128)S(1)}, f32[8,16,128]{2,1,0:T(8,128)S(1)}, u32[]{:S(2)}, u32[]{:S(2)}) collective-permute-start(f32[8,16,128]{2,1,0:T(8,128)S(1)} %get-tuple-element.21.refs_6_), channel_id=1, source_target_pairs={{2,4},{6,8},{10,12},{14,16},{18,20},{22,24},{26,28},{4,2},{8,6},{1... | collective-permute-start | bytes 196616 | tf_op jit(solution)/shard_map/ppermute | solution.py:360
  43.4 0.0 collective-permute-done.5.refs_1_
  43.4 1.1 %collective-permute-start.10 = (f32[8,16,128]{2,1,0:T(8,128)S(1)}, f32[8,16,128]{2,1,0:T(8,128)S(1)}, u32[]{:S(2)}, u32[]{:S(2)}) collective-permute-start(f32[8,16,128]{2,1,0:T(8,128)S(1)} %get-tuple-element.21.refs_6_), channel_id=1, source_target_pairs={{1,0},{0,1},{3,2},{2,3},{5,4},{4,5},{7,6},{6,7},{9,8},{8,9},{11,10... | collective-permute-start | bytes 196616 | tf_op jit(solution)/shard_map/ppermute | solution.py:369
  44.5 0.0 collective-permute-done.11.refs_8_
  44.5 0.1 collective-permute-start.12
  44.6 2.5 %collective-permute-done.13.refs_10_ = f32[8,16,128]{2,1,0:T(8,128)S(1)} collective-permute-done((f32[8,16,128]{2,1,0:T(8,128)S(1)}, f32[8,16,128]{2,1,0:T(8,128)S(1)}, u32[]{:S(2)}, u32[]{:S(2)}) %collective-permute-start.13) | collective-permute-done | bytes 65568 | tf_op jit(solution)/shard_map/ppermute | solution.py:360
  47.1 1.9 %collective-permute-start.14 = (f32[8,16,128]{2,1,0:T(8,128)S(1)}, f32[8,16,128]{2,1,0:T(8,128)S(1)}, u32[]{:S(2)}, u32[]{:S(2)}) collective-permute-start(f32[8,16,128]{2,1,0:T(8,128)S(1)} %collective-permute-done.13.refs_10_), channel_id=1, source_target_pairs={{1,0},{0,1},{3,2},{2,3},{5,4},{4,5},{7,6},{6,7},{9,8},{8,9},{11,10... | collective-permute-start | bytes 196616 | tf_op jit(solution)/shard_map/ppermute | solution.py:369
  49.0 0.0 collective-permute-done.7.refs_3_
  49.1 0.0 collective-permute-done.9.refs_5_
  49.1 0.0 collective-permute-done.10.refs_7_
  49.1 0.0 collective-permute-done.12.refs_9_
  49.1 0.9 %collective-permute-done.14.refs_11_ = f32[8,16,128]{2,1,0:T(8,128)S(1)} collective-permute-done((f32[8,16,128]{2,1,0:T(8,128)S(1)}, f32[8,16,128]{2,1,0:T(8,128)S(1)}, u32[]{:S(2)}, u32[]{:S(2)}) %collective-permute-start.14) | collective-permute-done | bytes 65568 | tf_op jit(solution)/shard_map/ppermute | solution.py:369
  50.0 19.9 %shard_map.77 = (f32[16,16,64]{2,1,0:T(8,128)}, f32[8,8,32]{2,1,0:T(8,128)}) custom-call(f32[2,8,16,128]{3,2,1,0:T(8,128)S(1)} %get-tuple-element.20.refs_0_, f32[2,8,16,128]{3,2,1,0:T(8,128)S(1)} %collective-permute-done.5.refs_1_, f32[2,8,16,128]{3,2,1,0:T(8,128)S(1)} %collective-permute-done.6.refs_2_, ...), custom_call_target="tpu_custom_call" | custom-call | tf_op jit(solution)/shard_map/pallas_call | solution.py:336
Async XLA Ops:
  0.6 1.0 %copy-start = (f32[32,32,128]{2,1,0:T(8,128)S(1)}, f32[32,32,128]{2,1,0:T(8,128)}, u32[]{:S(2)}) copy-start(f32[32,32,128]{2,1,0:T(8,128)} %src_ref.3) | copy-start | bytes 1572868
  1.7 1.0 %copy-start.1 = (f32[32,32,128]{2,1,0:T(8,128)S(1)}, f32[32,32,128]{2,1,0:T(8,128)}, u32[]{:S(2)}) copy-start(f32[32,32,128]{2,1,0:T(8,128)} %ab_ref.3) | copy-start | bytes 1572868
  2.7 1.0 %copy-start.3 = (f32[32,32,128]{2,1,0:T(8,128)S(1)}, f32[32,32,128]{2,1,0:T(8,128)}, u32[]{:S(2)}) copy-start(f32[32,32,128]{2,1,0:T(8,128)} %kap_ref.1) | copy-start | bytes 1572868
  3.8 0.7 copy-start.4
  4.5 22.4 %copy-start.2 = (f32[32,32,128]{2,1,0:T(8,128)S(1)}, f32[32,32,128]{2,1,0:T(8,128)}, u32[]{:S(2)}) copy-start(f32[32,32,128]{2,1,0:T(8,128)} %ab_ref.3) | copy-start | bytes 1572868
  4.9 6.2 %collective-permute-start = (f32[13,32,128]{2,1,0:T(8,128)S(1)}, f32[13,32,128]{2,1,0:T(8,128)S(1)}, u32[]{:S(2)}, u32[]{:S(2)}) collective-permute-start(f32[13,32,128]{2,1,0:T(8,128)S(1)} %get-tuple-element.15), channel_id=1, source_target_pairs={{0,2},{4,6},{8,10},{12,14},{16,18},{20,22},{24,26},{28,30},{2,0},{... | collective-permute-start | bytes 638984 | tf_op jit(solution)/shard_map/ppermute | solution.py:357
  5.2 12.0 %collective-permute-start.1 = (f32[13,32,128]{2,1,0:T(8,128)S(1)}, f32[13,32,128]{2,1,0:T(8,128)S(1)}, u32[]{:S(2)}, u32[]{:S(2)}) collective-permute-start(f32[13,32,128]{2,1,0:T(8,128)S(1)} %get-tuple-element.16), channel_id=1, source_target_pairs={{2,4},{6,8},{10,12},{14,16},{18,20},{22,24},{26,28},{4,2},{8,6},{1... | collective-permute-start | bytes 638984 | tf_op jit(solution)/shard_map/ppermute | solution.py:360
  9.3 17.6 %collective-permute-start.2 = (f32[3,32,8,128]{3,2,1,0:T(8,128)S(1)}, f32[3,32,8,128]{3,2,1,0:T(8,128)S(1)}, u32[]{:S(2)}, u32[]{:S(2)}) collective-permute-start(f32[3,32,8,128]{3,2,1,0:T(8,128)S(1)} %get-tuple-element.17), channel_id=1, source_target_pairs={{1,0},{0,1},{3,2},{2,3},{5,4},{4,5},{7,6},{6,7},{9,8},{8,9},{11,10... | collective-permute-start | bytes 1179656 | tf_op jit(solution)/shard_map/ppermute | solution.py:369
  11.1 15.8 %collective-permute-start.3 = (f32[13,32,128]{2,1,0:T(8,128)S(1)}, f32[13,32,128]{2,1,0:T(8,128)S(1)}, u32[]{:S(2)}, u32[]{:S(2)}) collective-permute-start(f32[13,32,128]{2,1,0:T(8,128)S(1)} %collective-permute-done.ra_ref), channel_id=1, source_target_pairs={{1,0},{0,1},{3,2},{2,3},{5,4},{4,5},{7,6},{6,7},{9,8},{8,9},{11,10... | collective-permute-start | bytes 638984 | tf_op jit(solution)/shard_map/ppermute | solution.py:369
  17.2 9.7 %collective-permute-start.4 = (f32[13,32,128]{2,1,0:T(8,128)S(1)}, f32[13,32,128]{2,1,0:T(8,128)S(1)}, u32[]{:S(2)}, u32[]{:S(2)}) collective-permute-start(f32[13,32,128]{2,1,0:T(8,128)S(1)} %collective-permute-done.1.rb_ref), channel_id=1, source_target_pairs={{1,0},{0,1},{3,2},{2,3},{5,4},{4,5},{7,6},{6,7},{9,8},{8,9},{11,10... | collective-permute-start | bytes 638984 | tf_op jit(solution)/shard_map/ppermute | solution.py:369
  18.2 5.1 %collective-permute-start.6 = (f32[2,8,16,128]{3,2,1,0:T(8,128)S(1)}, f32[2,8,16,128]{3,2,1,0:T(8,128)S(1)}, u32[]{:S(2)}, u32[]{:S(2)}) collective-permute-start(f32[2,8,16,128]{3,2,1,0:T(8,128)S(1)} %get-tuple-element.20.refs_0_), channel_id=1, source_target_pairs={{0,2},{4,6},{8,10},{12,14},{16,18},{20,22},{24,26},{28,30},{2,0},{... | collective-permute-start | bytes 393224 | tf_op jit(solution)/shard_map/ppermute | solution.py:357
  18.2 7.9 %collective-permute-start.8 = (f32[2,8,16,128]{3,2,1,0:T(8,128)S(1)}, f32[2,8,16,128]{3,2,1,0:T(8,128)S(1)}, u32[]{:S(2)}, u32[]{:S(2)}) collective-permute-start(f32[2,8,16,128]{3,2,1,0:T(8,128)S(1)} %get-tuple-element.20.refs_0_), channel_id=1, source_target_pairs={{2,4},{6,8},{10,12},{14,16},{18,20},{22,24},{26,28},{4,2},{8,6},{1... | collective-permute-start | bytes 393224 | tf_op jit(solution)/shard_map/ppermute | solution.py:360
  23.3 20.1 %collective-permute-start.5 = (f32[2,8,16,128]{3,2,1,0:T(8,128)S(1)}, f32[2,8,16,128]{3,2,1,0:T(8,128)S(1)}, u32[]{:S(2)}, u32[]{:S(2)}) collective-permute-start(f32[2,8,16,128]{3,2,1,0:T(8,128)S(1)} %get-tuple-element.20.refs_0_), channel_id=1, source_target_pairs={{1,0},{0,1},{3,2},{2,3},{5,4},{4,5},{7,6},{6,7},{9,8},{8,9},{11,10... | collective-permute-start | bytes 393224 | tf_op jit(solution)/shard_map/ppermute | solution.py:369
  26.1 23.0 %collective-permute-start.7 = (f32[2,8,16,128]{3,2,1,0:T(8,128)S(1)}, f32[2,8,16,128]{3,2,1,0:T(8,128)S(1)}, u32[]{:S(2)}, u32[]{:S(2)}) collective-permute-start(f32[2,8,16,128]{3,2,1,0:T(8,128)S(1)} %collective-permute-done.6.refs_2_), channel_id=1, source_target_pairs={{1,0},{0,1},{3,2},{2,3},{5,4},{4,5},{7,6},{6,7},{9,8},{8,9},{11,10... | collective-permute-start | bytes 393224 | tf_op jit(solution)/shard_map/ppermute | solution.py:369
  26.9 22.2 %collective-permute-start.9 = (f32[2,8,16,128]{3,2,1,0:T(8,128)S(1)}, f32[2,8,16,128]{3,2,1,0:T(8,128)S(1)}, u32[]{:S(2)}, u32[]{:S(2)}) collective-permute-start(f32[2,8,16,128]{3,2,1,0:T(8,128)S(1)} %collective-permute-done.8.refs_4_), channel_id=1, source_target_pairs={{1,0},{0,1},{3,2},{2,3},{5,4},{4,5},{7,6},{6,7},{9,8},{8,9},{11,10... | collective-permute-start | bytes 393224 | tf_op jit(solution)/shard_map/ppermute | solution.py:369
  38.9 5.7 %collective-permute-start.11 = (f32[8,16,128]{2,1,0:T(8,128)S(1)}, f32[8,16,128]{2,1,0:T(8,128)S(1)}, u32[]{:S(2)}, u32[]{:S(2)}) collective-permute-start(f32[8,16,128]{2,1,0:T(8,128)S(1)} %get-tuple-element.21.refs_6_), channel_id=1, source_target_pairs={{0,2},{4,6},{8,10},{12,14},{16,18},{20,22},{24,26},{28,30},{2,0},{... | collective-permute-start | bytes 196616 | tf_op jit(solution)/shard_map/ppermute | solution.py:357
  41.2 5.9 %collective-permute-start.13 = (f32[8,16,128]{2,1,0:T(8,128)S(1)}, f32[8,16,128]{2,1,0:T(8,128)S(1)}, u32[]{:S(2)}, u32[]{:S(2)}) collective-permute-start(f32[8,16,128]{2,1,0:T(8,128)S(1)} %get-tuple-element.21.refs_6_), channel_id=1, source_target_pairs={{2,4},{6,8},{10,12},{14,16},{18,20},{22,24},{26,28},{4,2},{8,6},{1... | collective-permute-start | bytes 196616 | tf_op jit(solution)/shard_map/ppermute | solution.py:360
  43.4 5.7 %collective-permute-start.10 = (f32[8,16,128]{2,1,0:T(8,128)S(1)}, f32[8,16,128]{2,1,0:T(8,128)S(1)}, u32[]{:S(2)}, u32[]{:S(2)}) collective-permute-start(f32[8,16,128]{2,1,0:T(8,128)S(1)} %get-tuple-element.21.refs_6_), channel_id=1, source_target_pairs={{1,0},{0,1},{3,2},{2,3},{5,4},{4,5},{7,6},{6,7},{9,8},{8,9},{11,10... | collective-permute-start | bytes 196616 | tf_op jit(solution)/shard_map/ppermute | solution.py:369
  44.5 4.5 %collective-permute-start.12 = (f32[8,16,128]{2,1,0:T(8,128)S(1)}, f32[8,16,128]{2,1,0:T(8,128)S(1)}, u32[]{:S(2)}, u32[]{:S(2)}) collective-permute-start(f32[8,16,128]{2,1,0:T(8,128)S(1)} %collective-permute-done.11.refs_8_), channel_id=1, source_target_pairs={{1,0},{0,1},{3,2},{2,3},{5,4},{4,5},{7,6},{6,7},{9,8},{8,9},{11,10... | collective-permute-start | bytes 196616 | tf_op jit(solution)/shard_map/ppermute | solution.py:369
  47.1 2.8 %collective-permute-start.14 = (f32[8,16,128]{2,1,0:T(8,128)S(1)}, f32[8,16,128]{2,1,0:T(8,128)S(1)}, u32[]{:S(2)}, u32[]{:S(2)}) collective-permute-start(f32[8,16,128]{2,1,0:T(8,128)S(1)} %collective-permute-done.13.refs_10_), channel_id=1, source_target_pairs={{1,0},{0,1},{3,2},{2,3},{5,4},{4,5},{7,6},{6,7},{9,8},{8,9},{11,10... | collective-permute-start | bytes 196616 | tf_op jit(solution)/shard_map/ppermute | solution.py:369

commit v2 on v1

v2 whole, which is shorter than its diff:
```python
import functools

import jax
import jax.numpy as jnp
from jax import lax
from jax.experimental import pallas as pl
from jax.experimental.pallas import tpu as pltpu
from jax.sharding import PartitionSpec as P

DEGREE = 4
COARSE_DEGREE = 6

STEP_SCALE = 4.0
SMOOTH_LOW = 0.3
SMOOTH_HIGH = 2.0
COARSE_LOW = 0.05

BRICK = 8
TILE = 8
VMEM_BYTES = 48 * 1024 * 1024


def chebyshev_constants(degree, lowest, highest):
    middle = (highest + lowest) / 2.0
    spread = (highest - lowest) / 2.0
    relative = middle / spread
    previous = 1.0 / relative
    steps = []
    for _ in range(degree - 1):
        following = 1.0 / (2.0 * relative - previous)
        steps.append((following * previous, 2.0 * following / spread))
        previous = following
    return 1.0 / middle, steps


def lane_index(shape):
    return lax.broadcasted_iota(jnp.int32, shape, len(shape) - 1)


def ahead(value, axis, step=1):
    return pltpu.roll(value, value.shape[axis] - step, axis)


def behind(value, axis, step=1):
    return pltpu.roll(value, step, axis)


def positive(value):
    return jnp.where(value > 0.0, 1.0, 0.0)


def rows_loop(start, stop, body, block=14):
    count = stop - start
    if count <= 0:
        return
    loops = -(-count // block)
    size = count // loops

    def run(j, carry):
        for t in range(size):
            body(start + j * size + t)
        return carry

    if loops > 1:
        lax.fori_loop(0, loops, run, 0)
    else:
        run(0, 0)
    for i in range(start + loops * size, stop):
        body(i)


def level_setup(lo, hi, zstep, factor, g_ref, a_ref, wx_ref, wy_ref, wz_ref, inv_ref, d_ref):
    half = 0.5 * factor

    def weight_x(i):
        here, there = g_ref[i], g_ref[i + 1]
        wx_ref[i] = jnp.where((here > 0.0) & (there > 0.0), half * (here + there), 0.0)

    weight_x(lo - 1)

    def row(i):
        weight_x(i)
        here = g_ref[i]
        lanes = lane_index(here.shape)
        inside = here > 0.0
        there_y = ahead(here, 0)
        there_z = ahead(here, 1, zstep)
        wy = jnp.where(inside & (there_y > 0.0), half * (here + there_y), 0.0)
        wz = jnp.where(inside & (there_z > 0.0) & (lanes < here.shape[1] - zstep), half * (here + there_z), 0.0)
        wy_ref[i] = wy
        wz_ref[i] = wz
        faces = [wx_ref[i], wx_ref[i - 1], wy, behind(wy, 0), wz, behind(wz, 1, zstep)]
        wall = factor * a_ref[i]
        diagonal = 1.0 + jnp.where(faces[0] > 0.0, faces[0], wall)
        for face in faces[1:]:
            diagonal = diagonal + jnp.where(face > 0.0, face, wall)
        d_ref[i] = diagonal
        inv_ref[i] = jnp.where(inside, 1.0 / diagonal, 0.0)

    rows_loop(lo, hi, row)


def level_start(lo, hi, lowest, b_ref, inv_ref, e_ref, u_ref):
    first, _ = chebyshev_constants(1, lowest, SMOOTH_HIGH)

    def row(i):
        e = inv_ref[i] * b_ref[i]
        e_ref[i] = e
        u_ref[i] = e * first

    rows_loop(lo, hi, row)


def level_pass(lo, hi, k, degree, lowest, zstep, inv_ref, wx_ref, wy_ref, wz_ref, e_ref, u_refs):
    _, steps = chebyshev_constants(degree, lowest, SMOOTH_HIGH)
    old = u_refs[k]

    def row(i):
        u = old[i]
        wy = wy_ref[i]
        wz = wz_ref[i]
        coupled = wx_ref[i] * old[i + 1] + wx_ref[i - 1] * old[i - 1]
        coupled = coupled + (wy * ahead(u, 0) + behind(wy * u, 0))
        coupled = coupled + (wz * ahead(u, 1, zstep) + behind(wz * u, 1, zstep))
        e = e_ref[i] - u + inv_ref[i] * coupled
        e_ref[i] = e
        if k + 1 < degree:
            u_refs[k + 1][i] = steps[k][0] * u + steps[k][1] * e

    rows_loop(lo, hi, row)


def level_sweeps(base, size, reach, degree, lowest, keep, zstep, b_ref, inv_ref, wx_ref, wy_ref, wz_ref, e_ref, u_refs):
    passes = degree if keep else degree - 1
    width = reach + passes
    level_start(base - width, base + size + width, lowest, b_ref, inv_ref, e_ref, u_refs[0])
    for k in range(passes):
        width = reach + passes - 1 - k
        level_pass(
            base - width, base + size + width, k, degree, lowest, zstep, inv_ref, wx_ref, wy_ref, wz_ref, e_ref, u_refs
        )


def coarsen_rows(one, two, pair_ref, zstep):
    pair_ref[...] = one + two
    half = pair_ref.shape[0] // 2
    summed = pair_ref[pl.ds(0, half, 2), :] + pair_ref[pl.ds(1, half, 2), :]
    return (summed + ahead(summed, 1, zstep)) * 0.125


def pack_two(one, two):
    return jnp.where(lane_index(one.shape) % 2 == 0, one, behind(two, 1))


def unpack_two(packed):
    even = lane_index(packed.shape) % 2 == 0
    return jnp.where(even, packed, 0.0), jnp.where(even, ahead(packed, 1), 0.0)


def spread_mask(lines, spread, ny):
    wide = jnp.dot(lines.astype(jnp.float32), spread, preferred_element_type=jnp.float32)
    tiles = [jnp.broadcast_to(wide[by : by + 1], (BRICK, wide.shape[1])) for by in range(ny // BRICK)]
    return jnp.concatenate(tiles, axis=0)


def spread_matrix(nbz, nz):
    shape = (nbz, nz)
    column, line = lax.broadcasted_iota(jnp.int32, shape, 1), lax.broadcasted_iota(jnp.int32, shape, 0)
    return jnp.where(column // BRICK == line, 1.0, 0.0)


def start_all(copies, sems):
    started = [pltpu.make_async_copy(src, dst, sems.at[n]) for n, (src, dst) in enumerate(copies)]
    for copy in started:
        copy.start()
    return started


def edge_kernel(src_hbm, kap_hbm, ab_hbm, brick_hbm, a_out, b_out, bricks, sems):
    nx, ny, nz = src_hbm.shape
    lower, upper = DEGREE, DEGREE + 1
    even = lax.axis_index("dom") % 2 == 0
    copies = [(brick_hbm, bricks)]
    ups = (even, jnp.logical_not(even))
    for out, up in zip((a_out, b_out), ups):
        four = pl.ds(jnp.where(up, nx - lower, 0), lower)
        five = pl.ds(jnp.where(up, nx - upper, 0), upper)
        copies += [
            (kap_hbm.at[five], out.at[pl.ds(2 * lower, upper)]),
            (src_hbm.at[four], out.at[pl.ds(0, lower)]),
            (ab_hbm.at[four], out.at[pl.ds(lower, lower)]),
        ]
    started = start_all(copies, sems)
    for copy in started:
        copy.wait()
    nbx, _, nbz = bricks.shape
    spread = spread_matrix(nbz, nz)
    for out, up in zip((a_out, b_out), ups):
        mask = spread_mask(bricks[jnp.where(up, nbx - 1, 0)], spread, ny)
        for j in range(upper):
            out[2 * lower + j] = out[2 * lower + j] * mask


def block_kernel(slots, src_hbm, kap_hbm, ab_hbm, brick_hbm, _, b_ref, a_ref, g_ref, q_ref, *rest):
    y_outs, (bricks, pair_ref, sems) = rest[:slots], rest[slots:]
    nx, ny, nz = src_hbm.shape
    started = start_all([(brick_hbm, bricks), (kap_hbm, g_ref), (ab_hbm, a_ref), (src_hbm, b_ref)], sems)
    spread = spread_matrix(bricks.shape[2], nz)
    started[0].wait()
    started[1].wait()
    for bx in range(nx // BRICK):
        mask = spread_mask(bricks[bx], spread, ny)
        for x in range(bx * BRICK, (bx + 1) * BRICK):
            g_ref[x] = g_ref[x] * mask

    def packed_rows(field, ref):
        for j in range(nx // 4):
            cells = []
            for t in range(2):
                x = 4 * j + 2 * t
                scratch = pair_ref.at[(field * (nx // 4) + j) * 2 + t]
                cells.append(coarsen_rows(ref[x], ref[x + 1], scratch, 1))
            q_ref[field, j] = pack_two(*cells)

    packed_rows(0, g_ref)
    started[2].wait()
    packed_rows(1, a_ref)
    started[3].wait()

    for slot, out in enumerate(y_outs):
        at = pl.multiple_of(jnp.where(sends_up(slots, slot), ny - TILE, 0), TILE)
        for x in range(nx):
            out[0, x] = b_ref[x, pl.ds(at, TILE), :]
            out[1, x] = a_ref[x, pl.ds(at, TILE), :]
            out[2, x] = g_ref[x, pl.ds(at, TILE), :]


def sends_up(slots, slot):
    return lax.axis_index("grp") == 0 if slots == 1 else slot == 1


def slot_is_upper(slots, slot):
    return lax.axis_index("grp") == 0 if slots == 1 else slot == 0


def keep_near(value, is_upper, reach):
    rows = lax.broadcasted_iota(jnp.int32, value.shape, 0)
    size = value.shape[0]
    low = jnp.where(is_upper, 0, size - reach)
    high = jnp.where(is_upper, reach, size)
    return jnp.where((rows >= low) & (rows < high), value, 0.0)


def pack_rows(j, row, pair_ref):
    cells = []
    for t in range(2):
        x = 4 * j + 2 * t
        cells.append(coarsen_rows(row(x), row(x + 1), pair_ref.at[2 * j + t], 1))
    return pack_two(*cells)


def inner_packs(nx):
    first = -(-(DEGREE + 1) // 4)
    return range(first, nx // 4 - first)


class Joined:
    def __init__(self, own_ref, y_refs, field):
        self.own_ref, self.y_refs, self.field = own_ref, y_refs, field

    def __getitem__(self, x):
        parts = [self.own_ref[x]]
        for slot, y_ref in enumerate(self.y_refs):
            tile = y_ref[self.field, x]
            if self.field == 2:
                tile = keep_near(tile, slot_is_upper(len(self.y_refs), slot), DEGREE + 1)
            parts.append(tile)
        return jnp.concatenate(parts, axis=0)


class Rim:
    def __init__(self, nx, new_ref, before=None):
        self.nx, self.new_ref, self.before, self.written = nx, new_ref, before, set()

    def place(self, x):
        rows = self.new_ref.shape[0]
        return x + DEGREE + 1 if x < self.nx // 2 else rows - (self.nx + DEGREE + 1) + x

    def __getitem__(self, x):
        return self.new_ref[self.place(x)] if x in self.written else self.before[x]

    def __setitem__(self, x, value):
        self.new_ref[self.place(x)] = value
        self.written.add(x)


def inner_kernel(slots, *refs):
    b_in, a_in, g_in = refs[:3]
    y_refs = refs[3 : 3 + slots]
    wx, wy, wz, inv, d_ref, e_ref, u0, u1, u2, u3, it_out, res_out, s_ref, pair_ref = refs[3 + slots :]
    nx, ny, _ = b_in.shape
    b_ref, a_ref, g_ref = (Joined(ref, y_refs, field) for field, ref in enumerate((b_in, a_in, g_in)))
    u_refs = (u0, u1, u2, u3)
    level_setup(1, nx - 1, 1, STEP_SCALE, g_ref, a_ref, wx, wy, wz, inv, d_ref)
    level_start(1, nx - 1, SMOOTH_LOW, b_ref, inv, e_ref, u0)
    for k in range(DEGREE):
        level_pass(2 + k, nx - 2 - k, k, DEGREE, SMOOTH_LOW, 1, inv, wx, wy, wz, e_ref, u_refs)

    def finish(x):
        it_out[x] = (u0[x, :ny] + u1[x, :ny]) + (u2[x, :ny] + u3[x, :ny])
        res_out[x] = d_ref[x, :ny] * e_ref[x, :ny]

    rows_loop(DEGREE + 1, nx - DEGREE - 1, finish)
    for j in inner_packs(nx):
        s_ref[j] = pack_rows(j, lambda x: res_out[x], pair_ref)


def corner_kernel(slots, ra_ref, rb_ref, _, *outs):
    rows, ny, _ = ra_ref.shape
    for slot, out in enumerate(outs):
        at = pl.multiple_of(jnp.where(sends_up(slots, slot), ny - TILE, 0), TILE)
        for j in range(rows):
            out[0, j] = ra_ref[j, pl.ds(at, TILE), :]
            out[1, j] = rb_ref[j, pl.ds(at, TILE), :]


def gather_kernel(a_ref, b_ref, *refs):
    out = refs[-1]
    for j in range(a_ref.shape[0]):
        out[0, j] = a_ref[j]
        out[1, j] = b_ref[j]


def rim_kernel(slots, *refs):
    b_in, a_in, g_in = refs[:3]
    y_refs = refs[3 : 3 + slots]
    before, refs = refs[3 + slots : 13 + slots], refs[13 + slots :]
    res_in, s_in, ra_ref, rb_ref = refs[:4]
    c_refs = refs[4 : 4 + slots]
    it_out, res_out, s_ref = refs[4 + slots : 7 + slots]
    scratch, pair_ref = refs[7 + slots : -1], refs[-1]
    nx, ny, _ = b_in.shape
    lower, upper = DEGREE, DEGREE + 1

    b_ref, a_ref, g_ref = (
        Rim(nx, scratch[field], Joined(ref, y_refs, field)) for field, ref in enumerate((b_in, a_in, g_in))
    )
    wx, wy, wz, inv, d_ref, e_ref, *u_refs = (Rim(nx, new, old) for new, old in zip(scratch[3:], before))

    even = lax.axis_index("dom") % 2 == 0

    def received(j, is_above):
        from_even = even if is_above else jnp.logical_not(even)
        parts = [jnp.where(from_even, ra_ref[j], rb_ref[j])]
        for slot in range(slots):
            is_upper = slot_is_upper(slots, slot)
            tile = jnp.where(from_even, c_refs[slot][0, j], c_refs[slot][1, j])
            if j >= 2 * lower:
                tile = keep_near(tile, is_upper, upper)
            parts.append(tile)
        return jnp.concatenate(parts, axis=0)

    for is_above in (False, True):
        for j in range(lower):
            x = nx + j if is_above else j - lower
            b_ref[x] = received(j, is_above)
            a_ref[x] = received(lower + j, is_above)
        for j in range(upper):
            x = nx + j if is_above else j - upper
            g_ref[x] = received(2 * lower + j, is_above)

    for lo, hi in ((-lower, 1), (nx - 1, nx + lower)):
        level_setup(lo, hi, 1, STEP_SCALE, g_ref, a_ref, wx, wy, wz, inv, d_ref)
        level_start(lo, hi, SMOOTH_LOW, b_ref, inv, e_ref, u_refs[0])
    for k in range(DEGREE):
        out = DEGREE - 1 - k
        for lo, hi in ((-out, 2 + k), (nx - 2 - k, nx + out)):
            level_pass(lo, hi, k, DEGREE, SMOOTH_LOW, 1, inv, wx, wy, wz, e_ref, u_refs)

    place = {x: x for x in range(upper)}
    place.update({nx - upper + x: upper + x for x in range(upper)})
    for x, at in place.items():
        total = [u_ref[x][:ny] for u_ref in u_refs]
        it_out[at] = (total[0] + total[1]) + (total[2] + total[3])
        res_out[at] = d_ref[x][:ny] * e_ref[x][:ny]
    inner = inner_packs(nx)
    for j in range(nx // 4):
        if j in inner:
            s_ref[j] = s_in[j]
        else:
            s_ref[j] = pack_rows(j, lambda x: res_out[place[x]] if x in place else res_in[x], pair_ref)


def output_kernel(it_in, res_in, it_rim, res_rim, it_out, res_out, done_ref, sems):
    done_ref[...] = jnp.zeros_like(done_ref)
    nx = it_in.shape[0]
    rim = DEGREE + 1
    copies = []
    for inside, near, out in ((it_in, it_rim, it_out), (res_in, res_rim, res_out)):
        middle = pl.ds(rim, nx - 2 * rim)
        copies += [
            (inside.at[middle], out.at[middle]),
            (near.at[pl.ds(0, rim)], out.at[pl.ds(0, rim)]),
            (near.at[pl.ds(rim, rim)], out.at[pl.ds(nx - rim, rim)]),
        ]
    for copy in start_all(copies, sems):
        copy.wait()


def compact(value, step):
    nz = value.shape[-1]
    shape = (nz, nz // step)
    pick = jnp.where(
        lax.broadcasted_iota(jnp.int32, shape, 0) == step * lax.broadcasted_iota(jnp.int32, shape, 1), 1.0, 0.0
    )
    return jnp.dot(value, pick, preferred_element_type=jnp.float32, precision=lax.Precision.HIGHEST)


def part_starts(nx):
    even = lax.axis_index("dom") % 2 == 0
    return [nx, jnp.where(even, 2 * nx, 0), jnp.where(even, 0, 2 * nx)]


def coefficient_kernel(slots, *refs):
    own_refs, around_refs, refs = refs[: 1 + slots], refs[1 + slots : 2 + 2 * slots], refs[2 + 2 * slots :]
    wx, wy, wz, inv, d_ref, cwx, cwy, cwz, cinv, a_ref, g_ref, ca, cg, cd, pair_ref = refs
    _, packed, ny, _ = own_refs[0].shape
    nx = 2 * packed
    base = nx

    for part, start in enumerate(part_starts(nx)):
        for slot in range(1 + slots):
            q_ref = around_refs[slot].at[part - 1] if part else own_refs[slot]
            at = slice(slot * ny, (slot + 1) * ny)
            for j in range(packed):
                g_rows, a_rows = unpack_two(q_ref[0, j]), unpack_two(q_ref[1, j])
                for t in range(2):
                    g_row = g_rows[t]
                    if slot:
                        g_row = keep_near(g_row, slot_is_upper(slots, slot - 1), ny - 1)
                    g_ref[start + 2 * j + t, at] = g_row
                    a_ref[start + 2 * j + t, at] = a_rows[t]

    width = 2 * (COARSE_DEGREE - 1) + DEGREE
    level_setup(base - width, base + nx + width, 2, STEP_SCALE / 4.0, g_ref, a_ref, wx, wy, wz, inv, d_ref)

    rows = cg.shape[0]
    offset = base - 2 * COARSE_DEGREE
    for i in range(rows):
        row = offset + 2 * i
        g0, g1 = g_ref[row], g_ref[row + 1]
        whole = coarsen_rows(positive(g0), positive(g1), pair_ref.at[3 * i], 2) > 0.75
        first = lane_index(whole.shape) % 4 == 0
        cg[i] = jnp.where(whole & first, coarsen_rows(g0, g1, pair_ref.at[3 * i + 1], 2), 0.0)
        ca[i] = coarsen_rows(a_ref[row], a_ref[row + 1], pair_ref.at[3 * i + 2], 2)
    level_setup(1, rows - 1, 4, STEP_SCALE / 16.0, cg, ca, cwx, cwy, cwz, cinv, cd)


def coarse_kernel(slots, *refs):
    own_refs, around_refs, refs = refs[: 1 + slots], refs[1 + slots : 2 + 2 * slots], refs[2 + 2 * slots :]
    wx, wy, wz, inv, d_ref, cwx, cwy, cwz, cinv, mid_out, coarse_out = refs[:11]
    b_ref, e_ref, u0, u1, u2, u3, cb, ce, v0, v1, v2, v3, v4, v5, pair_ref = refs[11:]
    packed, ny, nz = own_refs[0].shape
    nx = 2 * packed
    base = nx

    for part, start in enumerate(part_starts(nx)):
        for slot in range(1 + slots):
            s_ref = around_refs[slot].at[part - 1] if part else own_refs[slot]
            at = slice(slot * ny, (slot + 1) * ny)
            for j in range(packed):
                for t, b_row in enumerate(unpack_two(s_ref[j])):
                    b_ref[start + 2 * j + t, at] = b_row

    reach = 2 * (COARSE_DEGREE - 1)
    u_refs = (u0, u1, u2, u3)
    level_sweeps(base, nx, reach, DEGREE, SMOOTH_LOW, True, 2, b_ref, inv, wx, wy, wz, e_ref, u_refs)

    total = u0[base : base + nx, :ny]
    for u_ref in u_refs[1:]:
        total = total + u_ref[base : base + nx, :ny]
    mid_out[...] = compact(total.reshape(nx * ny, nz), 2).reshape(nx, ny, nz // 2)

    half, cny = nx // 2, ny // 2
    cbase = COARSE_DEGREE
    offset = base - 2 * cbase
    for i in range(1, half + 2 * cbase - 1):
        row = offset + 2 * i
        cb[i] = coarsen_rows(d_ref[row] * e_ref[row], d_ref[row + 1] * e_ref[row + 1], pair_ref.at[i], 2)

    v_refs = (v0, v1, v2, v3, v4, v5)
    level_sweeps(cbase, half, 0, COARSE_DEGREE, COARSE_LOW, False, 4, cb, cinv, cwx, cwy, cwz, ce, v_refs)
    total = v0[cbase : cbase + half, :cny]
    for v_ref in v_refs[1:]:
        total = total + v_ref[cbase : cbase + half, :cny]
    coarse_out[...] = compact(total.reshape(half * cny, nz), 4).reshape(half, cny, nz // 4)


def call(kernel, ins, outs, scratch=(), in_hbm=0, out_hbm=0):
    vmem, hbm = pl.BlockSpec(memory_space=pltpu.VMEM), pl.BlockSpec(memory_space=pltpu.HBM)
    return pl.pallas_call(
        kernel,
        out_shape=[jax.ShapeDtypeStruct(shape, jnp.float32) for shape in outs],
        in_specs=[hbm] * in_hbm + [vmem] * (len(ins) - in_hbm),
        out_specs=[hbm] * out_hbm + [vmem] * (len(outs) - out_hbm),
        scratch_shapes=[pltpu.VMEM(shape, jnp.float32) if isinstance(shape, tuple) else shape for shape in scratch],
        compiler_params=pltpu.CompilerParams(vmem_limit_bytes=VMEM_BYTES),
    )(*ins)


def body(source, conductivity, absorption, brick_mask):
    doms, grps = lax.axis_size("dom"), lax.axis_size("grp")
    slots = min(grps - 1, 2)
    nx, ny, nz = source.shape
    lower, upper = DEGREE, DEGREE + 1

    def pairing(first):
        pairs = [(i, i + 1) for i in range(first, doms - 1, 2)]
        return pairs + [(j, i) for i, j in pairs]

    def swap_even(array):
        return lax.ppermute(array, "dom", pairing(0))

    def swap_odd(array):
        return lax.ppermute(array, "dom", pairing(1))

    downward = [(i + 1, i) for i in range(grps - 1)]
    upward = [(i, i + 1) for i in range(grps - 1)]

    def along_grp(arrays):
        if slots == 0:
            return []
        if slots == 1:
            return [lax.ppermute(arrays[0], "grp", downward + upward)]
        return [lax.ppermute(arrays[0], "grp", downward), lax.ppermute(arrays[-1], "grp", upward)]

    fields = [pltpu.with_memory_space_constraint(x, pltpu.HBM) for x in (source, conductivity, absorption, brick_mask)]
    bricks = pltpu.VMEM(brick_mask.shape, brick_mask.dtype)
    payload = (2 * lower + upper, ny, nz)
    to_even, to_odd = call(
        edge_kernel, fields, [payload, payload], [bricks, pltpu.SemaphoreType.DMA((7,))], in_hbm=4
    )
    from_even, from_odd = swap_even(to_even), swap_odd(to_odd)

    packed = nx // 4
    small = (packed, ny // 2, nz)
    b_own, a_own, g_own, coeffs, *edges = call(
        functools.partial(block_kernel, slots),
        (*fields, to_even),
        [source.shape] * 3 + [(2, *small)] + [(3, nx, TILE, nz)] * slots,
        [bricks, (4 * packed, ny, nz), pltpu.SemaphoreType.DMA((4,))],
        in_hbm=4,
    )
    own = (b_own, a_own, g_own, *along_grp(edges))
    coeffs_beside = along_grp([coeffs])
    coeffs_even, coeffs_odd = swap_even(coeffs), swap_odd(coeffs)

    wide = (nx, ny + slots * TILE, nz)
    pairs = (nx // 2, ny, nz)
    *state, it_inner, res_inner, s_inner = call(
        functools.partial(inner_kernel, slots),
        own,
        [wide] * 10 + [source.shape, source.shape, small],
        [pairs],
    )
    corners = call(
        functools.partial(corner_kernel, slots),
        (from_even, from_odd, s_inner),
        [(2, payload[0], TILE, nz)] * slots,
    )
    corners_beside = along_grp(corners)
    (coeffs_around,) = call(gather_kernel, (coeffs_even, coeffs_odd, *corners_beside), [(2, 2, *small)])
    q_ins = [coeffs, *coeffs_beside, coeffs_around, *along_grp([coeffs_around])]
    rim = (2 * upper, ny, nz)
    near = (4 * upper + 2, ny + slots * TILE, nz)
    it_rim, res_rim, mid_source = call(
        functools.partial(rim_kernel, slots),
        (*own, *state, res_inner, s_inner, from_even, from_odd, *corners_beside),
        [rim, rim, small],
        [near] * 13 + [pairs],
    )
    fine_iterate, fine_residual, written = call(
        output_kernel,
        (it_inner, res_inner, it_rim, res_rim),
        [source.shape, source.shape, (TILE, nz)],
        [pltpu.SemaphoreType.DMA((6,))],
        out_hbm=2,
    )

    source_even, source_odd = swap_even(mid_source), swap_odd(mid_source)
    mid_y = (1 + slots) * ny // 2
    mid_wide = (3 * nx // 2, mid_y, nz)
    coarse_rows = nx // 4 + 2 * COARSE_DEGREE
    coarse_wide = (coarse_rows, mid_y // 2, nz)
    weights = call(
        functools.partial(coefficient_kernel, slots),
        q_ins,
        [mid_wide] * 5 + [coarse_wide] * 4,
        [mid_wide] * 2 + [coarse_wide] * 3 + [(3 * coarse_rows, mid_y, nz)],
    )
    (around,) = call(gather_kernel, (source_even, source_odd, weights[-1], written), [(2, *small)])
    s_ins = [mid_source, *along_grp([mid_source]), around, *along_grp([around])]
    mid_iterate, coarse_iterate = call(
        functools.partial(coarse_kernel, slots),
        (*s_ins, *weights),
        [(nx // 2, ny // 2, nz // 2), (nx // 4, ny // 4, nz // 4)],
        [mid_wide] * 6 + [coarse_wide] * 8 + [(coarse_rows, mid_y, nz)],
    )
    return (fine_iterate, fine_residual, mid_iterate, coarse_iterate)


def solution(mesh):
    spec = P("dom", "grp", None)
    return jax.shard_map(body, mesh=mesh, in_specs=(spec,) * 4, out_specs=(spec,) * 4, check_vma=False)
```

time: 70.5 us -> 42.5 us (0.60)
  the two profiles are of different devices: /device:TPU:19 before, /device:TPU:9 now
where the time goes in v2:
time: 42.5 us; the launch traced here: 42.2 us
  Pallas kernels  18.8 us (44%)
  starting transfers between devices  18.2 us (43%)
  waiting for transfers between devices  4.5 us (11%)
  between operations  0.75 us (2%)
    pallas_call x10, Pallas kernels, call(): pl.pallas_call(kernel, out_shape=[jax.ShapeDtypeStruct(shape, jnp.float32...  18.8 us
    ppermute x3, starting transfers between devices, swap_odd(): return lax.ppermute(array, 'dom', pairing(1))  7.66 us
    ppermute x3, starting transfers between devices, swap_even(): return lax.ppermute(array, 'dom', pairing(0))  5.84 us
    ppermute x6, starting transfers between devices, along_grp(): return [lax.ppermute(arrays[0], 'grp', downward + upward)]  4.71 us
    ppermute x3, waiting for transfers between devices, swap_odd(): return lax.ppermute(array, 'dom', pairing(1))  1.9 us
    ppermute x3, waiting for transfers between devices, swap_even(): return lax.ppermute(array, 'dom', pairing(0))  1.41 us
    ppermute x6, waiting for transfers between devices, along_grp(): return [lax.ppermute(arrays[0], 'grp', downward + upward)]  1.19 us
  transfers between devices with their start and end apart: 12, of which 3 were waited for; matrix products, arithmetic and copies ran while one was open for 0% of the time, Pallas kernels for 27%

profile of v2, /device:TPU:9, one launch (start us, length us, event | category | flops | bytes accessed | tf_op | source)
XLA Modules:
  0.0 42.2 jit_solution(4633235819371481107)
XLA Ops:
  0.6 1.2 %shard_map.75 = (f32[13,32,128]{2,1,0:T(8,128)S(1)}, f32[13,32,128]{2,1,0:T(8,128)S(1)}) custom-call(f32[32,32,128]{2,1,0:T(8,128)} %src_hbm.3, f32[32,32,128]{2,1,0:T(8,128)} %kap_hbm.3, f32[32,32,128]{2,1,0:T(8,128)} %ab_hbm.3, s32[4,4,16]{2,1,0:T(4,128)} %brick_hbm.3), custom_call_target="tpu_custom_call" | custom-call | tf_op jit(solution)/shard_map/pallas_call | solution.py:501
  1.9 1.7 %shard_map.76 = (f32[32,32,128]{2,1,0:T(8,128)S(1)}, f32[32,32,128]{2,1,0:T(8,128)S(1)}, f32[32,32,128]{2,1,0:T(8,128)S(1)}, f32[2,8,16,128]{3,2,1,0:T(8,128)S(1)}, f32[3,32,8,128]{3,2,1,0:T(8,128)S(1)}) custom-call(f32[32,32,128]{2,1,0:T(8,128)} %src_hbm.3, f32[32,32,128]{2,1,0:T(8,128)} %kap_hbm.3, f32[32,32,128]{2,1,0:T(8,128)} %ab_hbm.3, ...), custom_call_target="tpu_custom_call" | custom-call | tf_op jit(solution)/shard_map/pallas_call | solution.py:501
  3.5 0.7 %collective-permute-start = (f32[3,32,8,128]{3,2,1,0:T(8,128)S(1)}, f32[3,32,8,128]{3,2,1,0:T(8,128)S(1)}, u32[]{:S(2)}, u32[]{:S(2)}) collective-permute-start(f32[3,32,8,128]{3,2,1,0:T(8,128)S(1)} %get-tuple-element.45), channel_id=1, source_target_pairs={{1,0},{0,1},{3,2},{2,3},{5,4},{4,5},{7,6},{6,7},{9,8},{8,9},{11,10... | collective-permute-start | bytes 1179656 | tf_op jit(solution)/shard_map/ppermute | solution.py:534
  4.3 1.2 %collective-permute-start.1 = (f32[13,32,128]{2,1,0:T(8,128)S(1)}, f32[13,32,128]{2,1,0:T(8,128)S(1)}, u32[]{:S(2)}, u32[]{:S(2)}) collective-permute-start(f32[13,32,128]{2,1,0:T(8,128)S(1)} %get-tuple-element.41._), channel_id=1, source_target_pairs={{0,2},{4,6},{8,10},{12,14},{16,18},{20,22},{24,26},{28,30},{2,0},{... | collective-permute-start | bytes 638984 | tf_op jit(solution)/shard_map/ppermute | solution.py:522
  5.5 3.0 %collective-permute-start.2 = (f32[13,32,128]{2,1,0:T(8,128)S(1)}, f32[13,32,128]{2,1,0:T(8,128)S(1)}, u32[]{:S(2)}, u32[]{:S(2)}) collective-permute-start(f32[13,32,128]{2,1,0:T(8,128)S(1)} %get-tuple-element.59), channel_id=1, source_target_pairs={{2,4},{6,8},{10,12},{14,16},{18,20},{22,24},{26,28},{4,2},{8,6},{1... | collective-permute-start | bytes 638984 | tf_op jit(solution)/shard_map/ppermute | solution.py:525
  8.5 1.4 %collective-permute-start.8 = (f32[2,8,16,128]{3,2,1,0:T(8,128)S(1)}, f32[2,8,16,128]{3,2,1,0:T(8,128)S(1)}, u32[]{:S(2)}, u32[]{:S(2)}) collective-permute-start(f32[2,8,16,128]{3,2,1,0:T(8,128)S(1)} %get-tuple-element.65.refs_0_), channel_id=1, source_target_pairs={{0,2},{4,6},{8,10},{12,14},{16,18},{20,22},{24,26},{28,30},{2,0},{... | collective-permute-start | bytes 393224 | tf_op jit(solution)/shard_map/ppermute | solution.py:522
  9.9 2.8 %collective-permute-start.9 = (f32[2,8,16,128]{3,2,1,0:T(8,128)S(1)}, f32[2,8,16,128]{3,2,1,0:T(8,128)S(1)}, u32[]{:S(2)}, u32[]{:S(2)}) collective-permute-start(f32[2,8,16,128]{3,2,1,0:T(8,128)S(1)} %get-tuple-element.65.refs_0_), channel_id=1, source_target_pairs={{2,4},{6,8},{10,12},{14,16},{18,20},{22,24},{26,28},{4,2},{8,6},{1... | collective-permute-start | bytes 393224 | tf_op jit(solution)/shard_map/ppermute | solution.py:525
  12.7 0.0 collective-permute-done.refs_3_
  12.7 5.2 %shard_map.77 = (f32[32,40,128]{2,1,0:T(8,128)S(1)}, f32[32,40,128]{2,1,0:T(8,128)S(1)}, f32[32,40,128]{2,1,0:T(8,128)S(1)}, f32[32,40,128]{2,1,0:T(8,128)S(1)},...) custom-call(f32[32,32,128]{2,1,0:T(8,128)S(1)} %get-tuple-element.42, ...), custom_call_target="tpu_custom_call" | custom-call | tf_op jit(solution)/shard_map/pallas_call | solution.py:501
  17.9 0.0 collective-permute-done.1.ra_ref.refs_16_
  17.9 0.0 collective-permute-done.2.rb_ref.refs_17_
  17.9 1.0 %collective-permute-start.3 = (f32[2,13,8,128]{3,2,1,0:T(8,128)S(1)}, f32[2,13,8,128]{3,2,1,0:T(8,128)S(1)}, u32[]{:S(2)}, u32[]{:S(2)}) collective-permute-start(f32[2,13,8,128]{3,2,1,0:T(8,128)S(1)} %shard_map.78), channel_id=1, source_target_pairs={{1,0},{0,1},{3,2},{2,3},{5,4},{4,5},{7,6},{6,7},{9,8},{8,9},{11,10... | collective-permute-start | bytes 319496 | tf_op jit(solution)/shard_map/ppermute | solution.py:534
  18.9 1.4 %collective-permute-done.8.a_ref = f32[2,8,16,128]{3,2,1,0:T(8,128)S(1)} collective-permute-done((f32[2,8,16,128]{3,2,1,0:T(8,128)S(1)}, f32[2,8,16,128]{3,2,1,0:T(8,128)S(1)}, u32[]{:S(2)}, u32[]{:S(2)}) %collective-permute-start.8) | collective-permute-done | bytes 131104 | tf_op jit(solution)/shard_map/ppermute | solution.py:522
  20.3 0.0 collective-permute-done.9.b_ref
  20.3 0.0 collective-permute-done.3.refs_18_.refs_0_
  20.3 0.9 %collective-permute-start.10 = (f32[2,2,8,16,128]{4,3,2,1,0:T(8,128)S(1)}, f32[2,2,8,16,128]{4,3,2,1,0:T(8,128)S(1)}, u32[]{:S(2)}, u32[]{:S(2)}) collective-permute-start(f32[2,2,8,16,128]{4,3,2,1,0:T(8,128)S(1)} %shard_map.81.refs_2_), channel_id=1, source_target_pairs={{1,0},{0,1},{3,2},{2,3},{5,4},{4,5},{7,6},{6,7},{9,8},{8,9},{11,10... | collective-permute-start | bytes 786440 | tf_op jit(solution)/shard_map/ppermute | solution.py:534
  21.2 0.1 collective-permute-start.7
  21.3 3.2 %shard_map.79 = (f32[10,32,128]{2,1,0:T(8,128)S(1)}, f32[10,32,128]{2,1,0:T(8,128)S(1)}, f32[8,16,128]{2,1,0:T(8,128)S(1)}) custom-call(f32[32,32,128]{2,1,0:T(8,128)S(1)} %get-tuple-element.42.refs_0_, f32[32,32,128]{2,1,0:T(8,128)S(1)} %get-tuple-element.43.refs_1_, f32[32,32,128]{2,1,0:T(8,128)S(1)} %get-tuple-element.44.refs_2_, ...), custom_call_target="tpu_custom_call" | custom-call | tf_op jit(solution)/shard_map/pallas_call | solution.py:501
  24.5 3.2 %collective-permute-start.5 = (f32[8,16,128]{2,1,0:T(8,128)S(1)}, f32[8,16,128]{2,1,0:T(8,128)S(1)}, u32[]{:S(2)}, u32[]{:S(2)}) collective-permute-start(f32[8,16,128]{2,1,0:T(8,128)S(1)} %get-tuple-element.64.refs_0_), channel_id=1, source_target_pairs={{0,2},{4,6},{8,10},{12,14},{16,18},{20,22},{24,26},{28,30},{2,0},{... | collective-permute-start | bytes 196616 | tf_op jit(solution)/shard_map/ppermute | solution.py:522
  27.8 1.9 %collective-permute-start.6 = (f32[8,16,128]{2,1,0:T(8,128)S(1)}, f32[8,16,128]{2,1,0:T(8,128)S(1)}, u32[]{:S(2)}, u32[]{:S(2)}) collective-permute-start(f32[8,16,128]{2,1,0:T(8,128)S(1)} %get-tuple-element.64.refs_0_), channel_id=1, source_target_pairs={{2,4},{6,8},{10,12},{14,16},{18,20},{22,24},{26,28},{4,2},{8,6},{1... | collective-permute-start | bytes 196616 | tf_op jit(solution)/shard_map/ppermute | solution.py:525
  29.7 1.0 %shard_map.80 = (f32[32,32,128]{2,1,0:T(8,128)}, f32[32,32,128]{2,1,0:T(8,128)}, f32[8,128]{1,0:T(8,128)S(1)}) custom-call(f32[32,32,128]{2,1,0:T(8,128)S(1)} %get-tuple-element.46.it_in, f32[32,32,128]{2,1,0:T(8,128)S(1)} %get-tuple-element.47.refs_14_.res_in, f32[10,32,128]{2,1,0:T(8,128)S(1)} %get-tuple-element.60.it_rim, ...), custom_call_target="tpu_custom_call" | custom-call | tf_op jit(solution)/shard_map/pallas_call | solution.py:501
  30.7 0.0 collective-permute-done.7.refs_1_
  30.7 0.0 collective-permute-done.10.refs_3_
  30.7 1.9 %shard_map.82 = (f32[48,32,128]{2,1,0:T(8,128)S(1)}, f32[48,32,128]{2,1,0:T(8,128)S(1)}, f32[48,32,128]{2,1,0:T(8,128)S(1)}, f32[48,32,128]{2,1,0:T(8,128)S(1)},...) custom-call(f32[2,8,16,128]{3,2,1,0:T(8,128)S(1)} %get-tuple-element, ...), custom_call_target="tpu_custom_call" | custom-call | tf_op jit(solution)/shard_map/pallas_call | solution.py:501
  32.7 0.0 collective-permute-done.5.a_ref
  32.7 1.9 %collective-permute-done.6.b_ref = f32[8,16,128]{2,1,0:T(8,128)S(1)} collective-permute-done((f32[8,16,128]{2,1,0:T(8,128)S(1)}, f32[8,16,128]{2,1,0:T(8,128)S(1)}, u32[]{:S(2)}, u32[]{:S(2)}) %collective-permute-start.6) | collective-permute-done | bytes 65568 | tf_op jit(solution)/shard_map/ppermute | solution.py:525
  34.6 1.9 %collective-permute-start.11 = (f32[2,8,16,128]{3,2,1,0:T(8,128)S(1)}, f32[2,8,16,128]{3,2,1,0:T(8,128)S(1)}, u32[]{:S(2)}, u32[]{:S(2)}) collective-permute-start(f32[2,8,16,128]{3,2,1,0:T(8,128)S(1)} %shard_map.83.refs_2_), channel_id=1, source_target_pairs={{1,0},{0,1},{3,2},{2,3},{5,4},{4,5},{7,6},{6,7},{9,8},{8,9},{11,10... | collective-permute-start | bytes 393224 | tf_op jit(solution)/shard_map/ppermute | solution.py:534
  36.5 0.1 collective-permute-start.4
  36.6 1.2 %collective-permute-done.4.refs_1_ = f32[8,16,128]{2,1,0:T(8,128)S(1)} collective-permute-done((f32[8,16,128]{2,1,0:T(8,128)S(1)}, f32[8,16,128]{2,1,0:T(8,128)S(1)}, u32[]{:S(2)}, u32[]{:S(2)}) %collective-permute-start.4) | collective-permute-done | bytes 65568 | tf_op jit(solution)/shard_map/ppermute | solution.py:534
  37.8 0.0 collective-permute-done.11.refs_3_
  37.8 4.5 %shard_map.84 = (f32[16,16,64]{2,1,0:T(8,128)}, f32[8,8,32]{2,1,0:T(8,128)}) custom-call(f32[8,16,128]{2,1,0:T(8,128)S(1)} %get-tuple-element.64.refs_0_, f32[8,16,128]{2,1,0:T(8,128)S(1)} %collective-permute-done.4.refs_1_, f32[2,8,16,128]{3,2,1,0:T(8,128)S(1)} %shard_map.83.refs_2_, f32[2,8,16,128]{3,2,1,0:T(8,128)S(1)} %collective-permute-done.11.refs_3_, ...), custom_call_target="tpu_custom_call" | custom-call | tf_op jit(solution)/shard_map/pallas_call | solution.py:501
  (3 shorter events, 0.1 us)
Async XLA Ops:
  3.5 9.1 %collective-permute-start = (f32[3,32,8,128]{3,2,1,0:T(8,128)S(1)}, f32[3,32,8,128]{3,2,1,0:T(8,128)S(1)}, u32[]{:S(2)}, u32[]{:S(2)}) collective-permute-start(f32[3,32,8,128]{3,2,1,0:T(8,128)S(1)} %get-tuple-element.45), channel_id=1, source_target_pairs={{1,0},{0,1},{3,2},{2,3},{5,4},{4,5},{7,6},{6,7},{9,8},{8,9},{11,10... | collective-permute-start | bytes 1179656 | tf_op jit(solution)/shard_map/ppermute | solution.py:534
  4.3 13.6 %collective-permute-start.1 = (f32[13,32,128]{2,1,0:T(8,128)S(1)}, f32[13,32,128]{2,1,0:T(8,128)S(1)}, u32[]{:S(2)}, u32[]{:S(2)}) collective-permute-start(f32[13,32,128]{2,1,0:T(8,128)S(1)} %get-tuple-element.41._), channel_id=1, source_target_pairs={{0,2},{4,6},{8,10},{12,14},{16,18},{20,22},{24,26},{28,30},{2,0},{... | collective-permute-start | bytes 638984 | tf_op jit(solution)/shard_map/ppermute | solution.py:522
  5.5 12.4 %collective-permute-start.2 = (f32[13,32,128]{2,1,0:T(8,128)S(1)}, f32[13,32,128]{2,1,0:T(8,128)S(1)}, u32[]{:S(2)}, u32[]{:S(2)}) collective-permute-start(f32[13,32,128]{2,1,0:T(8,128)S(1)} %get-tuple-element.59), channel_id=1, source_target_pairs={{2,4},{6,8},{10,12},{14,16},{18,20},{22,24},{26,28},{4,2},{8,6},{1... | collective-permute-start | bytes 638984 | tf_op jit(solution)/shard_map/ppermute | solution.py:525
  8.5 11.8 %collective-permute-start.8 = (f32[2,8,16,128]{3,2,1,0:T(8,128)S(1)}, f32[2,8,16,128]{3,2,1,0:T(8,128)S(1)}, u32[]{:S(2)}, u32[]{:S(2)}) collective-permute-start(f32[2,8,16,128]{3,2,1,0:T(8,128)S(1)} %get-tuple-element.65.refs_0_), channel_id=1, source_target_pairs={{0,2},{4,6},{8,10},{12,14},{16,18},{20,22},{24,26},{28,30},{2,0},{... | collective-permute-start | bytes 393224 | tf_op jit(solution)/shard_map/ppermute | solution.py:522
  9.9 10.4 %collective-permute-start.9 = (f32[2,8,16,128]{3,2,1,0:T(8,128)S(1)}, f32[2,8,16,128]{3,2,1,0:T(8,128)S(1)}, u32[]{:S(2)}, u32[]{:S(2)}) collective-permute-start(f32[2,8,16,128]{3,2,1,0:T(8,128)S(1)} %get-tuple-element.65.refs_0_), channel_id=1, source_target_pairs={{2,4},{6,8},{10,12},{14,16},{18,20},{22,24},{26,28},{4,2},{8,6},{1... | collective-permute-start | bytes 393224 | tf_op jit(solution)/shard_map/ppermute | solution.py:525
  17.9 2.4 %collective-permute-start.3 = (f32[2,13,8,128]{3,2,1,0:T(8,128)S(1)}, f32[2,13,8,128]{3,2,1,0:T(8,128)S(1)}, u32[]{:S(2)}, u32[]{:S(2)}) collective-permute-start(f32[2,13,8,128]{3,2,1,0:T(8,128)S(1)} %shard_map.78), channel_id=1, source_target_pairs={{1,0},{0,1},{3,2},{2,3},{5,4},{4,5},{7,6},{6,7},{9,8},{8,9},{11,10... | collective-permute-start | bytes 319496 | tf_op jit(solution)/shard_map/ppermute | solution.py:534
  20.3 10.4 %collective-permute-start.10 = (f32[2,2,8,16,128]{4,3,2,1,0:T(8,128)S(1)}, f32[2,2,8,16,128]{4,3,2,1,0:T(8,128)S(1)}, u32[]{:S(2)}, u32[]{:S(2)}) collective-permute-start(f32[2,2,8,16,128]{4,3,2,1,0:T(8,128)S(1)} %shard_map.81.refs_2_), channel_id=1, source_target_pairs={{1,0},{0,1},{3,2},{2,3},{5,4},{4,5},{7,6},{6,7},{9,8},{8,9},{11,10... | collective-permute-start | bytes 786440 | tf_op jit(solution)/shard_map/ppermute | solution.py:534
  21.2 9.5 %collective-permute-start.7 = (f32[2,8,16,128]{3,2,1,0:T(8,128)S(1)}, f32[2,8,16,128]{3,2,1,0:T(8,128)S(1)}, u32[]{:S(2)}, u32[]{:S(2)}) collective-permute-start(f32[2,8,16,128]{3,2,1,0:T(8,128)S(1)} %get-tuple-element.65.refs_0_), channel_id=1, source_target_pairs={{1,0},{0,1},{3,2},{2,3},{5,4},{4,5},{7,6},{6,7},{9,8},{8,9},{11,10... | collective-permute-start | bytes 393224 | tf_op jit(solution)/shard_map/ppermute | solution.py:534
  24.5 8.1 %collective-permute-start.5 = (f32[8,16,128]{2,1,0:T(8,128)S(1)}, f32[8,16,128]{2,1,0:T(8,128)S(1)}, u32[]{:S(2)}, u32[]{:S(2)}) collective-permute-start(f32[8,16,128]{2,1,0:T(8,128)S(1)} %get-tuple-element.64.refs_0_), channel_id=1, source_target_pairs={{0,2},{4,6},{8,10},{12,14},{16,18},{20,22},{24,26},{28,30},{2,0},{... | collective-permute-start | bytes 196616 | tf_op jit(solution)/shard_map/ppermute | solution.py:522
  27.8 6.8 %collective-permute-start.6 = (f32[8,16,128]{2,1,0:T(8,128)S(1)}, f32[8,16,128]{2,1,0:T(8,128)S(1)}, u32[]{:S(2)}, u32[]{:S(2)}) collective-permute-start(f32[8,16,128]{2,1,0:T(8,128)S(1)} %get-tuple-element.64.refs_0_), channel_id=1, source_target_pairs={{2,4},{6,8},{10,12},{14,16},{18,20},{22,24},{26,28},{4,2},{8,6},{1... | collective-permute-start | bytes 196616 | tf_op jit(solution)/shard_map/ppermute | solution.py:525
  34.6 3.2 %collective-permute-start.11 = (f32[2,8,16,128]{3,2,1,0:T(8,128)S(1)}, f32[2,8,16,128]{3,2,1,0:T(8,128)S(1)}, u32[]{:S(2)}, u32[]{:S(2)}) collective-permute-start(f32[2,8,16,128]{3,2,1,0:T(8,128)S(1)} %shard_map.83.refs_2_), channel_id=1, source_target_pairs={{1,0},{0,1},{3,2},{2,3},{5,4},{4,5},{7,6},{6,7},{9,8},{8,9},{11,10... | collective-permute-start | bytes 393224 | tf_op jit(solution)/shard_map/ppermute | solution.py:534
  36.5 1.3 %collective-permute-start.4 = (f32[8,16,128]{2,1,0:T(8,128)S(1)}, f32[8,16,128]{2,1,0:T(8,128)S(1)}, u32[]{:S(2)}, u32[]{:S(2)}) collective-permute-start(f32[8,16,128]{2,1,0:T(8,128)S(1)} %get-tuple-element.64.refs_0_), channel_id=1, source_target_pairs={{1,0},{0,1},{3,2},{2,3},{5,4},{4,5},{7,6},{6,7},{9,8},{8,9},{11,10... | collective-permute-start | bytes 196616 | tf_op jit(solution)/shard_map/ppermute | solution.py:534

commit v3 on v2

--- a/solution.py
+++ b/solution.py
@@ -17,7 +17,7 @@
 
 BRICK = 8
 TILE = 8
-VMEM_BYTES = 48 * 1024 * 1024
+VMEM_BYTES = 24 * 1024 * 1024
 
 
 def chebyshev_constants(degree, lowest, highest):
@@ -49,7 +49,7 @@
     return jnp.where(value > 0.0, 1.0, 0.0)
 
 
-def rows_loop(start, stop, body, block=14):
+def rows_loop(start, stop, body, block=50):
     count = stop - start
     if count <= 0:
         return
@@ -97,7 +97,7 @@
         d_ref[i] = diagonal
         inv_ref[i] = jnp.where(inside, 1.0 / diagonal, 0.0)
 
-    rows_loop(lo, hi, row)
+    rows_loop(lo, hi, row, block=15)
 
 
 def level_start(lo, hi, lowest, b_ref, inv_ref, e_ref, u_ref):
@@ -176,34 +176,10 @@
     return started
 
 
-def edge_kernel(src_hbm, kap_hbm, ab_hbm, brick_hbm, a_out, b_out, bricks, sems):
+def block_kernel(slots, src_hbm, kap_hbm, ab_hbm, brick_hbm, b_ref, a_ref, g_ref, to_even, to_odd, q_ref, *rest):
+    y_outs, (bricks, pair_ref, sems) = rest[:slots], rest[slots:]
     nx, ny, nz = src_hbm.shape
     lower, upper = DEGREE, DEGREE + 1
-    even = lax.axis_index("dom") % 2 == 0
-    copies = [(brick_hbm, bricks)]
-    ups = (even, jnp.logical_not(even))
-    for out, up in zip((a_out, b_out), ups):
-        four = pl.ds(jnp.where(up, nx - lower, 0), lower)
-        five = pl.ds(jnp.where(up, nx - upper, 0), upper)
-        copies += [
-            (kap_hbm.at[five], out.at[pl.ds(2 * lower, upper)]),
-            (src_hbm.at[four], out.at[pl.ds(0, lower)]),
-            (ab_hbm.at[four], out.at[pl.ds(lower, lower)]),
-        ]
-    started = start_all(copies, sems)
-    for copy in started:
-        copy.wait()
-    nbx, _, nbz = bricks.shape
-    spread = spread_matrix(nbz, nz)
-    for out, up in zip((a_out, b_out), ups):
-        mask = spread_mask(bricks[jnp.where(up, nbx - 1, 0)], spread, ny)
-        for j in range(upper):
-            out[2 * lower + j] = out[2 * lower + j] * mask
-
-
-def block_kernel(slots, src_hbm, kap_hbm, ab_hbm, brick_hbm, _, b_ref, a_ref, g_ref, q_ref, *rest):
-    y_outs, (bricks, pair_ref, sems) = rest[:slots], rest[slots:]
-    nx, ny, nz = src_hbm.shape
     started = start_all([(brick_hbm, bricks), (kap_hbm, g_ref), (ab_hbm, a_ref), (src_hbm, b_ref)], sems)
     spread = spread_matrix(bricks.shape[2], nz)
     started[0].wait()
@@ -220,12 +196,22 @@
                 x = 4 * j + 2 * t
                 scratch = pair_ref.at[(field * (nx // 4) + j) * 2 + t]
                 cells.append(coarsen_rows(ref[x], ref[x + 1], scratch, 1))
-            q_ref[field, j] = pack_two(*cells)
+            q_ref[field * (nx // 4) + j] = pack_two(*cells)
 
     packed_rows(0, g_ref)
     started[2].wait()
     packed_rows(1, a_ref)
     started[3].wait()
+
+    even = lax.axis_index("dom") % 2 == 0
+    for out, up in ((to_even, even), (to_odd, jnp.logical_not(even))):
+        four = jnp.where(up, nx - lower, 0)
+        five = jnp.where(up, nx - upper, 0)
+        for j in range(lower):
+            out[j] = b_ref[four + j]
+            out[lower + j] = a_ref[four + j]
+        for j in range(upper):
+            out[2 * lower + j] = g_ref[five + j]
 
     for slot, out in enumerate(y_outs):
         at = pl.multiple_of(jnp.where(sends_up(slots, slot), ny - TILE, 0), TILE)
@@ -324,11 +310,18 @@
             out[1, j] = rb_ref[j, pl.ds(at, TILE), :]
 
 
-def gather_kernel(a_ref, b_ref, *refs):
+def stack_kernel(count, *refs):
     out = refs[-1]
-    for j in range(a_ref.shape[0]):
-        out[0, j] = a_ref[j]
-        out[1, j] = b_ref[j]
+    for part in range(count):
+        for j in range(out.shape[1]):
+            out[part, j] = refs[part][j]
+
+
+def stack(arrays, *earlier):
+    (out,) = call(
+        functools.partial(stack_kernel, len(arrays)), (*arrays, *earlier), [(len(arrays), *arrays[0].shape)]
+    )
+    return out
 
 
 def rim_kernel(slots, *refs):
@@ -416,30 +409,38 @@
     return jnp.dot(value, pick, preferred_element_type=jnp.float32, precision=lax.Precision.HIGHEST)
 
 
-def part_starts(nx):
-    even = lax.axis_index("dom") % 2 == 0
-    return [nx, jnp.where(even, 2 * nx, 0), jnp.where(even, 0, 2 * nx)]
+def placed_parts(slots, nx, own_refs, around_refs):
+    parts = [(nx, slot, ref) for slot, ref in enumerate(own_refs)]
+    if slots == 1:
+        core = lax.axis_index("grp")
+        for which, (ref, above) in enumerate(zip(around_refs, (core == 0, core == 1))):
+            start = jnp.where(above, 2 * nx, 0)
+            parts += [(start, 0, ref.at[1 - which]), (start, 1, ref.at[which])]
+    else:
+        even = lax.axis_index("dom") % 2 == 0
+        for which, above in enumerate((even, jnp.logical_not(even))):
+            start = jnp.where(above, 2 * nx, 0)
+            parts += [(start, slot, ref.at[which]) for slot, ref in enumerate(around_refs)]
+    return parts
 
 
 def coefficient_kernel(slots, *refs):
     own_refs, around_refs, refs = refs[: 1 + slots], refs[1 + slots : 2 + 2 * slots], refs[2 + 2 * slots :]
     wx, wy, wz, inv, d_ref, cwx, cwy, cwz, cinv, a_ref, g_ref, ca, cg, cd, pair_ref = refs
-    _, packed, ny, _ = own_refs[0].shape
+    packed, ny = own_refs[0].shape[0] // 2, own_refs[0].shape[1]
     nx = 2 * packed
     base = nx
 
-    for part, start in enumerate(part_starts(nx)):
-        for slot in range(1 + slots):
-            q_ref = around_refs[slot].at[part - 1] if part else own_refs[slot]
-            at = slice(slot * ny, (slot + 1) * ny)
-            for j in range(packed):
-                g_rows, a_rows = unpack_two(q_ref[0, j]), unpack_two(q_ref[1, j])
-                for t in range(2):
-                    g_row = g_rows[t]
-                    if slot:
-                        g_row = keep_near(g_row, slot_is_upper(slots, slot - 1), ny - 1)
-                    g_ref[start + 2 * j + t, at] = g_row
-                    a_ref[start + 2 * j + t, at] = a_rows[t]
+    for start, slot, q_ref in placed_parts(slots, nx, own_refs, around_refs):
+        at = slice(slot * ny, (slot + 1) * ny)
+        for j in range(packed):
+            g_rows, a_rows = unpack_two(q_ref[j]), unpack_two(q_ref[packed + j])
+            for t in range(2):
+                g_row = g_rows[t]
+                if slot:
+                    g_row = keep_near(g_row, slot_is_upper(slots, slot - 1), ny - 1)
+                g_ref[start + 2 * j + t, at] = g_row
+                a_ref[start + 2 * j + t, at] = a_rows[t]
 
     width = 2 * (COARSE_DEGREE - 1) + DEGREE
     level_setup(base - width, base + nx + width, 2, STEP_SCALE / 4.0, g_ref, a_ref, wx, wy, wz, inv, d_ref)
@@ -464,13 +465,11 @@
     nx = 2 * packed
     base = nx
 
-    for part, start in enumerate(part_starts(nx)):
-        for slot in range(1 + slots):
-            s_ref = around_refs[slot].at[part - 1] if part else own_refs[slot]
-            at = slice(slot * ny, (slot + 1) * ny)
-            for j in range(packed):
-                for t, b_row in enumerate(unpack_two(s_ref[j])):
-                    b_ref[start + 2 * j + t, at] = b_row
+    for start, slot, s_ref in placed_parts(slots, nx, own_refs, around_refs):
+        at = slice(slot * ny, (slot + 1) * ny)
+        for j in range(packed):
+            for t, b_row in enumerate(unpack_two(s_ref[j])):
+                b_ref[start + 2 * j + t, at] = b_row
 
     reach = 2 * (COARSE_DEGREE - 1)
     u_refs = (u0, u1, u2, u3)
@@ -534,26 +533,38 @@
             return [lax.ppermute(arrays[0], "grp", downward + upward)]
         return [lax.ppermute(arrays[0], "grp", downward), lax.ppermute(arrays[-1], "grp", upward)]
 
+    crossing = []
+    for i in range(doms - 1):
+        crossing += [(i * grps, (i + 1) * grps + 1), ((i + 1) * grps + 1, i * grps)]
+
+    def send_around(own, beside):
+        if slots == 1:
+            core = lax.axis_index("grp")
+            both = stack([own, beside[0]])
+            return [lax.ppermute(both, ("dom", "grp"), crossing)]
+        return [swap_even(own), swap_odd(own)]
+
+    def share_around(arrays, *earlier):
+        both = stack(arrays, *earlier)
+        both = both.reshape(2, *both.shape[-3:])
+        return [both, *along_grp([both])]
+
     fields = [pltpu.with_memory_space_constraint(x, pltpu.HBM) for x in (source, conductivity, absorption, brick_mask)]
     bricks = pltpu.VMEM(brick_mask.shape, brick_mask.dtype)
     payload = (2 * lower + upper, ny, nz)
-    to_even, to_odd = call(
-        edge_kernel, fields, [payload, payload], [bricks, pltpu.SemaphoreType.DMA((7,))], in_hbm=4
-    )
-    from_even, from_odd = swap_even(to_even), swap_odd(to_odd)
-
     packed = nx // 4
     small = (packed, ny // 2, nz)
-    b_own, a_own, g_own, coeffs, *edges = call(
+    b_own, a_own, g_own, to_even, to_odd, coeffs, *edges = call(
         functools.partial(block_kernel, slots),
-        (*fields, to_even),
-        [source.shape] * 3 + [(2, *small)] + [(3, nx, TILE, nz)] * slots,
+        fields,
+        [source.shape] * 3 + [payload] * 2 + [(2 * packed, ny // 2, nz)] + [(3, nx, TILE, nz)] * slots,
         [bricks, (4 * packed, ny, nz), pltpu.SemaphoreType.DMA((4,))],
         in_hbm=4,
     )
+    from_even, from_odd = swap_even(to_even), swap_odd(to_odd)
     own = (b_own, a_own, g_own, *along_grp(edges))
     coeffs_beside = along_grp([coeffs])
-    coeffs_even, coeffs_odd = swap_even(coeffs), swap_odd(coeffs)
+    coeffs_sent = send_around(coeffs, coeffs_beside)
 
     wide = (nx, ny + slots * TILE, nz)
     pairs = (nx // 2, ny, nz)
@@ -569,8 +580,6 @@
         [(2, payload[0], TILE, nz)] * slots,
     )
     corners_beside = along_grp(corners)
-    (coeffs_around,) = call(gather_kernel, (coeffs_even, coeffs_odd, *corners_beside), [(2, 2, *small)])
-    q_ins = [coeffs, *coeffs_beside, coeffs_around, *along_grp([coeffs_around])]
     rim = (2 * upper, ny, nz)
     near = (4 * upper + 2, ny + slots * TILE, nz)
     it_rim, res_rim, mid_source = call(
@@ -587,7 +596,9 @@
         out_hbm=2,
     )
 
-    source_even, source_odd = swap_even(mid_source), swap_odd(mid_source)
+    source_beside = along_grp([mid_source])
+    source_sent = send_around(mid_source, source_beside)
+    q_ins = [coeffs, *coeffs_beside, *share_around(coeffs_sent, mid_source)]
     mid_y = (1 + slots) * ny // 2
     mid_wide = (3 * nx // 2, mid_y, nz)
     coarse_rows = nx // 4 + 2 * COARSE_DEGREE
@@ -598,8 +609,7 @@
         [mid_wide] * 5 + [coarse_wide] * 4,
         [mid_wide] * 2 + [coarse_wide] * 3 + [(3 * coarse_rows, mid_y, nz)],
     )
-    (around,) = call(gather_kernel, (source_even, source_odd, weights[-1], written), [(2, *small)])
-    s_ins = [mid_source, *along_grp([mid_source]), around, *along_grp([around])]
+    s_ins = [mid_source, *source_beside, *share_around(source_sent, weights[-1], written)]
     mid_iterate, coarse_iterate = call(
         functools.partial(coarse_kernel, slots),
         (*s_ins, *weights),

time: 42.5 us -> 36.2 us (0.85)
  the two profiles are of different devices: /device:TPU:9 before, /device:TPU:19 now
where the time goes in v3:
time: 36.2 us; the launch traced here: 35.9 us
  starting transfers between devices  14.8 us (41%)
  Pallas kernels  12.2 us (34%)
  waiting for transfers between devices  8.16 us (23%)
  between operations  0.75 us (2%)
    pallas_call x11, Pallas kernels, call(): pl.pallas_call(kernel, out_shape=[jax.ShapeDtypeStruct(shape, jnp.float32...  12.2 us
    ppermute x6, starting transfers between devices, along_grp(): return [lax.ppermute(arrays[0], 'grp', downward + upward)]  5.66 us
    ppermute x2, starting transfers between devices, send_around(): return [lax.ppermute(both, ('dom', 'grp'), crossing)]  4.85 us
    ppermute x1, starting transfers between devices, swap_odd(): return lax.ppermute(array, 'dom', pairing(1))  4.06 us
    ppermute x2, waiting for transfers between devices, send_around(): return [lax.ppermute(both, ('dom', 'grp'), crossing)]  3.3 us
    ppermute x6, waiting for transfers between devices, along_grp(): return [lax.ppermute(arrays[0], 'grp', downward + upward)]  3.13 us
    ppermute x1, waiting for transfers between devices, swap_odd(): return lax.ppermute(array, 'dom', pairing(1))  1.74 us
  transfers between devices with their start and end apart: 10, of which 6 were waited for; matrix products, arithmetic and copies ran while one was open for 0% of the time, Pallas kernels for 19%

profile of v3, /device:TPU:19, one launch (start us, length us, event | category | flops | bytes accessed | tf_op | source)
XLA Modules:
  0.0 35.9 jit_solution(3531721829112805765)
XLA Ops:
  0.6 1.7 %shard_map.75 = (f32[32,32,128]{2,1,0:T(8,128)S(1)}, f32[32,32,128]{2,1,0:T(8,128)S(1)}, f32[32,32,128]{2,1,0:T(8,128)S(1)}, f32[13,32,128]{2,1,0:T(8,128)S(1)},...) custom-call(f32[32,32,128]{2,1,0:T(8,128)} %src_hbm.1, ...), custom_call_target="tpu_custom_call" | custom-call | tf_op jit(solution)/shard_map/pallas_call | solution.py:500
  2.3 0.7 %collective-permute-start = (f32[3,32,8,128]{3,2,1,0:T(8,128)S(1)}, f32[3,32,8,128]{3,2,1,0:T(8,128)S(1)}, u32[]{:S(2)}, u32[]{:S(2)}) collective-permute-start(f32[3,32,8,128]{3,2,1,0:T(8,128)S(1)} %get-tuple-element.44), channel_id=1, source_target_pairs={{1,0},{0,1},{3,2},{2,3},{5,4},{4,5},{7,6},{6,7},{9,8},{8,9},{11,10... | collective-permute-start | bytes 1179656 | tf_op jit(solution)/shard_map/ppermute | solution.py:533
  3.1 0.1 collective-permute-start.6
  3.1 0.3 collective-permute-start.1
  3.4 4.1 %collective-permute-start.2 = (f32[13,32,128]{2,1,0:T(8,128)S(1)}, f32[13,32,128]{2,1,0:T(8,128)S(1)}, u32[]{:S(2)}, u32[]{:S(2)}) collective-permute-start(f32[13,32,128]{2,1,0:T(8,128)S(1)} %get-tuple-element.59), channel_id=1, source_target_pairs={{2,4},{6,8},{10,12},{14,16},{18,20},{22,24},{26,28},{4,2},{8,6},{1... | collective-permute-start | bytes 638984 | tf_op jit(solution)/shard_map/ppermute | solution.py:524
  7.5 0.0 collective-permute-done.6.refs_1_
  7.5 2.9 %collective-permute-start.7 = (f32[2,16,16,128]{3,2,1,0:T(8,128)S(1)}, f32[2,16,16,128]{3,2,1,0:T(8,128)S(1)}, u32[]{:S(2)}, u32[]{:S(2)}) collective-permute-start(f32[2,16,16,128]{3,2,1,0:T(8,128)S(1)} %shard_map.81), channel_id=1, source_target_pairs={{0,3},{3,0},{2,5},{5,2},{4,7},{7,4},{6,9},{9,6},{8,11},{11,8},{10,... | collective-permute-start | bytes 786440 | tf_op jit(solution)/shard_map/ppermute | solution.py:544
  10.4 0.0 collective-permute-done.refs_3_
  10.4 2.9 %shard_map.76 = (f32[32,40,128]{2,1,0:T(8,128)S(1)}, f32[32,40,128]{2,1,0:T(8,128)S(1)}, f32[32,40,128]{2,1,0:T(8,128)S(1)}, f32[32,40,128]{2,1,0:T(8,128)S(1)},...) custom-call(f32[32,32,128]{2,1,0:T(8,128)S(1)} %get-tuple-element.41, ...), custom_call_target="tpu_custom_call" | custom-call | tf_op jit(solution)/shard_map/pallas_call | solution.py:500
  13.3 0.0 collective-permute-done.1.ra_ref.refs_16_
  13.3 1.7 %collective-permute-done.2.rb_ref.refs_17_ = f32[13,32,128]{2,1,0:T(8,128)S(1)} collective-permute-done((f32[13,32,128]{2,1,0:T(8,128)S(1)}, f32[13,32,128]{2,1,0:T(8,128)S(1)}, u32[]{:S(2)}, u32[]{:S(2)}) %collective-permute-start.2) | collective-permute-done | bytes 213024 | tf_op jit(solution)/shard_map/ppermute | solution.py:524
  15.1 3.2 %collective-permute-start.3 = (f32[2,13,8,128]{3,2,1,0:T(8,128)S(1)}, f32[2,13,8,128]{3,2,1,0:T(8,128)S(1)}, u32[]{:S(2)}, u32[]{:S(2)}) collective-permute-start(f32[2,13,8,128]{3,2,1,0:T(8,128)S(1)} %shard_map.77), channel_id=1, source_target_pairs={{1,0},{0,1},{3,2},{2,3},{5,4},{4,5},{7,6},{6,7},{9,8},{8,9},{11,10... | collective-permute-start | bytes 319496 | tf_op jit(solution)/shard_map/ppermute | solution.py:533
  18.3 1.0 %collective-permute-done.3.refs_18_ = f32[2,13,8,128]{3,2,1,0:T(8,128)S(1)} collective-permute-done((f32[2,13,8,128]{3,2,1,0:T(8,128)S(1)}, f32[2,13,8,128]{3,2,1,0:T(8,128)S(1)}, u32[]{:S(2)}, u32[]{:S(2)}) %collective-permute-start.3) | collective-permute-done | bytes 106528 | tf_op jit(solution)/shard_map/ppermute | solution.py:533
  19.2 1.2 %shard_map.78 = (f32[10,32,128]{2,1,0:T(8,128)S(1)}, f32[10,32,128]{2,1,0:T(8,128)S(1)}, f32[8,16,128]{2,1,0:T(8,128)S(1)}) custom-call(f32[32,32,128]{2,1,0:T(8,128)S(1)} %get-tuple-element.41.refs_0_, f32[32,32,128]{2,1,0:T(8,128)S(1)} %get-tuple-element.42.refs_1_, f32[32,32,128]{2,1,0:T(8,128)S(1)} %get-tuple-element.43.refs_2_, ...), custom_call_target="tpu_custom_call" | custom-call | tf_op jit(solution)/shard_map/pallas_call | solution.py:500
  20.4 0.2 collective-permute-done.7.refs_0_
  20.6 0.5 %collective-permute-start.8 = (f32[2,16,16,128]{3,2,1,0:T(8,128)S(1)}, f32[2,16,16,128]{3,2,1,0:T(8,128)S(1)}, u32[]{:S(2)}, u32[]{:S(2)}) collective-permute-start(f32[2,16,16,128]{3,2,1,0:T(8,128)S(1)} %bitcast.2), channel_id=1, source_target_pairs={{1,0},{0,1},{3,2},{2,3},{5,4},{4,5},{7,6},{6,7},{9,8},{8,9},{11,10... | collective-permute-start | bytes 786440 | tf_op jit(solution)/shard_map/ppermute | solution.py:533
  21.2 0.1 collective-permute-start.4
  21.2 1.2 %collective-permute-done.4.refs_1_ = f32[8,16,128]{2,1,0:T(8,128)S(1)} collective-permute-done((f32[8,16,128]{2,1,0:T(8,128)S(1)}, f32[8,16,128]{2,1,0:T(8,128)S(1)}, u32[]{:S(2)}, u32[]{:S(2)}) %collective-permute-start.4) | collective-permute-done | bytes 65568 | tf_op jit(solution)/shard_map/ppermute | solution.py:533
  22.4 1.9 %collective-permute-start.5 = (f32[2,8,16,128]{3,2,1,0:T(8,128)S(1)}, f32[2,8,16,128]{3,2,1,0:T(8,128)S(1)}, u32[]{:S(2)}, u32[]{:S(2)}) collective-permute-start(f32[2,8,16,128]{3,2,1,0:T(8,128)S(1)} %shard_map.80), channel_id=1, source_target_pairs={{0,3},{3,0},{2,5},{5,2},{4,7},{7,4},{6,9},{9,6},{8,11},{11,8},{10,... | collective-permute-start | bytes 393224 | tf_op jit(solution)/shard_map/ppermute | solution.py:544
  24.3 1.0 %shard_map.79 = (f32[32,32,128]{2,1,0:T(8,128)}, f32[32,32,128]{2,1,0:T(8,128)}, f32[8,128]{1,0:T(8,128)S(1)}) custom-call(f32[32,32,128]{2,1,0:T(8,128)S(1)} %get-tuple-element.45.it_in, f32[32,32,128]{2,1,0:T(8,128)S(1)} %get-tuple-element.46.refs_14_.res_in, f32[10,32,128]{2,1,0:T(8,128)S(1)} %get-tuple-element.60.it_rim, ...), custom_call_target="tpu_custom_call" | custom-call | tf_op jit(solution)/shard_map/pallas_call | solution.py:500
  25.4 0.0 collective-permute-done.8.refs_3_
  25.4 1.9 %shard_map.83 = (f32[48,32,128]{2,1,0:T(8,128)S(1)}, f32[48,32,128]{2,1,0:T(8,128)S(1)}, f32[48,32,128]{2,1,0:T(8,128)S(1)}, f32[48,32,128]{2,1,0:T(8,128)S(1)},...) custom-call(f32[16,16,128]{2,1,0:T(8,128)S(1)} %get-tuple-element.65, ...), custom_call_target="tpu_custom_call" | custom-call | tf_op jit(solution)/shard_map/pallas_call | solution.py:500
  27.3 3.1 %collective-permute-done.5.refs_0_ = f32[2,8,16,128]{3,2,1,0:T(8,128)S(1)} collective-permute-done((f32[2,8,16,128]{3,2,1,0:T(8,128)S(1)}, f32[2,8,16,128]{3,2,1,0:T(8,128)S(1)}, u32[]{:S(2)}, u32[]{:S(2)}) %collective-permute-start.5) | collective-permute-done | bytes 131104 | tf_op jit(solution)/shard_map/ppermute | solution.py:544
  30.4 1.0 %collective-permute-start.9 = (f32[2,8,16,128]{3,2,1,0:T(8,128)S(1)}, f32[2,8,16,128]{3,2,1,0:T(8,128)S(1)}, u32[]{:S(2)}, u32[]{:S(2)}) collective-permute-start(f32[2,8,16,128]{3,2,1,0:T(8,128)S(1)} %bitcast.4), channel_id=1, source_target_pairs={{1,0},{0,1},{3,2},{2,3},{5,4},{4,5},{7,6},{6,7},{9,8},{8,9},{11,10... | collective-permute-start | bytes 393224 | tf_op jit(solution)/shard_map/ppermute | solution.py:533
  31.4 1.0 %collective-permute-done.9.refs_3_ = f32[2,8,16,128]{3,2,1,0:T(8,128)S(1)} collective-permute-done((f32[2,8,16,128]{3,2,1,0:T(8,128)S(1)}, f32[2,8,16,128]{3,2,1,0:T(8,128)S(1)}, u32[]{:S(2)}, u32[]{:S(2)}) %collective-permute-start.9) | collective-permute-done | bytes 131104 | tf_op jit(solution)/shard_map/ppermute | solution.py:533
  32.4 3.5 %shard_map.85 = (f32[16,16,64]{2,1,0:T(8,128)}, f32[8,8,32]{2,1,0:T(8,128)}) custom-call(f32[8,16,128]{2,1,0:T(8,128)S(1)} %get-tuple-element.64.refs_0_.refs_1_, f32[8,16,128]{2,1,0:T(8,128)S(1)} %collective-permute-done.4.refs_1_, f32[2,8,16,128]{3,2,1,0:T(8,128)S(1)} %bitcast.5, f32[2,8,16,128]{3,2,1,0:T(8,128)S(1)} %collective-permute-done.9.refs_3_, ...), custom_call_target="tpu_custom_call" | custom-call | tf_op jit(solution)/shard_map/pallas_call | solution.py:500
  (5 shorter events, 0.1 us)
Async XLA Ops:
  2.3 8.1 %collective-permute-start = (f32[3,32,8,128]{3,2,1,0:T(8,128)S(1)}, f32[3,32,8,128]{3,2,1,0:T(8,128)S(1)}, u32[]{:S(2)}, u32[]{:S(2)}) collective-permute-start(f32[3,32,8,128]{3,2,1,0:T(8,128)S(1)} %get-tuple-element.44), channel_id=1, source_target_pairs={{1,0},{0,1},{3,2},{2,3},{5,4},{4,5},{7,6},{6,7},{9,8},{8,9},{11,10... | collective-permute-start | bytes 1179656 | tf_op jit(solution)/shard_map/ppermute | solution.py:533
  3.1 4.4 %collective-permute-start.6 = (f32[16,16,128]{2,1,0:T(8,128)S(1)}, f32[16,16,128]{2,1,0:T(8,128)S(1)}, u32[]{:S(2)}, u32[]{:S(2)}) collective-permute-start(f32[16,16,128]{2,1,0:T(8,128)S(1)} %get-tuple-element.65.refs_0_), channel_id=1, source_target_pairs={{1,0},{0,1},{3,2},{2,3},{5,4},{4,5},{7,6},{6,7},{9,8},{8,9},{11,10... | collective-permute-start | bytes 393224 | tf_op jit(solution)/shard_map/ppermute | solution.py:533
  3.1 10.2 %collective-permute-start.1 = (f32[13,32,128]{2,1,0:T(8,128)S(1)}, f32[13,32,128]{2,1,0:T(8,128)S(1)}, u32[]{:S(2)}, u32[]{:S(2)}) collective-permute-start(f32[13,32,128]{2,1,0:T(8,128)S(1)} %get-tuple-element.58), channel_id=1, source_target_pairs={{0,2},{4,6},{8,10},{12,14},{16,18},{20,22},{24,26},{28,30},{2,0},{... | collective-permute-start | bytes 638984 | tf_op jit(solution)/shard_map/ppermute | solution.py:521
  3.4 11.7 %collective-permute-start.2 = (f32[13,32,128]{2,1,0:T(8,128)S(1)}, f32[13,32,128]{2,1,0:T(8,128)S(1)}, u32[]{:S(2)}, u32[]{:S(2)}) collective-permute-start(f32[13,32,128]{2,1,0:T(8,128)S(1)} %get-tuple-element.59), channel_id=1, source_target_pairs={{2,4},{6,8},{10,12},{14,16},{18,20},{22,24},{26,28},{4,2},{8,6},{1... | collective-permute-start | bytes 638984 | tf_op jit(solution)/shard_map/ppermute | solution.py:524
  7.5 13.1 %collective-permute-start.7 = (f32[2,16,16,128]{3,2,1,0:T(8,128)S(1)}, f32[2,16,16,128]{3,2,1,0:T(8,128)S(1)}, u32[]{:S(2)}, u32[]{:S(2)}) collective-permute-start(f32[2,16,16,128]{3,2,1,0:T(8,128)S(1)} %shard_map.81), channel_id=1, source_target_pairs={{0,3},{3,0},{2,5},{5,2},{4,7},{7,4},{6,9},{9,6},{8,11},{11,8},{10,... | collective-permute-start | bytes 786440 | tf_op jit(solution)/shard_map/ppermute | solution.py:544
  15.1 4.2 %collective-permute-start.3 = (f32[2,13,8,128]{3,2,1,0:T(8,128)S(1)}, f32[2,13,8,128]{3,2,1,0:T(8,128)S(1)}, u32[]{:S(2)}, u32[]{:S(2)}) collective-permute-start(f32[2,13,8,128]{3,2,1,0:T(8,128)S(1)} %shard_map.77), channel_id=1, source_target_pairs={{1,0},{0,1},{3,2},{2,3},{5,4},{4,5},{7,6},{6,7},{9,8},{8,9},{11,10... | collective-permute-start | bytes 319496 | tf_op jit(solution)/shard_map/ppermute | solution.py:533
  20.6 4.8 %collective-permute-start.8 = (f32[2,16,16,128]{3,2,1,0:T(8,128)S(1)}, f32[2,16,16,128]{3,2,1,0:T(8,128)S(1)}, u32[]{:S(2)}, u32[]{:S(2)}) collective-permute-start(f32[2,16,16,128]{3,2,1,0:T(8,128)S(1)} %bitcast.2), channel_id=1, source_target_pairs={{1,0},{0,1},{3,2},{2,3},{5,4},{4,5},{7,6},{6,7},{9,8},{8,9},{11,10... | collective-permute-start | bytes 786440 | tf_op jit(solution)/shard_map/ppermute | solution.py:533
  21.2 1.3 %collective-permute-start.4 = (f32[8,16,128]{2,1,0:T(8,128)S(1)}, f32[8,16,128]{2,1,0:T(8,128)S(1)}, u32[]{:S(2)}, u32[]{:S(2)}) collective-permute-start(f32[8,16,128]{2,1,0:T(8,128)S(1)} %get-tuple-element.64.refs_0_.refs_1_), channel_id=1, source_target_pairs={{1,0},{0,1},{3,2},{2,3},{5,4},{4,5},{7,6},{6,7},{9,8},{8,9},{11,10... | collective-permute-start | bytes 196616 | tf_op jit(solution)/shard_map/ppermute | solution.py:533
  22.4 8.0 %collective-permute-start.5 = (f32[2,8,16,128]{3,2,1,0:T(8,128)S(1)}, f32[2,8,16,128]{3,2,1,0:T(8,128)S(1)}, u32[]{:S(2)}, u32[]{:S(2)}) collective-permute-start(f32[2,8,16,128]{3,2,1,0:T(8,128)S(1)} %shard_map.80), channel_id=1, source_target_pairs={{0,3},{3,0},{2,5},{5,2},{4,7},{7,4},{6,9},{9,6},{8,11},{11,8},{10,... | collective-permute-start | bytes 393224 | tf_op jit(solution)/shard_map/ppermute | solution.py:544
  30.4 2.0 %collective-permute-start.9 = (f32[2,8,16,128]{3,2,1,0:T(8,128)S(1)}, f32[2,8,16,128]{3,2,1,0:T(8,128)S(1)}, u32[]{:S(2)}, u32[]{:S(2)}) collective-permute-start(f32[2,8,16,128]{3,2,1,0:T(8,128)S(1)} %bitcast.4), channel_id=1, source_target_pairs={{1,0},{0,1},{3,2},{2,3},{5,4},{4,5},{7,6},{6,7},{9,8},{8,9},{11,10... | collective-permute-start | bytes 393224 | tf_op jit(solution)/shard_map/ppermute | solution.py:533

commit v4 on v3

--- a/solution.py
+++ b/solution.py
@@ -69,11 +69,24 @@
         body(i)
 
 
-def level_setup(lo, hi, zstep, factor, g_ref, a_ref, wx_ref, wy_ref, wz_ref, inv_ref, d_ref):
+def next_row(value, following, packed):
+    if not packed:
+        return following
+    return jnp.where((lane_index(value.shape) & 1) == 0, ahead(value, 1), behind(following, 1))
+
+
+def previous_row(before, value, packed):
+    if not packed:
+        return before
+    return jnp.where((lane_index(value.shape) & 1) == 0, ahead(before, 1), behind(value, 1))
+
+
+def level_setup(lo, hi, zstep, factor, g_ref, a_ref, wx_ref, wy_ref, wz_ref, inv_ref, d_ref, packed=False, wb_ref=None):
     half = 0.5 * factor
 
     def weight_x(i):
-        here, there = g_ref[i], g_ref[i + 1]
+        here = g_ref[i]
+        there = next_row(here, g_ref[i + 1], packed)
         wx_ref[i] = jnp.where((here > 0.0) & (there > 0.0), half * (here + there), 0.0)
 
     weight_x(lo - 1)
@@ -89,7 +102,11 @@
         wz = jnp.where(inside & (there_z > 0.0) & (lanes < here.shape[1] - zstep), half * (here + there_z), 0.0)
         wy_ref[i] = wy
         wz_ref[i] = wz
-        faces = [wx_ref[i], wx_ref[i - 1], wy, behind(wy, 0), wz, behind(wz, 1, zstep)]
+        wx = wx_ref[i]
+        wb = behind(wy, 0)
+        if wb_ref is not None:
+            wb_ref[i] = wb
+        faces = [wx, previous_row(wx_ref[i - 1], wx, packed), wy, wb, wz, behind(wz, 1, zstep)]
         wall = factor * a_ref[i]
         diagonal = 1.0 + jnp.where(faces[0] > 0.0, faces[0], wall)
         for face in faces[1:]:
@@ -100,6 +117,22 @@
     rows_loop(lo, hi, row, block=15)
 
 
+class Circular:
+    def __init__(self, ref):
+        self.ref, self.size = ref, ref.shape[1] - 2 * TILE
+
+    def __getitem__(self, i):
+        return self.ref[i, TILE : TILE + self.size]
+
+    def __setitem__(self, i, value):
+        self.ref[i, TILE : TILE + self.size] = value
+        self.ref[i, :TILE] = value[self.size - TILE :]
+        self.ref[i, TILE + self.size :] = value[:TILE]
+
+    def shifted(self, i, step):
+        return self.ref[i, TILE + step : TILE + step + self.size]
+
+
 def level_start(lo, hi, lowest, b_ref, inv_ref, e_ref, u_ref):
     first, _ = chebyshev_constants(1, lowest, SMOOTH_HIGH)
 
@@ -111,16 +144,21 @@
     rows_loop(lo, hi, row)
 
 
-def level_pass(lo, hi, k, degree, lowest, zstep, inv_ref, wx_ref, wy_ref, wz_ref, e_ref, u_refs):
+def level_pass(lo, hi, k, degree, lowest, zstep, inv_ref, wx_ref, wy_ref, wz_ref, e_ref, u_refs, packed=False, wb_ref=None):
     _, steps = chebyshev_constants(degree, lowest, SMOOTH_HIGH)
     old = u_refs[k]
 
     def row(i):
         u = old[i]
+        wx = wx_ref[i]
         wy = wy_ref[i]
         wz = wz_ref[i]
-        coupled = wx_ref[i] * old[i + 1] + wx_ref[i - 1] * old[i - 1]
-        coupled = coupled + (wy * ahead(u, 0) + behind(wy * u, 0))
+        coupled = wx * next_row(u, old[i + 1], packed)
+        coupled = coupled + previous_row(wx_ref[i - 1] * old[i - 1], wx * u if packed else None, packed)
+        if wb_ref is None:
+            coupled = coupled + (wy * ahead(u, 0) + behind(wy * u, 0))
+        else:
+            coupled = coupled + (wy * old.shifted(i, 1) + wb_ref[i] * old.shifted(i, -1))
         coupled = coupled + (wz * ahead(u, 1, zstep) + behind(wz * u, 1, zstep))
         e = e_ref[i] - u + inv_ref[i] * coupled
         e_ref[i] = e
@@ -130,15 +168,17 @@
     rows_loop(lo, hi, row)
 
 
-def level_sweeps(base, size, reach, degree, lowest, keep, zstep, b_ref, inv_ref, wx_ref, wy_ref, wz_ref, e_ref, u_refs):
+def level_sweeps(
+    base, size, reach, degree, lowest, keep, zstep, b_ref, inv_ref, wx_ref, wy_ref, wz_ref, e_ref, u_refs, packed=False, wb_ref=None
+):
     passes = degree if keep else degree - 1
-    width = reach + passes
+    per = 2 if packed else 1
+    width = -(-(reach + passes) // per)
     level_start(base - width, base + size + width, lowest, b_ref, inv_ref, e_ref, u_refs[0])
+    weights = (inv_ref, wx_ref, wy_ref, wz_ref)
     for k in range(passes):
-        width = reach + passes - 1 - k
-        level_pass(
-            base - width, base + size + width, k, degree, lowest, zstep, inv_ref, wx_ref, wy_ref, wz_ref, e_ref, u_refs
-        )
+        width = -(-(reach + passes - 1 - k) // per)
+        level_pass(base - width, base + size + width, k, degree, lowest, zstep, *weights, e_ref, u_refs, packed, wb_ref)
 
 
 def coarsen_rows(one, two, pair_ref, zstep):
@@ -149,12 +189,15 @@
 
 
 def pack_two(one, two):
-    return jnp.where(lane_index(one.shape) % 2 == 0, one, behind(two, 1))
-
-
-def unpack_two(packed):
-    even = lane_index(packed.shape) % 2 == 0
-    return jnp.where(even, packed, 0.0), jnp.where(even, ahead(packed, 1), 0.0)
+    return jnp.where((lane_index(one.shape) & 1) == 0, one, behind(two, 1))
+
+
+def coarsen_packed(value, pair_ref):
+    pair_ref[...] = value
+    half = pair_ref.shape[0] // 2
+    summed = pair_ref[pl.ds(0, half, 2), :] + pair_ref[pl.ds(1, half, 2), :]
+    summed = summed + ahead(summed, 1)
+    return (summed + ahead(summed, 1, 2)) * 0.125
 
 
 def spread_mask(lines, spread, ny):
@@ -400,93 +443,90 @@
         copy.wait()
 
 
-def compact(value, step):
+def compact(value, step, first=0):
     nz = value.shape[-1]
     shape = (nz, nz // step)
     pick = jnp.where(
-        lax.broadcasted_iota(jnp.int32, shape, 0) == step * lax.broadcasted_iota(jnp.int32, shape, 1), 1.0, 0.0
+        lax.broadcasted_iota(jnp.int32, shape, 0) == first + step * lax.broadcasted_iota(jnp.int32, shape, 1), 1.0, 0.0
     )
     return jnp.dot(value, pick, preferred_element_type=jnp.float32, precision=lax.Precision.HIGHEST)
 
 
-def placed_parts(slots, nx, own_refs, around_refs):
-    parts = [(nx, slot, ref) for slot, ref in enumerate(own_refs)]
+def placed_parts(slots, rows, own_refs, around_refs):
+    parts = [(rows, slot, ref) for slot, ref in enumerate(own_refs)]
     if slots == 1:
         core = lax.axis_index("grp")
         for which, (ref, above) in enumerate(zip(around_refs, (core == 0, core == 1))):
-            start = jnp.where(above, 2 * nx, 0)
+            start = jnp.where(above, 2 * rows, 0)
             parts += [(start, 0, ref.at[1 - which]), (start, 1, ref.at[which])]
     else:
         even = lax.axis_index("dom") % 2 == 0
         for which, above in enumerate((even, jnp.logical_not(even))):
-            start = jnp.where(above, 2 * nx, 0)
+            start = jnp.where(above, 2 * rows, 0)
             parts += [(start, slot, ref.at[which]) for slot, ref in enumerate(around_refs)]
     return parts
 
 
 def coefficient_kernel(slots, *refs):
     own_refs, around_refs, refs = refs[: 1 + slots], refs[1 + slots : 2 + 2 * slots], refs[2 + 2 * slots :]
-    wx, wy, wz, inv, d_ref, cwx, cwy, cwz, cinv, a_ref, g_ref, ca, cg, cd, pair_ref = refs
-    packed, ny = own_refs[0].shape[0] // 2, own_refs[0].shape[1]
-    nx = 2 * packed
-    base = nx
-
-    for start, slot, q_ref in placed_parts(slots, nx, own_refs, around_refs):
+    wx, wy, wz, wb, inv, d_ref, cwx, cwy, cwz, cinv, a_ref, g_ref, ca, cg, cd, pair_ref = refs
+    rows, ny = own_refs[0].shape[0] // 2, own_refs[0].shape[1]
+    for start, slot, q_ref in placed_parts(slots, rows, own_refs, around_refs):
         at = slice(slot * ny, (slot + 1) * ny)
-        for j in range(packed):
-            g_rows, a_rows = unpack_two(q_ref[j]), unpack_two(q_ref[packed + j])
-            for t in range(2):
-                g_row = g_rows[t]
-                if slot:
-                    g_row = keep_near(g_row, slot_is_upper(slots, slot - 1), ny - 1)
-                g_ref[start + 2 * j + t, at] = g_row
-                a_ref[start + 2 * j + t, at] = a_rows[t]
-
-    width = 2 * (COARSE_DEGREE - 1) + DEGREE
-    level_setup(base - width, base + nx + width, 2, STEP_SCALE / 4.0, g_ref, a_ref, wx, wy, wz, inv, d_ref)
-
-    rows = cg.shape[0]
-    offset = base - 2 * COARSE_DEGREE
-    for i in range(rows):
-        row = offset + 2 * i
-        g0, g1 = g_ref[row], g_ref[row + 1]
-        whole = coarsen_rows(positive(g0), positive(g1), pair_ref.at[3 * i], 2) > 0.75
-        first = lane_index(whole.shape) % 4 == 0
-        cg[i] = jnp.where(whole & first, coarsen_rows(g0, g1, pair_ref.at[3 * i + 1], 2), 0.0)
-        ca[i] = coarsen_rows(a_ref[row], a_ref[row + 1], pair_ref.at[3 * i + 2], 2)
-    level_setup(1, rows - 1, 4, STEP_SCALE / 16.0, cg, ca, cwx, cwy, cwz, cinv, cd)
+        for j in range(rows):
+            g_row = q_ref[j]
+            if slot:
+                g_row = keep_near(g_row, slot_is_upper(slots, slot - 1), ny - 1)
+            g_ref[start + j, at] = g_row
+            a_ref[start + j, at] = q_ref[rows + j]
+
+    width = -(-(2 * (COARSE_DEGREE - 1) + DEGREE) // 2)
+    level_setup(rows - width, 2 * rows + width, 2, STEP_SCALE / 4.0, g_ref, a_ref, wx, wy, wz, inv, d_ref, True, wb)
+
+    coarse_rows = cg.shape[0]
+    def coefficients(i):
+        row = rows - COARSE_DEGREE + i
+        g = g_ref[row]
+        whole = coarsen_packed(positive(g), pair_ref.at[3 * i]) > 0.75
+        first = (lane_index(whole.shape) & 3) == 0
+        cg[i] = jnp.where(whole & first, coarsen_packed(g, pair_ref.at[3 * i + 1]), 0.0)
+        ca[i] = coarsen_packed(a_ref[row], pair_ref.at[3 * i + 2])
+
+    rows_loop(0, coarse_rows, coefficients, block=10)
+    level_setup(1, coarse_rows - 1, 4, STEP_SCALE / 16.0, cg, ca, cwx, cwy, cwz, cinv, cd)
 
 
 def coarse_kernel(slots, *refs):
     own_refs, around_refs, refs = refs[: 1 + slots], refs[1 + slots : 2 + 2 * slots], refs[2 + 2 * slots :]
-    wx, wy, wz, inv, d_ref, cwx, cwy, cwz, cinv, mid_out, coarse_out = refs[:11]
-    b_ref, e_ref, u0, u1, u2, u3, cb, ce, v0, v1, v2, v3, v4, v5, pair_ref = refs[11:]
-    packed, ny, nz = own_refs[0].shape
-    nx = 2 * packed
-    base = nx
-
-    for start, slot, s_ref in placed_parts(slots, nx, own_refs, around_refs):
+    wx, wy, wz, wb, inv, d_ref, cwx, cwy, cwz, cinv, mid_out, coarse_out = refs[:12]
+    b_ref, e_ref, u0, u1, u2, u3, cb, ce, v0, v1, v2, v3, v4, v5, pair_ref = refs[12:]
+    rows, ny, nz = own_refs[0].shape
+    for start, slot, s_ref in placed_parts(slots, rows, own_refs, around_refs):
         at = slice(slot * ny, (slot + 1) * ny)
-        for j in range(packed):
-            for t, b_row in enumerate(unpack_two(s_ref[j])):
-                b_ref[start + 2 * j + t, at] = b_row
+        for j in range(rows):
+            b_ref[start + j, at] = s_ref[j]
 
     reach = 2 * (COARSE_DEGREE - 1)
     u_refs = (u0, u1, u2, u3)
-    level_sweeps(base, nx, reach, DEGREE, SMOOTH_LOW, True, 2, b_ref, inv, wx, wy, wz, e_ref, u_refs)
-
-    total = u0[base : base + nx, :ny]
+    updates = [Circular(u_ref) for u_ref in u_refs]
+    level_sweeps(rows, rows, reach, DEGREE, SMOOTH_LOW, True, 2, b_ref, inv, wx, wy, wz, e_ref, updates, True, wb)
+
+    total = u0[rows : 2 * rows, TILE : TILE + ny]
     for u_ref in u_refs[1:]:
-        total = total + u_ref[base : base + nx, :ny]
-    mid_out[...] = compact(total.reshape(nx * ny, nz), 2).reshape(nx, ny, nz // 2)
-
-    half, cny = nx // 2, ny // 2
+        total = total + u_ref[rows : 2 * rows, TILE : TILE + ny]
+    total = total.reshape(rows * ny, nz)
+    for t in range(2):
+        lines = compact(total, 2, t).reshape(rows, ny, nz // 2)
+        for j in range(rows):
+            mid_out[2 * j + t] = lines[j]
+
+    half, cny = rows, ny // 2
     cbase = COARSE_DEGREE
-    offset = base - 2 * cbase
-    for i in range(1, half + 2 * cbase - 1):
-        row = offset + 2 * i
-        cb[i] = coarsen_rows(d_ref[row] * e_ref[row], d_ref[row + 1] * e_ref[row + 1], pair_ref.at[i], 2)
-
+    def source(i):
+        row = rows - cbase + i
+        cb[i] = coarsen_packed(d_ref[row] * e_ref[row], pair_ref.at[i])
+
+    rows_loop(1, half + 2 * cbase - 1, source)
     v_refs = (v0, v1, v2, v3, v4, v5)
     level_sweeps(cbase, half, 0, COARSE_DEGREE, COARSE_LOW, False, 4, cb, cinv, cwx, cwy, cwz, ce, v_refs)
     total = v0[cbase : cbase + half, :cny]
@@ -539,10 +579,9 @@
 
     def send_around(own, beside):
         if slots == 1:
-            core = lax.axis_index("grp")
             both = stack([own, beside[0]])
-            return [lax.ppermute(both, ("dom", "grp"), crossing)]
-        return [swap_even(own), swap_odd(own)]
+            return [lax.ppermute(both, ("dom", "grp"), crossing)], both
+        return [swap_even(own), swap_odd(own)], own
 
     def share_around(arrays, *earlier):
         both = stack(arrays, *earlier)
@@ -564,7 +603,7 @@
     from_even, from_odd = swap_even(to_even), swap_odd(to_odd)
     own = (b_own, a_own, g_own, *along_grp(edges))
     coeffs_beside = along_grp([coeffs])
-    coeffs_sent = send_around(coeffs, coeffs_beside)
+    coeffs_sent, _ = send_around(coeffs, coeffs_beside)
 
     wide = (nx, ny + slots * TILE, nz)
     pairs = (nx // 2, ny, nz)
@@ -597,16 +636,16 @@
     )
 
     source_beside = along_grp([mid_source])
-    source_sent = send_around(mid_source, source_beside)
-    q_ins = [coeffs, *coeffs_beside, *share_around(coeffs_sent, mid_source)]
+    source_sent, sending = send_around(mid_source, source_beside)
+    q_ins = [coeffs, *coeffs_beside, *share_around(coeffs_sent, sending)]
     mid_y = (1 + slots) * ny // 2
-    mid_wide = (3 * nx // 2, mid_y, nz)
+    mid_wide = (3 * packed, mid_y, nz)
     coarse_rows = nx // 4 + 2 * COARSE_DEGREE
     coarse_wide = (coarse_rows, mid_y // 2, nz)
     weights = call(
         functools.partial(coefficient_kernel, slots),
         q_ins,
-        [mid_wide] * 5 + [coarse_wide] * 4,
+        [mid_wide] * 6 + [coarse_wide] * 4,
         [mid_wide] * 2 + [coarse_wide] * 3 + [(3 * coarse_rows, mid_y, nz)],
     )
     s_ins = [mid_source, *source_beside, *share_around(source_sent, weights[-1], written)]
@@ -614,7 +653,7 @@
         functools.partial(coarse_kernel, slots),
         (*s_ins, *weights),
         [(nx // 2, ny // 2, nz // 2), (nx // 4, ny // 4, nz // 4)],
-        [mid_wide] * 6 + [coarse_wide] * 8 + [(coarse_rows, mid_y, nz)],
+        [mid_wide] * 2 + [(3 * packed, mid_y + 2 * TILE, nz)] * 4 + [coarse_wide] * 8 + [(coarse_rows, mid_y, nz)],
     )
     return (fine_iterate, fine_residual, mid_iterate, coarse_iterate)
 

time: 36.2 us -> 35.4 us (0.978)
  waiting for transfers between devices: 8.16 us -> 7.13 us
  Pallas kernels: 12.2 us -> 12.6 us
    ppermute x2, waiting for transfers between devices: 3.3 us -> 2.54 us  [send_around(): return ([lax.ppermute(both, ('dom', 'grp'), crossing)], both)]
    pallas_call x11, Pallas kernels: 12.2 us -> 12.6 us  [call(): pl.pallas_call(kernel, out_shape=[jax.ShapeDtypeStruct(shape, jnp.float32...]
  transfers between devices with their start and end apart: 10 -> 10, of which waited for: 6 -> 5; matrix products, arithmetic and copies ran while one was open for 0% -> 0% of each run, Pallas kernels for 19% -> 21%
where the time goes in v4:
time: 35.4 us; the launch traced here: 35.1 us
  starting transfers between devices  14.6 us (41%)
  Pallas kernels  12.6 us (36%)
  waiting for transfers between devices  7.13 us (20%)
  between operations  0.76 us (2%)
    pallas_call x11, Pallas kernels, call(): pl.pallas_call(kernel, out_shape=[jax.ShapeDtypeStruct(shape, jnp.float32...  12.6 us
    ppermute x6, starting transfers between devices, along_grp(): return [lax.ppermute(arrays[0], 'grp', downward + upward)]  5.43 us
    ppermute x2, starting transfers between devices, send_around(): return ([lax.ppermute(both, ('dom', 'grp'), crossing)], both)  4.83 us
    ppermute x1, starting transfers between devices, swap_odd(): return lax.ppermute(array, 'dom', pairing(1))  4.06 us
    ppermute x6, waiting for transfers between devices, along_grp(): return [lax.ppermute(arrays[0], 'grp', downward + upward)]  2.85 us
    ppermute x2, waiting for transfers between devices, send_around(): return ([lax.ppermute(both, ('dom', 'grp'), crossing)], both)  2.54 us
    ppermute x1, waiting for transfers between devices, swap_odd(): return lax.ppermute(array, 'dom', pairing(1))  1.74 us
  transfers between devices with their start and end apart: 10, of which 5 were waited for; matrix products, arithmetic and copies ran while one was open for 0% of the time, Pallas kernels for 21%

profile of v4, /device:TPU:19, one launch (start us, length us, event | category | flops | bytes accessed | tf_op | source)
XLA Modules:
  0.0 35.1 jit_solution(7512883721935093449)
XLA Ops:
  0.6 1.7 %shard_map.75 = (f32[32,32,128]{2,1,0:T(8,128)S(1)}, f32[32,32,128]{2,1,0:T(8,128)S(1)}, f32[32,32,128]{2,1,0:T(8,128)S(1)}, f32[13,32,128]{2,1,0:T(8,128)S(1)},...) custom-call(f32[32,32,128]{2,1,0:T(8,128)} %src_hbm.1, ...), custom_call_target="tpu_custom_call" | custom-call | tf_op jit(solution)/shard_map/pallas_call | solution.py:540
  2.3 0.7 %collective-permute-start = (f32[3,32,8,128]{3,2,1,0:T(8,128)S(1)}, f32[3,32,8,128]{3,2,1,0:T(8,128)S(1)}, u32[]{:S(2)}, u32[]{:S(2)}) collective-permute-start(f32[3,32,8,128]{3,2,1,0:T(8,128)S(1)} %get-tuple-element.45), channel_id=1, source_target_pairs={{1,0},{0,1},{3,2},{2,3},{5,4},{4,5},{7,6},{6,7},{9,8},{8,9},{11,10... | collective-permute-start | bytes 1179656 | tf_op jit(solution)/shard_map/ppermute | solution.py:573
  3.1 0.1 collective-permute-start.6
  3.1 0.3 collective-permute-start.1
  3.4 4.1 %collective-permute-start.2 = (f32[13,32,128]{2,1,0:T(8,128)S(1)}, f32[13,32,128]{2,1,0:T(8,128)S(1)}, u32[]{:S(2)}, u32[]{:S(2)}) collective-permute-start(f32[13,32,128]{2,1,0:T(8,128)S(1)} %get-tuple-element.60), channel_id=1, source_target_pairs={{2,4},{6,8},{10,12},{14,16},{18,20},{22,24},{26,28},{4,2},{8,6},{1... | collective-permute-start | bytes 638984 | tf_op jit(solution)/shard_map/ppermute | solution.py:564
  7.5 0.0 collective-permute-done.6.refs_1_
  7.5 2.9 %collective-permute-start.7 = (f32[2,16,16,128]{3,2,1,0:T(8,128)S(1)}, f32[2,16,16,128]{3,2,1,0:T(8,128)S(1)}, u32[]{:S(2)}, u32[]{:S(2)}) collective-permute-start(f32[2,16,16,128]{3,2,1,0:T(8,128)S(1)} %shard_map.81), channel_id=1, source_target_pairs={{0,3},{3,0},{2,5},{5,2},{4,7},{7,4},{6,9},{9,6},{8,11},{11,8},{10,... | collective-permute-start | bytes 786440 | tf_op jit(solution)/shard_map/ppermute | solution.py:583
  10.4 0.0 collective-permute-done.refs_3_
  10.4 2.9 %shard_map.76 = (f32[32,40,128]{2,1,0:T(8,128)S(1)}, f32[32,40,128]{2,1,0:T(8,128)S(1)}, f32[32,40,128]{2,1,0:T(8,128)S(1)}, f32[32,40,128]{2,1,0:T(8,128)S(1)},...) custom-call(f32[32,32,128]{2,1,0:T(8,128)S(1)} %get-tuple-element.42, ...), custom_call_target="tpu_custom_call" | custom-call | tf_op jit(solution)/shard_map/pallas_call | solution.py:540
  13.3 0.0 collective-permute-done.1.ra_ref.refs_16_
  13.3 1.7 %collective-permute-done.2.rb_ref.refs_17_ = f32[13,32,128]{2,1,0:T(8,128)S(1)} collective-permute-done((f32[13,32,128]{2,1,0:T(8,128)S(1)}, f32[13,32,128]{2,1,0:T(8,128)S(1)}, u32[]{:S(2)}, u32[]{:S(2)}) %collective-permute-start.2) | collective-permute-done | bytes 213024 | tf_op jit(solution)/shard_map/ppermute | solution.py:564
  15.1 3.2 %collective-permute-start.3 = (f32[2,13,8,128]{3,2,1,0:T(8,128)S(1)}, f32[2,13,8,128]{3,2,1,0:T(8,128)S(1)}, u32[]{:S(2)}, u32[]{:S(2)}) collective-permute-start(f32[2,13,8,128]{3,2,1,0:T(8,128)S(1)} %shard_map.77), channel_id=1, source_target_pairs={{1,0},{0,1},{3,2},{2,3},{5,4},{4,5},{7,6},{6,7},{9,8},{8,9},{11,10... | collective-permute-start | bytes 319496 | tf_op jit(solution)/shard_map/ppermute | solution.py:573
  18.3 1.0 %collective-permute-done.3.refs_18_ = f32[2,13,8,128]{3,2,1,0:T(8,128)S(1)} collective-permute-done((f32[2,13,8,128]{3,2,1,0:T(8,128)S(1)}, f32[2,13,8,128]{3,2,1,0:T(8,128)S(1)}, u32[]{:S(2)}, u32[]{:S(2)}) %collective-permute-start.3) | collective-permute-done | bytes 106528 | tf_op jit(solution)/shard_map/ppermute | solution.py:573
  19.2 1.2 %shard_map.78 = (f32[10,32,128]{2,1,0:T(8,128)S(1)}, f32[10,32,128]{2,1,0:T(8,128)S(1)}, f32[8,16,128]{2,1,0:T(8,128)S(1)}) custom-call(f32[32,32,128]{2,1,0:T(8,128)S(1)} %get-tuple-element.42.refs_0_, f32[32,32,128]{2,1,0:T(8,128)S(1)} %get-tuple-element.43.refs_1_, f32[32,32,128]{2,1,0:T(8,128)S(1)} %get-tuple-element.44.refs_2_, ...), custom_call_target="tpu_custom_call" | custom-call | tf_op jit(solution)/shard_map/pallas_call | solution.py:540
  20.4 0.4 %collective-permute-start.4 = (f32[8,16,128]{2,1,0:T(8,128)S(1)}, f32[8,16,128]{2,1,0:T(8,128)S(1)}, u32[]{:S(2)}, u32[]{:S(2)}) collective-permute-start(f32[8,16,128]{2,1,0:T(8,128)S(1)} %get-tuple-element.65.refs_0_), channel_id=1, source_target_pairs={{1,0},{0,1},{3,2},{2,3},{5,4},{4,5},{7,6},{6,7},{9,8},{8,9},{11,10... | collective-permute-start | bytes 196616 | tf_op jit(solution)/shard_map/ppermute | solution.py:573
  20.8 0.9 %collective-permute-done.4.refs_1_ = f32[8,16,128]{2,1,0:T(8,128)S(1)} collective-permute-done((f32[8,16,128]{2,1,0:T(8,128)S(1)}, f32[8,16,128]{2,1,0:T(8,128)S(1)}, u32[]{:S(2)}, u32[]{:S(2)}) %collective-permute-start.4) | collective-permute-done | bytes 65568 | tf_op jit(solution)/shard_map/ppermute | solution.py:573
  21.7 0.0 collective-permute-done.7.refs_0_
  21.8 0.4 %collective-permute-start.8 = (f32[2,16,16,128]{3,2,1,0:T(8,128)S(1)}, f32[2,16,16,128]{3,2,1,0:T(8,128)S(1)}, u32[]{:S(2)}, u32[]{:S(2)}) collective-permute-start(f32[2,16,16,128]{3,2,1,0:T(8,128)S(1)} %bitcast.2), channel_id=1, source_target_pairs={{1,0},{0,1},{3,2},{2,3},{5,4},{4,5},{7,6},{6,7},{9,8},{8,9},{11,10... | collective-permute-start | bytes 786440 | tf_op jit(solution)/shard_map/ppermute | solution.py:573
  22.2 1.9 %collective-permute-start.5 = (f32[2,8,16,128]{3,2,1,0:T(8,128)S(1)}, f32[2,8,16,128]{3,2,1,0:T(8,128)S(1)}, u32[]{:S(2)}, u32[]{:S(2)}) collective-permute-start(f32[2,8,16,128]{3,2,1,0:T(8,128)S(1)} %shard_map.80.refs_1_), channel_id=1, source_target_pairs={{0,3},{3,0},{2,5},{5,2},{4,7},{7,4},{6,9},{9,6},{8,11},{11,8},{10,... | collective-permute-start | bytes 393224 | tf_op jit(solution)/shard_map/ppermute | solution.py:583
  24.1 1.0 %shard_map.79 = (f32[32,32,128]{2,1,0:T(8,128)}, f32[32,32,128]{2,1,0:T(8,128)}, f32[8,128]{1,0:T(8,128)S(1)}) custom-call(f32[32,32,128]{2,1,0:T(8,128)S(1)} %get-tuple-element.46.it_in, f32[32,32,128]{2,1,0:T(8,128)S(1)} %get-tuple-element.47.refs_14_.res_in, f32[10,32,128]{2,1,0:T(8,128)S(1)} %get-tuple-element.61.it_rim, ...), custom_call_target="tpu_custom_call" | custom-call | tf_op jit(solution)/shard_map/pallas_call | solution.py:540
  25.1 0.0 collective-permute-done.8.refs_3_
  25.1 2.4 %shard_map.83 = (f32[24,32,128]{2,1,0:T(8,128)S(1)}, f32[24,32,128]{2,1,0:T(8,128)S(1)}, f32[24,32,128]{2,1,0:T(8,128)S(1)}, f32[24,32,128]{2,1,0:T(8,128)S(1)},...) custom-call(f32[16,16,128]{2,1,0:T(8,128)S(1)} %get-tuple-element.66, ...), custom_call_target="tpu_custom_call" | custom-call | tf_op jit(solution)/shard_map/pallas_call | solution.py:540
  27.5 2.5 %collective-permute-done.5.refs_0_ = f32[2,8,16,128]{3,2,1,0:T(8,128)S(1)} collective-permute-done((f32[2,8,16,128]{3,2,1,0:T(8,128)S(1)}, f32[2,8,16,128]{3,2,1,0:T(8,128)S(1)}, u32[]{:S(2)}, u32[]{:S(2)}) %collective-permute-start.5) | collective-permute-done | bytes 131104 | tf_op jit(solution)/shard_map/ppermute | solution.py:583
  30.0 0.6 %collective-permute-start.9 = (f32[2,8,16,128]{3,2,1,0:T(8,128)S(1)}, f32[2,8,16,128]{3,2,1,0:T(8,128)S(1)}, u32[]{:S(2)}, u32[]{:S(2)}) collective-permute-start(f32[2,8,16,128]{3,2,1,0:T(8,128)S(1)} %bitcast.4), channel_id=1, source_target_pairs={{1,0},{0,1},{3,2},{2,3},{5,4},{4,5},{7,6},{6,7},{9,8},{8,9},{11,10... | collective-permute-start | bytes 393224 | tf_op jit(solution)/shard_map/ppermute | solution.py:573
  30.6 1.0 %collective-permute-done.9.refs_3_ = f32[2,8,16,128]{3,2,1,0:T(8,128)S(1)} collective-permute-done((f32[2,8,16,128]{3,2,1,0:T(8,128)S(1)}, f32[2,8,16,128]{3,2,1,0:T(8,128)S(1)}, u32[]{:S(2)}, u32[]{:S(2)}) %collective-permute-start.9) | collective-permute-done | bytes 131104 | tf_op jit(solution)/shard_map/ppermute | solution.py:573
  31.6 3.5 %shard_map.85 = (f32[16,16,64]{2,1,0:T(8,128)}, f32[8,8,32]{2,1,0:T(8,128)}) custom-call(f32[8,16,128]{2,1,0:T(8,128)S(1)} %get-tuple-element.65.refs_0_, f32[8,16,128]{2,1,0:T(8,128)S(1)} %collective-permute-done.4.refs_1_, f32[2,8,16,128]{3,2,1,0:T(8,128)S(1)} %bitcast.5, f32[2,8,16,128]{3,2,1,0:T(8,128)S(1)} %collective-permute-done.9.refs_3_, ...), custom_call_target="tpu_custom_call" | custom-call | tf_op jit(solution)/shard_map/pallas_call | solution.py:540
  (5 shorter events, 0.1 us)
Async XLA Ops:
  2.3 8.1 %collective-permute-start = (f32[3,32,8,128]{3,2,1,0:T(8,128)S(1)}, f32[3,32,8,128]{3,2,1,0:T(8,128)S(1)}, u32[]{:S(2)}, u32[]{:S(2)}) collective-permute-start(f32[3,32,8,128]{3,2,1,0:T(8,128)S(1)} %get-tuple-element.45), channel_id=1, source_target_pairs={{1,0},{0,1},{3,2},{2,3},{5,4},{4,5},{7,6},{6,7},{9,8},{8,9},{11,10... | collective-permute-start | bytes 1179656 | tf_op jit(solution)/shard_map/ppermute | solution.py:573
  3.1 4.4 %collective-permute-start.6 = (f32[16,16,128]{2,1,0:T(8,128)S(1)}, f32[16,16,128]{2,1,0:T(8,128)S(1)}, u32[]{:S(2)}, u32[]{:S(2)}) collective-permute-start(f32[16,16,128]{2,1,0:T(8,128)S(1)} %get-tuple-element.66.refs_0_), channel_id=1, source_target_pairs={{1,0},{0,1},{3,2},{2,3},{5,4},{4,5},{7,6},{6,7},{9,8},{8,9},{11,10... | collective-permute-start | bytes 393224 | tf_op jit(solution)/shard_map/ppermute | solution.py:573
  3.1 10.2 %collective-permute-start.1 = (f32[13,32,128]{2,1,0:T(8,128)S(1)}, f32[13,32,128]{2,1,0:T(8,128)S(1)}, u32[]{:S(2)}, u32[]{:S(2)}) collective-permute-start(f32[13,32,128]{2,1,0:T(8,128)S(1)} %get-tuple-element.59), channel_id=1, source_target_pairs={{0,2},{4,6},{8,10},{12,14},{16,18},{20,22},{24,26},{28,30},{2,0},{... | collective-permute-start | bytes 638984 | tf_op jit(solution)/shard_map/ppermute | solution.py:561
  3.4 11.7 %collective-permute-start.2 = (f32[13,32,128]{2,1,0:T(8,128)S(1)}, f32[13,32,128]{2,1,0:T(8,128)S(1)}, u32[]{:S(2)}, u32[]{:S(2)}) collective-permute-start(f32[13,32,128]{2,1,0:T(8,128)S(1)} %get-tuple-element.60), channel_id=1, source_target_pairs={{2,4},{6,8},{10,12},{14,16},{18,20},{22,24},{26,28},{4,2},{8,6},{1... | collective-permute-start | bytes 638984 | tf_op jit(solution)/shard_map/ppermute | solution.py:564
  7.5 14.2 %collective-permute-start.7 = (f32[2,16,16,128]{3,2,1,0:T(8,128)S(1)}, f32[2,16,16,128]{3,2,1,0:T(8,128)S(1)}, u32[]{:S(2)}, u32[]{:S(2)}) collective-permute-start(f32[2,16,16,128]{3,2,1,0:T(8,128)S(1)} %shard_map.81), channel_id=1, source_target_pairs={{0,3},{3,0},{2,5},{5,2},{4,7},{7,4},{6,9},{9,6},{8,11},{11,8},{10,... | collective-permute-start | bytes 786440 | tf_op jit(solution)/shard_map/ppermute | solution.py:583
  15.1 4.2 %collective-permute-start.3 = (f32[2,13,8,128]{3,2,1,0:T(8,128)S(1)}, f32[2,13,8,128]{3,2,1,0:T(8,128)S(1)}, u32[]{:S(2)}, u32[]{:S(2)}) collective-permute-start(f32[2,13,8,128]{3,2,1,0:T(8,128)S(1)} %shard_map.77), channel_id=1, source_target_pairs={{1,0},{0,1},{3,2},{2,3},{5,4},{4,5},{7,6},{6,7},{9,8},{8,9},{11,10... | collective-permute-start | bytes 319496 | tf_op jit(solution)/shard_map/ppermute | solution.py:573
  20.4 1.3 %collective-permute-start.4 = (f32[8,16,128]{2,1,0:T(8,128)S(1)}, f32[8,16,128]{2,1,0:T(8,128)S(1)}, u32[]{:S(2)}, u32[]{:S(2)}) collective-permute-start(f32[8,16,128]{2,1,0:T(8,128)S(1)} %get-tuple-element.65.refs_0_), channel_id=1, source_target_pairs={{1,0},{0,1},{3,2},{2,3},{5,4},{4,5},{7,6},{6,7},{9,8},{8,9},{11,10... | collective-permute-start | bytes 196616 | tf_op jit(solution)/shard_map/ppermute | solution.py:573
  21.8 3.4 %collective-permute-start.8 = (f32[2,16,16,128]{3,2,1,0:T(8,128)S(1)}, f32[2,16,16,128]{3,2,1,0:T(8,128)S(1)}, u32[]{:S(2)}, u32[]{:S(2)}) collective-permute-start(f32[2,16,16,128]{3,2,1,0:T(8,128)S(1)} %bitcast.2), channel_id=1, source_target_pairs={{1,0},{0,1},{3,2},{2,3},{5,4},{4,5},{7,6},{6,7},{9,8},{8,9},{11,10... | collective-permute-start | bytes 786440 | tf_op jit(solution)/shard_map/ppermute | solution.py:573
  22.2 7.8 %collective-permute-start.5 = (f32[2,8,16,128]{3,2,1,0:T(8,128)S(1)}, f32[2,8,16,128]{3,2,1,0:T(8,128)S(1)}, u32[]{:S(2)}, u32[]{:S(2)}) collective-permute-start(f32[2,8,16,128]{3,2,1,0:T(8,128)S(1)} %shard_map.80.refs_1_), channel_id=1, source_target_pairs={{0,3},{3,0},{2,5},{5,2},{4,7},{7,4},{6,9},{9,6},{8,11},{11,8},{10,... | collective-permute-start | bytes 393224 | tf_op jit(solution)/shard_map/ppermute | solution.py:583
  30.0 1.6 %collective-permute-start.9 = (f32[2,8,16,128]{3,2,1,0:T(8,128)S(1)}, f32[2,8,16,128]{3,2,1,0:T(8,128)S(1)}, u32[]{:S(2)}, u32[]{:S(2)}) collective-permute-start(f32[2,8,16,128]{3,2,1,0:T(8,128)S(1)} %bitcast.4), channel_id=1, source_target_pairs={{1,0},{0,1},{3,2},{2,3},{5,4},{4,5},{7,6},{6,7},{9,8},{8,9},{11,10... | collective-permute-start | bytes 393224 | tf_op jit(solution)/shard_map/ppermute | solution.py:573

commit v5 on v4

--- a/solution.py
+++ b/solution.py
@@ -147,14 +147,21 @@
 def level_pass(lo, hi, k, degree, lowest, zstep, inv_ref, wx_ref, wy_ref, wz_ref, e_ref, u_refs, packed=False, wb_ref=None):
     _, steps = chebyshev_constants(degree, lowest, SMOOTH_HIGH)
     old = u_refs[k]
+    kept = {}
 
     def row(i):
-        u = old[i]
+        if isinstance(i, int) and i - 1 in kept:
+            u, before = kept.pop(i - 1)
+        else:
+            u, before = old[i], wx_ref[i - 1] * old[i - 1]
+        following = old[i + 1]
         wx = wx_ref[i]
         wy = wy_ref[i]
         wz = wz_ref[i]
-        coupled = wx * next_row(u, old[i + 1], packed)
-        coupled = coupled + previous_row(wx_ref[i - 1] * old[i - 1], wx * u if packed else None, packed)
+        weighted = wx * u
+        if isinstance(i, int):
+            kept[i] = following, weighted
+        coupled = wx * next_row(u, following, packed) + previous_row(before, weighted, packed)
         if wb_ref is None:
             coupled = coupled + (wy * ahead(u, 0) + behind(wy * u, 0))
         else:
@@ -355,15 +362,17 @@
 
 def stack_kernel(count, *refs):
     out = refs[-1]
+    spare = refs[0].shape[0] - out.shape[1]
+    first = jnp.where(lax.axis_index("grp") == 0, spare, 0) if spare else 0
     for part in range(count):
         for j in range(out.shape[1]):
-            out[part, j] = refs[part][j]
-
-
-def stack(arrays, *earlier):
-    (out,) = call(
-        functools.partial(stack_kernel, len(arrays)), (*arrays, *earlier), [(len(arrays), *arrays[0].shape)]
-    )
+            out[part, j] = refs[part][first + j]
+
+
+def stack(arrays, *earlier, spare=0):
+    rows, *rest = arrays[0].shape
+    shape = (len(arrays), rows - spare, *rest)
+    (out,) = call(functools.partial(stack_kernel, len(arrays)), (*arrays, *earlier), [shape])
     return out
 
 
@@ -452,12 +461,12 @@
     return jnp.dot(value, pick, preferred_element_type=jnp.float32, precision=lax.Precision.HIGHEST)
 
 
-def placed_parts(slots, rows, own_refs, around_refs):
+def placed_parts(slots, rows, own_refs, around_refs, unread=0):
     parts = [(rows, slot, ref) for slot, ref in enumerate(own_refs)]
     if slots == 1:
         core = lax.axis_index("grp")
         for which, (ref, above) in enumerate(zip(around_refs, (core == 0, core == 1))):
-            start = jnp.where(above, 2 * rows, 0)
+            start = jnp.where(above, 2 * rows, unread)
             parts += [(start, 0, ref.at[1 - which]), (start, 1, ref.at[which])]
     else:
         even = lax.axis_index("dom") % 2 == 0
@@ -501,9 +510,10 @@
     wx, wy, wz, wb, inv, d_ref, cwx, cwy, cwz, cinv, mid_out, coarse_out = refs[:12]
     b_ref, e_ref, u0, u1, u2, u3, cb, ce, v0, v1, v2, v3, v4, v5, pair_ref = refs[12:]
     rows, ny, nz = own_refs[0].shape
-    for start, slot, s_ref in placed_parts(slots, rows, own_refs, around_refs):
+    unread = rows - around_refs[0].shape[1]
+    for start, slot, s_ref in placed_parts(slots, rows, own_refs, around_refs, unread):
         at = slice(slot * ny, (slot + 1) * ny)
-        for j in range(rows):
+        for j in range(s_ref.shape[0]):
             b_ref[start + j, at] = s_ref[j]
 
     reach = 2 * (COARSE_DEGREE - 1)
@@ -577,9 +587,9 @@
     for i in range(doms - 1):
         crossing += [(i * grps, (i + 1) * grps + 1), ((i + 1) * grps + 1, i * grps)]
 
-    def send_around(own, beside):
+    def send_around(own, beside, spare=0):
         if slots == 1:
-            both = stack([own, beside[0]])
+            both = stack([own, beside[0]], spare=spare)
             return [lax.ppermute(both, ("dom", "grp"), crossing)], both
         return [swap_even(own), swap_odd(own)], own
 
@@ -636,7 +646,8 @@
     )
 
     source_beside = along_grp([mid_source])
-    source_sent, sending = send_around(mid_source, source_beside)
+    unread = packed - -(-(2 * (COARSE_DEGREE - 1) + DEGREE) // 2)
+    source_sent, sending = send_around(mid_source, source_beside, unread)
     q_ins = [coeffs, *coeffs_beside, *share_around(coeffs_sent, sending)]
     mid_y = (1 + slots) * ny // 2
     mid_wide = (3 * packed, mid_y, nz)

time: 35.4 us -> 35 us (0.989)
  no operation moved by 1% of the time
where the time goes in v5:
time: 35 us; the launch traced here: 34.7 us
  starting transfers between devices  14.6 us (42%)
  Pallas kernels  12.5 us (36%)
  waiting for transfers between devices  6.89 us (20%)
  between operations  0.76 us (2%)
    pallas_call x11, Pallas kernels, call(): pl.pallas_call(kernel, out_shape=[jax.ShapeDtypeStruct(shape, jnp.float32...  12.5 us
    ppermute x6, starting transfers between devices, along_grp(): return [lax.ppermute(arrays[0], 'grp', downward + upward)]  5.42 us
    ppermute x2, starting transfers between devices, send_around(): return ([lax.ppermute(both, ('dom', 'grp'), crossing)], both)  4.83 us
    ppermute x1, starting transfers between devices, swap_odd(): return lax.ppermute(array, 'dom', pairing(1))  4.06 us
    ppermute x6, waiting for transfers between devices, along_grp(): return [lax.ppermute(arrays[0], 'grp', downward + upward)]  2.83 us
    ppermute x2, waiting for transfers between devices, send_around(): return ([lax.ppermute(both, ('dom', 'grp'), crossing)], both)  2.2 us
    ppermute x1, waiting for transfers between devices, swap_odd(): return lax.ppermute(array, 'dom', pairing(1))  1.86 us
  transfers between devices with their start and end apart: 10, of which 5 were waited for; matrix products, arithmetic and copies ran while one was open for 0% of the time, Pallas kernels for 21%

profile of v5, /device:TPU:19, one launch (start us, length us, event | category | flops | bytes accessed | tf_op | source)
XLA Modules:
  0.0 34.7 jit_solution(15575462947854221610)
XLA Ops:
  0.6 1.7 %shard_map.75 = (f32[32,32,128]{2,1,0:T(8,128)S(1)}, f32[32,32,128]{2,1,0:T(8,128)S(1)}, f32[32,32,128]{2,1,0:T(8,128)S(1)}, f32[13,32,128]{2,1,0:T(8,128)S(1)},...) custom-call(f32[32,32,128]{2,1,0:T(8,128)} %src_hbm.1, ...), custom_call_target="tpu_custom_call" | custom-call | tf_op jit(solution)/shard_map/pallas_call | solution.py:550
  2.3 0.7 %collective-permute-start = (f32[3,32,8,128]{3,2,1,0:T(8,128)S(1)}, f32[3,32,8,128]{3,2,1,0:T(8,128)S(1)}, u32[]{:S(2)}, u32[]{:S(2)}) collective-permute-start(f32[3,32,8,128]{3,2,1,0:T(8,128)S(1)} %get-tuple-element.45), channel_id=1, source_target_pairs={{1,0},{0,1},{3,2},{2,3},{5,4},{4,5},{7,6},{6,7},{9,8},{8,9},{11,10... | collective-permute-start | bytes 1179656 | tf_op jit(solution)/shard_map/ppermute | solution.py:583
  3.1 0.1 collective-permute-start.6
  3.1 0.3 collective-permute-start.1
  3.4 4.1 %collective-permute-start.2 = (f32[13,32,128]{2,1,0:T(8,128)S(1)}, f32[13,32,128]{2,1,0:T(8,128)S(1)}, u32[]{:S(2)}, u32[]{:S(2)}) collective-permute-start(f32[13,32,128]{2,1,0:T(8,128)S(1)} %get-tuple-element.60), channel_id=1, source_target_pairs={{2,4},{6,8},{10,12},{14,16},{18,20},{22,24},{26,28},{4,2},{8,6},{1... | collective-permute-start | bytes 638984 | tf_op jit(solution)/shard_map/ppermute | solution.py:574
  7.5 0.0 collective-permute-done.6.refs_1_
  7.5 2.9 %collective-permute-start.7 = (f32[2,16,16,128]{3,2,1,0:T(8,128)S(1)}, f32[2,16,16,128]{3,2,1,0:T(8,128)S(1)}, u32[]{:S(2)}, u32[]{:S(2)}) collective-permute-start(f32[2,16,16,128]{3,2,1,0:T(8,128)S(1)} %shard_map.81), channel_id=1, source_target_pairs={{0,3},{3,0},{2,5},{5,2},{4,7},{7,4},{6,9},{9,6},{8,11},{11,8},{10,... | collective-permute-start | bytes 786440 | tf_op jit(solution)/shard_map/ppermute | solution.py:593
  10.4 0.0 collective-permute-done.refs_3_
  10.4 2.7 %shard_map.76 = (f32[32,40,128]{2,1,0:T(8,128)S(1)}, f32[32,40,128]{2,1,0:T(8,128)S(1)}, f32[32,40,128]{2,1,0:T(8,128)S(1)}, f32[32,40,128]{2,1,0:T(8,128)S(1)},...) custom-call(f32[32,32,128]{2,1,0:T(8,128)S(1)} %get-tuple-element.42, ...), custom_call_target="tpu_custom_call" | custom-call | tf_op jit(solution)/shard_map/pallas_call | solution.py:550
  13.2 0.0 collective-permute-done.1.ra_ref.refs_16_
  13.2 1.9 %collective-permute-done.2.rb_ref.refs_17_ = f32[13,32,128]{2,1,0:T(8,128)S(1)} collective-permute-done((f32[13,32,128]{2,1,0:T(8,128)S(1)}, f32[13,32,128]{2,1,0:T(8,128)S(1)}, u32[]{:S(2)}, u32[]{:S(2)}) %collective-permute-start.2) | collective-permute-done | bytes 213024 | tf_op jit(solution)/shard_map/ppermute | solution.py:574
  15.1 3.2 %collective-permute-start.3 = (f32[2,13,8,128]{3,2,1,0:T(8,128)S(1)}, f32[2,13,8,128]{3,2,1,0:T(8,128)S(1)}, u32[]{:S(2)}, u32[]{:S(2)}) collective-permute-start(f32[2,13,8,128]{3,2,1,0:T(8,128)S(1)} %shard_map.77), channel_id=1, source_target_pairs={{1,0},{0,1},{3,2},{2,3},{5,4},{4,5},{7,6},{6,7},{9,8},{8,9},{11,10... | collective-permute-start | bytes 319496 | tf_op jit(solution)/shard_map/ppermute | solution.py:583
  18.3 1.0 %collective-permute-done.3.refs_18_ = f32[2,13,8,128]{3,2,1,0:T(8,128)S(1)} collective-permute-done((f32[2,13,8,128]{3,2,1,0:T(8,128)S(1)}, f32[2,13,8,128]{3,2,1,0:T(8,128)S(1)}, u32[]{:S(2)}, u32[]{:S(2)}) %collective-permute-start.3) | collective-permute-done | bytes 106528 | tf_op jit(solution)/shard_map/ppermute | solution.py:583
  19.2 1.2 %shard_map.78 = (f32[10,32,128]{2,1,0:T(8,128)S(1)}, f32[10,32,128]{2,1,0:T(8,128)S(1)}, f32[8,16,128]{2,1,0:T(8,128)S(1)}) custom-call(f32[32,32,128]{2,1,0:T(8,128)S(1)} %get-tuple-element.42.refs_0_, f32[32,32,128]{2,1,0:T(8,128)S(1)} %get-tuple-element.43.refs_1_, f32[32,32,128]{2,1,0:T(8,128)S(1)} %get-tuple-element.44.refs_2_, ...), custom_call_target="tpu_custom_call" | custom-call | tf_op jit(solution)/shard_map/pallas_call | solution.py:550
  20.4 0.4 %collective-permute-start.4 = (f32[8,16,128]{2,1,0:T(8,128)S(1)}, f32[8,16,128]{2,1,0:T(8,128)S(1)}, u32[]{:S(2)}, u32[]{:S(2)}) collective-permute-start(f32[8,16,128]{2,1,0:T(8,128)S(1)} %get-tuple-element.65.refs_0_), channel_id=1, source_target_pairs={{1,0},{0,1},{3,2},{2,3},{5,4},{4,5},{7,6},{6,7},{9,8},{8,9},{11,10... | collective-permute-start | bytes 196616 | tf_op jit(solution)/shard_map/ppermute | solution.py:583
  20.8 0.9 %collective-permute-done.4.refs_1_ = f32[8,16,128]{2,1,0:T(8,128)S(1)} collective-permute-done((f32[8,16,128]{2,1,0:T(8,128)S(1)}, f32[8,16,128]{2,1,0:T(8,128)S(1)}, u32[]{:S(2)}, u32[]{:S(2)}) %collective-permute-start.4) | collective-permute-done | bytes 65568 | tf_op jit(solution)/shard_map/ppermute | solution.py:583
  21.7 0.0 collective-permute-done.7.refs_0_
  21.8 0.4 %collective-permute-start.8 = (f32[2,16,16,128]{3,2,1,0:T(8,128)S(1)}, f32[2,16,16,128]{3,2,1,0:T(8,128)S(1)}, u32[]{:S(2)}, u32[]{:S(2)}) collective-permute-start(f32[2,16,16,128]{3,2,1,0:T(8,128)S(1)} %bitcast.2), channel_id=1, source_target_pairs={{1,0},{0,1},{3,2},{2,3},{5,4},{4,5},{7,6},{6,7},{9,8},{8,9},{11,10... | collective-permute-start | bytes 786440 | tf_op jit(solution)/shard_map/ppermute | solution.py:583
  22.2 1.9 %collective-permute-start.5 = (f32[2,7,16,128]{3,2,1,0:T(8,128)S(1)}, f32[2,7,16,128]{3,2,1,0:T(8,128)S(1)}, u32[]{:S(2)}, u32[]{:S(2)}) collective-permute-start(f32[2,7,16,128]{3,2,1,0:T(8,128)S(1)} %shard_map.80.refs_1_), channel_id=1, source_target_pairs={{0,3},{3,0},{2,5},{5,2},{4,7},{7,4},{6,9},{9,6},{8,11},{11,8},{10,... | collective-permute-start | bytes 344072 | tf_op jit(solution)/shard_map/ppermute | solution.py:593
  24.1 1.0 %shard_map.79 = (f32[32,32,128]{2,1,0:T(8,128)}, f32[32,32,128]{2,1,0:T(8,128)}, f32[8,128]{1,0:T(8,128)S(1)}) custom-call(f32[32,32,128]{2,1,0:T(8,128)S(1)} %get-tuple-element.46.it_in, f32[32,32,128]{2,1,0:T(8,128)S(1)} %get-tuple-element.47.refs_14_.res_in, f32[10,32,128]{2,1,0:T(8,128)S(1)} %get-tuple-element.61.it_rim, ...), custom_call_target="tpu_custom_call" | custom-call | tf_op jit(solution)/shard_map/pallas_call | solution.py:550
  25.1 0.0 collective-permute-done.8.refs_3_
  25.1 2.4 %shard_map.83 = (f32[24,32,128]{2,1,0:T(8,128)S(1)}, f32[24,32,128]{2,1,0:T(8,128)S(1)}, f32[24,32,128]{2,1,0:T(8,128)S(1)}, f32[24,32,128]{2,1,0:T(8,128)S(1)},...) custom-call(f32[16,16,128]{2,1,0:T(8,128)S(1)} %get-tuple-element.66, ...), custom_call_target="tpu_custom_call" | custom-call | tf_op jit(solution)/shard_map/pallas_call | solution.py:550
  27.5 2.2 %collective-permute-done.5.refs_0_ = f32[2,7,16,128]{3,2,1,0:T(8,128)S(1)} collective-permute-done((f32[2,7,16,128]{3,2,1,0:T(8,128)S(1)}, f32[2,7,16,128]{3,2,1,0:T(8,128)S(1)}, u32[]{:S(2)}, u32[]{:S(2)}) %collective-permute-start.5) | collective-permute-done | bytes 114720 | tf_op jit(solution)/shard_map/ppermute | solution.py:593
  29.7 0.6 %collective-permute-start.9 = (f32[2,7,16,128]{3,2,1,0:T(8,128)S(1)}, f32[2,7,16,128]{3,2,1,0:T(8,128)S(1)}, u32[]{:S(2)}, u32[]{:S(2)}) collective-permute-start(f32[2,7,16,128]{3,2,1,0:T(8,128)S(1)} %bitcast.4), channel_id=1, source_target_pairs={{1,0},{0,1},{3,2},{2,3},{5,4},{4,5},{7,6},{6,7},{9,8},{8,9},{11,10... | collective-permute-start | bytes 344072 | tf_op jit(solution)/shard_map/ppermute | solution.py:583
  30.3 1.0 %collective-permute-done.9.refs_3_ = f32[2,7,16,128]{3,2,1,0:T(8,128)S(1)} collective-permute-done((f32[2,7,16,128]{3,2,1,0:T(8,128)S(1)}, f32[2,7,16,128]{3,2,1,0:T(8,128)S(1)}, u32[]{:S(2)}, u32[]{:S(2)}) %collective-permute-start.9) | collective-permute-done | bytes 114720 | tf_op jit(solution)/shard_map/ppermute | solution.py:583
  31.2 3.5 %shard_map.85 = (f32[16,16,64]{2,1,0:T(8,128)}, f32[8,8,32]{2,1,0:T(8,128)}) custom-call(f32[8,16,128]{2,1,0:T(8,128)S(1)} %get-tuple-element.65.refs_0_, f32[8,16,128]{2,1,0:T(8,128)S(1)} %collective-permute-done.4.refs_1_, f32[2,7,16,128]{3,2,1,0:T(8,128)S(1)} %bitcast.5, f32[2,7,16,128]{3,2,1,0:T(8,128)S(1)} %collective-permute-done.9.refs_3_, ...), custom_call_target="tpu_custom_call" | custom-call | tf_op jit(solution)/shard_map/pallas_call | solution.py:550
  (5 shorter events, 0.1 us)
Async XLA Ops:
  2.3 8.1 %collective-permute-start = (f32[3,32,8,128]{3,2,1,0:T(8,128)S(1)}, f32[3,32,8,128]{3,2,1,0:T(8,128)S(1)}, u32[]{:S(2)}, u32[]{:S(2)}) collective-permute-start(f32[3,32,8,128]{3,2,1,0:T(8,128)S(1)} %get-tuple-element.45), channel_id=1, source_target_pairs={{1,0},{0,1},{3,2},{2,3},{5,4},{4,5},{7,6},{6,7},{9,8},{8,9},{11,10... | collective-permute-start | bytes 1179656 | tf_op jit(solution)/shard_map/ppermute | solution.py:583
  3.1 4.4 %collective-permute-start.6 = (f32[16,16,128]{2,1,0:T(8,128)S(1)}, f32[16,16,128]{2,1,0:T(8,128)S(1)}, u32[]{:S(2)}, u32[]{:S(2)}) collective-permute-start(f32[16,16,128]{2,1,0:T(8,128)S(1)} %get-tuple-element.66.refs_0_), channel_id=1, source_target_pairs={{1,0},{0,1},{3,2},{2,3},{5,4},{4,5},{7,6},{6,7},{9,8},{8,9},{11,10... | collective-permute-start | bytes 393224 | tf_op jit(solution)/shard_map/ppermute | solution.py:583
  3.1 10.0 %collective-permute-start.1 = (f32[13,32,128]{2,1,0:T(8,128)S(1)}, f32[13,32,128]{2,1,0:T(8,128)S(1)}, u32[]{:S(2)}, u32[]{:S(2)}) collective-permute-start(f32[13,32,128]{2,1,0:T(8,128)S(1)} %get-tuple-element.59), channel_id=1, source_target_pairs={{0,2},{4,6},{8,10},{12,14},{16,18},{20,22},{24,26},{28,30},{2,0},{... | collective-permute-start | bytes 638984 | tf_op jit(solution)/shard_map/ppermute | solution.py:571
  3.4 11.7 %collective-permute-start.2 = (f32[13,32,128]{2,1,0:T(8,128)S(1)}, f32[13,32,128]{2,1,0:T(8,128)S(1)}, u32[]{:S(2)}, u32[]{:S(2)}) collective-permute-start(f32[13,32,128]{2,1,0:T(8,128)S(1)} %get-tuple-element.60), channel_id=1, source_target_pairs={{2,4},{6,8},{10,12},{14,16},{18,20},{22,24},{26,28},{4,2},{8,6},{1... | collective-permute-start | bytes 638984 | tf_op jit(solution)/shard_map/ppermute | solution.py:574
  7.5 14.2 %collective-permute-start.7 = (f32[2,16,16,128]{3,2,1,0:T(8,128)S(1)}, f32[2,16,16,128]{3,2,1,0:T(8,128)S(1)}, u32[]{:S(2)}, u32[]{:S(2)}) collective-permute-start(f32[2,16,16,128]{3,2,1,0:T(8,128)S(1)} %shard_map.81), channel_id=1, source_target_pairs={{0,3},{3,0},{2,5},{5,2},{4,7},{7,4},{6,9},{9,6},{8,11},{11,8},{10,... | collective-permute-start | bytes 786440 | tf_op jit(solution)/shard_map/ppermute | solution.py:593
  15.1 4.2 %collective-permute-start.3 = (f32[2,13,8,128]{3,2,1,0:T(8,128)S(1)}, f32[2,13,8,128]{3,2,1,0:T(8,128)S(1)}, u32[]{:S(2)}, u32[]{:S(2)}) collective-permute-start(f32[2,13,8,128]{3,2,1,0:T(8,128)S(1)} %shard_map.77), channel_id=1, source_target_pairs={{1,0},{0,1},{3,2},{2,3},{5,4},{4,5},{7,6},{6,7},{9,8},{8,9},{11,10... | collective-permute-start | bytes 319496 | tf_op jit(solution)/shard_map/ppermute | solution.py:583
  20.4 1.3 %collective-permute-start.4 = (f32[8,16,128]{2,1,0:T(8,128)S(1)}, f32[8,16,128]{2,1,0:T(8,128)S(1)}, u32[]{:S(2)}, u32[]{:S(2)}) collective-permute-start(f32[8,16,128]{2,1,0:T(8,128)S(1)} %get-tuple-element.65.refs_0_), channel_id=1, source_target_pairs={{1,0},{0,1},{3,2},{2,3},{5,4},{4,5},{7,6},{6,7},{9,8},{8,9},{11,10... | collective-permute-start | bytes 196616 | tf_op jit(solution)/shard_map/ppermute | solution.py:583
  21.8 3.4 %collective-permute-start.8 = (f32[2,16,16,128]{3,2,1,0:T(8,128)S(1)}, f32[2,16,16,128]{3,2,1,0:T(8,128)S(1)}, u32[]{:S(2)}, u32[]{:S(2)}) collective-permute-start(f32[2,16,16,128]{3,2,1,0:T(8,128)S(1)} %bitcast.2), channel_id=1, source_target_pairs={{1,0},{0,1},{3,2},{2,3},{5,4},{4,5},{7,6},{6,7},{9,8},{8,9},{11,10... | collective-permute-start | bytes 786440 | tf_op jit(solution)/shard_map/ppermute | solution.py:583
  22.2 7.5 %collective-permute-start.5 = (f32[2,7,16,128]{3,2,1,0:T(8,128)S(1)}, f32[2,7,16,128]{3,2,1,0:T(8,128)S(1)}, u32[]{:S(2)}, u32[]{:S(2)}) collective-permute-start(f32[2,7,16,128]{3,2,1,0:T(8,128)S(1)} %shard_map.80.refs_1_), channel_id=1, source_target_pairs={{0,3},{3,0},{2,5},{5,2},{4,7},{7,4},{6,9},{9,6},{8,11},{11,8},{10,... | collective-permute-start | bytes 344072 | tf_op jit(solution)/shard_map/ppermute | solution.py:593
  29.7 1.5 %collective-permute-start.9 = (f32[2,7,16,128]{3,2,1,0:T(8,128)S(1)}, f32[2,7,16,128]{3,2,1,0:T(8,128)S(1)}, u32[]{:S(2)}, u32[]{:S(2)}) collective-permute-start(f32[2,7,16,128]{3,2,1,0:T(8,128)S(1)} %bitcast.4), channel_id=1, source_target_pairs={{1,0},{0,1},{3,2},{2,3},{5,4},{4,5},{7,6},{6,7},{9,8},{8,9},{11,10... | collective-permute-start | bytes 344072 | tf_op jit(solution)/shard_map/ppermute | solution.py:583

commit v6 on v5

--- a/solution.py
+++ b/solution.py
@@ -478,7 +478,7 @@
 
 def coefficient_kernel(slots, *refs):
     own_refs, around_refs, refs = refs[: 1 + slots], refs[1 + slots : 2 + 2 * slots], refs[2 + 2 * slots :]
-    wx, wy, wz, wb, inv, d_ref, cwx, cwy, cwz, cinv, a_ref, g_ref, ca, cg, cd, pair_ref = refs
+    wx, wy, wz, wb, inv, d_ref, cwx, cwy, cwz, cwb, cinv, a_ref, g_ref, ca, cg, cd, pair_ref = refs
     rows, ny = own_refs[0].shape[0] // 2, own_refs[0].shape[1]
     for start, slot, q_ref in placed_parts(slots, rows, own_refs, around_refs):
         at = slice(slot * ny, (slot + 1) * ny)
@@ -502,13 +502,13 @@
         ca[i] = coarsen_packed(a_ref[row], pair_ref.at[3 * i + 2])
 
     rows_loop(0, coarse_rows, coefficients, block=10)
-    level_setup(1, coarse_rows - 1, 4, STEP_SCALE / 16.0, cg, ca, cwx, cwy, cwz, cinv, cd)
+    level_setup(1, coarse_rows - 1, 4, STEP_SCALE / 16.0, cg, ca, cwx, cwy, cwz, cinv, cd, wb_ref=cwb)
 
 
 def coarse_kernel(slots, *refs):
     own_refs, around_refs, refs = refs[: 1 + slots], refs[1 + slots : 2 + 2 * slots], refs[2 + 2 * slots :]
-    wx, wy, wz, wb, inv, d_ref, cwx, cwy, cwz, cinv, mid_out, coarse_out = refs[:12]
-    b_ref, e_ref, u0, u1, u2, u3, cb, ce, v0, v1, v2, v3, v4, v5, pair_ref = refs[12:]
+    wx, wy, wz, wb, inv, d_ref, cwx, cwy, cwz, cwb, cinv, mid_out, coarse_out = refs[:13]
+    b_ref, e_ref, u0, u1, u2, u3, cb, ce, v0, v1, v2, v3, v4, v5, pair_ref = refs[13:]
     rows, ny, nz = own_refs[0].shape
     unread = rows - around_refs[0].shape[1]
     for start, slot, s_ref in placed_parts(slots, rows, own_refs, around_refs, unread):
@@ -538,10 +538,12 @@
 
     rows_loop(1, half + 2 * cbase - 1, source)
     v_refs = (v0, v1, v2, v3, v4, v5)
-    level_sweeps(cbase, half, 0, COARSE_DEGREE, COARSE_LOW, False, 4, cb, cinv, cwx, cwy, cwz, ce, v_refs)
-    total = v0[cbase : cbase + half, :cny]
+    updates = [Circular(v_ref) for v_ref in v_refs]
+    weights = (cinv, cwx, cwy, cwz)
+    level_sweeps(cbase, half, 0, COARSE_DEGREE, COARSE_LOW, False, 4, cb, *weights, ce, updates, wb_ref=cwb)
+    total = v0[cbase : cbase + half, TILE : TILE + cny]
     for v_ref in v_refs[1:]:
-        total = total + v_ref[cbase : cbase + half, :cny]
+        total = total + v_ref[cbase : cbase + half, TILE : TILE + cny]
     coarse_out[...] = compact(total.reshape(half * cny, nz), 4).reshape(half, cny, nz // 4)
 
 
@@ -656,7 +658,7 @@
     weights = call(
         functools.partial(coefficient_kernel, slots),
         q_ins,
-        [mid_wide] * 6 + [coarse_wide] * 4,
+        [mid_wide] * 6 + [coarse_wide] * 5,
         [mid_wide] * 2 + [coarse_wide] * 3 + [(3 * coarse_rows, mid_y, nz)],
     )
     s_ins = [mid_source, *source_beside, *share_around(source_sent, weights[-1], written)]
@@ -664,7 +666,7 @@
         functools.partial(coarse_kernel, slots),
         (*s_ins, *weights),
         [(nx // 2, ny // 2, nz // 2), (nx // 4, ny // 4, nz // 4)],
-        [mid_wide] * 2 + [(3 * packed, mid_y + 2 * TILE, nz)] * 4 + [coarse_wide] * 8 + [(coarse_rows, mid_y, nz)],
+        [mid_wide] * 2 + [(3 * packed, mid_y + 2 * TILE, nz)] * 4 + [coarse_wide] * 2 + [(coarse_rows, mid_y // 2 + 2 * TILE, nz)] * 6 + [(coarse_rows, mid_y, nz)],
     )
     return (fine_iterate, fine_residual, mid_iterate, coarse_iterate)
 

time: 35 us -> 35 us (level)
  no operation moved by 1% of the time
where the time goes in v6:
time: 35 us; the launch traced here: 34.7 us
  starting transfers between devices  14.6 us (42%)
  Pallas kernels  12.5 us (36%)
  waiting for transfers between devices  6.89 us (20%)
  between operations  0.76 us (2%)
    pallas_call x11, Pallas kernels, call(): pl.pallas_call(kernel, out_shape=[jax.ShapeDtypeStruct(shape, jnp.float32...  12.5 us
    ppermute x6, starting transfers between devices, along_grp(): return [lax.ppermute(arrays[0], 'grp', downward + upward)]  5.42 us
    ppermute x2, starting transfers between devices, send_around(): return ([lax.ppermute(both, ('dom', 'grp'), crossing)], both)  4.83 us
    ppermute x1, starting transfers between devices, swap_odd(): return lax.ppermute(array, 'dom', pairing(1))  4.06 us
    ppermute x6, waiting for transfers between devices, along_grp(): return [lax.ppermute(arrays[0], 'grp', downward + upward)]  2.83 us
    ppermute x2, waiting for transfers between devices, send_around(): return ([lax.ppermute(both, ('dom', 'grp'), crossing)], both)  2.19 us
    ppermute x1, waiting for transfers between devices, swap_odd(): return lax.ppermute(array, 'dom', pairing(1))  1.86 us
  transfers between devices with their start and end apart: 10, of which 5 were waited for; matrix products, arithmetic and copies ran while one was open for 0% of the time, Pallas kernels for 21%

profile of v6, /device:TPU:19, one launch (start us, length us, event | category | flops | bytes accessed | tf_op | source)
XLA Modules:
  0.0 34.7 jit_solution(14182901662231560031)
XLA Ops:
  0.6 1.7 %shard_map.75 = (f32[32,32,128]{2,1,0:T(8,128)S(1)}, f32[32,32,128]{2,1,0:T(8,128)S(1)}, f32[32,32,128]{2,1,0:T(8,128)S(1)}, f32[13,32,128]{2,1,0:T(8,128)S(1)},...) custom-call(f32[32,32,128]{2,1,0:T(8,128)} %src_hbm.1, ...), custom_call_target="tpu_custom_call" | custom-call | tf_op jit(solution)/shard_map/pallas_call | solution.py:552
  2.3 0.7 %collective-permute-start = (f32[3,32,8,128]{3,2,1,0:T(8,128)S(1)}, f32[3,32,8,128]{3,2,1,0:T(8,128)S(1)}, u32[]{:S(2)}, u32[]{:S(2)}) collective-permute-start(f32[3,32,8,128]{3,2,1,0:T(8,128)S(1)} %get-tuple-element.46), channel_id=1, source_target_pairs={{1,0},{0,1},{3,2},{2,3},{5,4},{4,5},{7,6},{6,7},{9,8},{8,9},{11,10... | collective-permute-start | bytes 1179656 | tf_op jit(solution)/shard_map/ppermute | solution.py:585
  3.1 0.1 collective-permute-start.6
  3.1 0.3 collective-permute-start.1
  3.4 4.1 %collective-permute-start.2 = (f32[13,32,128]{2,1,0:T(8,128)S(1)}, f32[13,32,128]{2,1,0:T(8,128)S(1)}, u32[]{:S(2)}, u32[]{:S(2)}) collective-permute-start(f32[13,32,128]{2,1,0:T(8,128)S(1)} %get-tuple-element.61), channel_id=1, source_target_pairs={{2,4},{6,8},{10,12},{14,16},{18,20},{22,24},{26,28},{4,2},{8,6},{1... | collective-permute-start | bytes 638984 | tf_op jit(solution)/shard_map/ppermute | solution.py:576
  7.5 0.0 collective-permute-done.6.refs_1_
  7.5 2.9 %collective-permute-start.7 = (f32[2,16,16,128]{3,2,1,0:T(8,128)S(1)}, f32[2,16,16,128]{3,2,1,0:T(8,128)S(1)}, u32[]{:S(2)}, u32[]{:S(2)}) collective-permute-start(f32[2,16,16,128]{3,2,1,0:T(8,128)S(1)} %shard_map.81), channel_id=1, source_target_pairs={{0,3},{3,0},{2,5},{5,2},{4,7},{7,4},{6,9},{9,6},{8,11},{11,8},{10,... | collective-permute-start | bytes 786440 | tf_op jit(solution)/shard_map/ppermute | solution.py:595
  10.4 0.0 collective-permute-done.refs_3_
  10.4 2.7 %shard_map.76 = (f32[32,40,128]{2,1,0:T(8,128)S(1)}, f32[32,40,128]{2,1,0:T(8,128)S(1)}, f32[32,40,128]{2,1,0:T(8,128)S(1)}, f32[32,40,128]{2,1,0:T(8,128)S(1)},...) custom-call(f32[32,32,128]{2,1,0:T(8,128)S(1)} %get-tuple-element.43, ...), custom_call_target="tpu_custom_call" | custom-call | tf_op jit(solution)/shard_map/pallas_call | solution.py:552
  13.2 0.0 collective-permute-done.1.ra_ref.refs_16_
  13.2 1.9 %collective-permute-done.2.rb_ref.refs_17_ = f32[13,32,128]{2,1,0:T(8,128)S(1)} collective-permute-done((f32[13,32,128]{2,1,0:T(8,128)S(1)}, f32[13,32,128]{2,1,0:T(8,128)S(1)}, u32[]{:S(2)}, u32[]{:S(2)}) %collective-permute-start.2) | collective-permute-done | bytes 213024 | tf_op jit(solution)/shard_map/ppermute | solution.py:576
  15.1 3.2 %collective-permute-start.3 = (f32[2,13,8,128]{3,2,1,0:T(8,128)S(1)}, f32[2,13,8,128]{3,2,1,0:T(8,128)S(1)}, u32[]{:S(2)}, u32[]{:S(2)}) collective-permute-start(f32[2,13,8,128]{3,2,1,0:T(8,128)S(1)} %shard_map.77), channel_id=1, source_target_pairs={{1,0},{0,1},{3,2},{2,3},{5,4},{4,5},{7,6},{6,7},{9,8},{8,9},{11,10... | collective-permute-start | bytes 319496 | tf_op jit(solution)/shard_map/ppermute | solution.py:585
  18.3 1.0 %collective-permute-done.3.refs_18_ = f32[2,13,8,128]{3,2,1,0:T(8,128)S(1)} collective-permute-done((f32[2,13,8,128]{3,2,1,0:T(8,128)S(1)}, f32[2,13,8,128]{3,2,1,0:T(8,128)S(1)}, u32[]{:S(2)}, u32[]{:S(2)}) %collective-permute-start.3) | collective-permute-done | bytes 106528 | tf_op jit(solution)/shard_map/ppermute | solution.py:585
  19.2 1.2 %shard_map.78 = (f32[10,32,128]{2,1,0:T(8,128)S(1)}, f32[10,32,128]{2,1,0:T(8,128)S(1)}, f32[8,16,128]{2,1,0:T(8,128)S(1)}) custom-call(f32[32,32,128]{2,1,0:T(8,128)S(1)} %get-tuple-element.43.refs_0_, f32[32,32,128]{2,1,0:T(8,128)S(1)} %get-tuple-element.44.refs_1_, f32[32,32,128]{2,1,0:T(8,128)S(1)} %get-tuple-element.45.refs_2_, ...), custom_call_target="tpu_custom_call" | custom-call | tf_op jit(solution)/shard_map/pallas_call | solution.py:552
  20.4 0.4 %collective-permute-start.4 = (f32[8,16,128]{2,1,0:T(8,128)S(1)}, f32[8,16,128]{2,1,0:T(8,128)S(1)}, u32[]{:S(2)}, u32[]{:S(2)}) collective-permute-start(f32[8,16,128]{2,1,0:T(8,128)S(1)} %get-tuple-element.66.refs_0_), channel_id=1, source_target_pairs={{1,0},{0,1},{3,2},{2,3},{5,4},{4,5},{7,6},{6,7},{9,8},{8,9},{11,10... | collective-permute-start | bytes 196616 | tf_op jit(solution)/shard_map/ppermute | solution.py:585
  20.8 0.9 %collective-permute-done.4.refs_1_ = f32[8,16,128]{2,1,0:T(8,128)S(1)} collective-permute-done((f32[8,16,128]{2,1,0:T(8,128)S(1)}, f32[8,16,128]{2,1,0:T(8,128)S(1)}, u32[]{:S(2)}, u32[]{:S(2)}) %collective-permute-start.4) | collective-permute-done | bytes 65568 | tf_op jit(solution)/shard_map/ppermute | solution.py:585
  21.7 0.0 collective-permute-done.7.refs_0_
  21.8 0.4 %collective-permute-start.8 = (f32[2,16,16,128]{3,2,1,0:T(8,128)S(1)}, f32[2,16,16,128]{3,2,1,0:T(8,128)S(1)}, u32[]{:S(2)}, u32[]{:S(2)}) collective-permute-start(f32[2,16,16,128]{3,2,1,0:T(8,128)S(1)} %bitcast.2), channel_id=1, source_target_pairs={{1,0},{0,1},{3,2},{2,3},{5,4},{4,5},{7,6},{6,7},{9,8},{8,9},{11,10... | collective-permute-start | bytes 786440 | tf_op jit(solution)/shard_map/ppermute | solution.py:585
  22.2 1.9 %collective-permute-start.5 = (f32[2,7,16,128]{3,2,1,0:T(8,128)S(1)}, f32[2,7,16,128]{3,2,1,0:T(8,128)S(1)}, u32[]{:S(2)}, u32[]{:S(2)}) collective-permute-start(f32[2,7,16,128]{3,2,1,0:T(8,128)S(1)} %shard_map.80.refs_1_), channel_id=1, source_target_pairs={{0,3},{3,0},{2,5},{5,2},{4,7},{7,4},{6,9},{9,6},{8,11},{11,8},{10,... | collective-permute-start | bytes 344072 | tf_op jit(solution)/shard_map/ppermute | solution.py:595
  24.1 1.0 %shard_map.79 = (f32[32,32,128]{2,1,0:T(8,128)}, f32[32,32,128]{2,1,0:T(8,128)}, f32[8,128]{1,0:T(8,128)S(1)}) custom-call(f32[32,32,128]{2,1,0:T(8,128)S(1)} %get-tuple-element.47.it_in, f32[32,32,128]{2,1,0:T(8,128)S(1)} %get-tuple-element.48.refs_14_.res_in, f32[10,32,128]{2,1,0:T(8,128)S(1)} %get-tuple-element.62.it_rim, ...), custom_call_target="tpu_custom_call" | custom-call | tf_op jit(solution)/shard_map/pallas_call | solution.py:552
  25.1 0.0 collective-permute-done.8.refs_3_
  25.1 2.4 %shard_map.83 = (f32[24,32,128]{2,1,0:T(8,128)S(1)}, f32[24,32,128]{2,1,0:T(8,128)S(1)}, f32[24,32,128]{2,1,0:T(8,128)S(1)}, f32[24,32,128]{2,1,0:T(8,128)S(1)},...) custom-call(f32[16,16,128]{2,1,0:T(8,128)S(1)} %get-tuple-element.67, ...), custom_call_target="tpu_custom_call" | custom-call | tf_op jit(solution)/shard_map/pallas_call | solution.py:552
  27.5 2.2 %collective-permute-done.5.refs_0_ = f32[2,7,16,128]{3,2,1,0:T(8,128)S(1)} collective-permute-done((f32[2,7,16,128]{3,2,1,0:T(8,128)S(1)}, f32[2,7,16,128]{3,2,1,0:T(8,128)S(1)}, u32[]{:S(2)}, u32[]{:S(2)}) %collective-permute-start.5) | collective-permute-done | bytes 114720 | tf_op jit(solution)/shard_map/ppermute | solution.py:595
  29.7 0.6 %collective-permute-start.9 = (f32[2,7,16,128]{3,2,1,0:T(8,128)S(1)}, f32[2,7,16,128]{3,2,1,0:T(8,128)S(1)}, u32[]{:S(2)}, u32[]{:S(2)}) collective-permute-start(f32[2,7,16,128]{3,2,1,0:T(8,128)S(1)} %bitcast.4), channel_id=1, source_target_pairs={{1,0},{0,1},{3,2},{2,3},{5,4},{4,5},{7,6},{6,7},{9,8},{8,9},{11,10... | collective-permute-start | bytes 344072 | tf_op jit(solution)/shard_map/ppermute | solution.py:585
  30.3 1.0 %collective-permute-done.9.refs_3_ = f32[2,7,16,128]{3,2,1,0:T(8,128)S(1)} collective-permute-done((f32[2,7,16,128]{3,2,1,0:T(8,128)S(1)}, f32[2,7,16,128]{3,2,1,0:T(8,128)S(1)}, u32[]{:S(2)}, u32[]{:S(2)}) %collective-permute-start.9) | collective-permute-done | bytes 114720 | tf_op jit(solution)/shard_map/ppermute | solution.py:585
  31.2 3.5 %shard_map.85 = (f32[16,16,64]{2,1,0:T(8,128)}, f32[8,8,32]{2,1,0:T(8,128)}) custom-call(f32[8,16,128]{2,1,0:T(8,128)S(1)} %get-tuple-element.66.refs_0_, f32[8,16,128]{2,1,0:T(8,128)S(1)} %collective-permute-done.4.refs_1_, f32[2,7,16,128]{3,2,1,0:T(8,128)S(1)} %bitcast.5, f32[2,7,16,128]{3,2,1,0:T(8,128)S(1)} %collective-permute-done.9.refs_3_, ...), custom_call_target="tpu_custom_call" | custom-call | tf_op jit(solution)/shard_map/pallas_call | solution.py:552
  (5 shorter events, 0.1 us)
Async XLA Ops:
  2.3 8.1 %collective-permute-start = (f32[3,32,8,128]{3,2,1,0:T(8,128)S(1)}, f32[3,32,8,128]{3,2,1,0:T(8,128)S(1)}, u32[]{:S(2)}, u32[]{:S(2)}) collective-permute-start(f32[3,32,8,128]{3,2,1,0:T(8,128)S(1)} %get-tuple-element.46), channel_id=1, source_target_pairs={{1,0},{0,1},{3,2},{2,3},{5,4},{4,5},{7,6},{6,7},{9,8},{8,9},{11,10... | collective-permute-start | bytes 1179656 | tf_op jit(solution)/shard_map/ppermute | solution.py:585
  3.1 4.4 %collective-permute-start.6 = (f32[16,16,128]{2,1,0:T(8,128)S(1)}, f32[16,16,128]{2,1,0:T(8,128)S(1)}, u32[]{:S(2)}, u32[]{:S(2)}) collective-permute-start(f32[16,16,128]{2,1,0:T(8,128)S(1)} %get-tuple-element.67.refs_0_), channel_id=1, source_target_pairs={{1,0},{0,1},{3,2},{2,3},{5,4},{4,5},{7,6},{6,7},{9,8},{8,9},{11,10... | collective-permute-start | bytes 393224 | tf_op jit(solution)/shard_map/ppermute | solution.py:585
  3.1 10.0 %collective-permute-start.1 = (f32[13,32,128]{2,1,0:T(8,128)S(1)}, f32[13,32,128]{2,1,0:T(8,128)S(1)}, u32[]{:S(2)}, u32[]{:S(2)}) collective-permute-start(f32[13,32,128]{2,1,0:T(8,128)S(1)} %get-tuple-element.60), channel_id=1, source_target_pairs={{0,2},{4,6},{8,10},{12,14},{16,18},{20,22},{24,26},{28,30},{2,0},{... | collective-permute-start | bytes 638984 | tf_op jit(solution)/shard_map/ppermute | solution.py:573
  3.4 11.7 %collective-permute-start.2 = (f32[13,32,128]{2,1,0:T(8,128)S(1)}, f32[13,32,128]{2,1,0:T(8,128)S(1)}, u32[]{:S(2)}, u32[]{:S(2)}) collective-permute-start(f32[13,32,128]{2,1,0:T(8,128)S(1)} %get-tuple-element.61), channel_id=1, source_target_pairs={{2,4},{6,8},{10,12},{14,16},{18,20},{22,24},{26,28},{4,2},{8,6},{1... | collective-permute-start | bytes 638984 | tf_op jit(solution)/shard_map/ppermute | solution.py:576
  7.5 14.2 %collective-permute-start.7 = (f32[2,16,16,128]{3,2,1,0:T(8,128)S(1)}, f32[2,16,16,128]{3,2,1,0:T(8,128)S(1)}, u32[]{:S(2)}, u32[]{:S(2)}) collective-permute-start(f32[2,16,16,128]{3,2,1,0:T(8,128)S(1)} %shard_map.81), channel_id=1, source_target_pairs={{0,3},{3,0},{2,5},{5,2},{4,7},{7,4},{6,9},{9,6},{8,11},{11,8},{10,... | collective-permute-start | bytes 786440 | tf_op jit(solution)/shard_map/ppermute | solution.py:595
  15.1 4.2 %collective-permute-start.3 = (f32[2,13,8,128]{3,2,1,0:T(8,128)S(1)}, f32[2,13,8,128]{3,2,1,0:T(8,128)S(1)}, u32[]{:S(2)}, u32[]{:S(2)}) collective-permute-start(f32[2,13,8,128]{3,2,1,0:T(8,128)S(1)} %shard_map.77), channel_id=1, source_target_pairs={{1,0},{0,1},{3,2},{2,3},{5,4},{4,5},{7,6},{6,7},{9,8},{8,9},{11,10... | collective-permute-start | bytes 319496 | tf_op jit(solution)/shard_map/ppermute | solution.py:585
  20.4 1.3 %collective-permute-start.4 = (f32[8,16,128]{2,1,0:T(8,128)S(1)}, f32[8,16,128]{2,1,0:T(8,128)S(1)}, u32[]{:S(2)}, u32[]{:S(2)}) collective-permute-start(f32[8,16,128]{2,1,0:T(8,128)S(1)} %get-tuple-element.66.refs_0_), channel_id=1, source_target_pairs={{1,0},{0,1},{3,2},{2,3},{5,4},{4,5},{7,6},{6,7},{9,8},{8,9},{11,10... | collective-permute-start | bytes 196616 | tf_op jit(solution)/shard_map/ppermute | solution.py:585
  21.8 3.4 %collective-permute-start.8 = (f32[2,16,16,128]{3,2,1,0:T(8,128)S(1)}, f32[2,16,16,128]{3,2,1,0:T(8,128)S(1)}, u32[]{:S(2)}, u32[]{:S(2)}) collective-permute-start(f32[2,16,16,128]{3,2,1,0:T(8,128)S(1)} %bitcast.2), channel_id=1, source_target_pairs={{1,0},{0,1},{3,2},{2,3},{5,4},{4,5},{7,6},{6,7},{9,8},{8,9},{11,10... | collective-permute-start | bytes 786440 | tf_op jit(solution)/shard_map/ppermute | solution.py:585
  22.2 7.5 %collective-permute-start.5 = (f32[2,7,16,128]{3,2,1,0:T(8,128)S(1)}, f32[2,7,16,128]{3,2,1,0:T(8,128)S(1)}, u32[]{:S(2)}, u32[]{:S(2)}) collective-permute-start(f32[2,7,16,128]{3,2,1,0:T(8,128)S(1)} %shard_map.80.refs_1_), channel_id=1, source_target_pairs={{0,3},{3,0},{2,5},{5,2},{4,7},{7,4},{6,9},{9,6},{8,11},{11,8},{10,... | collective-permute-start | bytes 344072 | tf_op jit(solution)/shard_map/ppermute | solution.py:595
  29.7 1.5 %collective-permute-start.9 = (f32[2,7,16,128]{3,2,1,0:T(8,128)S(1)}, f32[2,7,16,128]{3,2,1,0:T(8,128)S(1)}, u32[]{:S(2)}, u32[]{:S(2)}) collective-permute-start(f32[2,7,16,128]{3,2,1,0:T(8,128)S(1)} %bitcast.4), channel_id=1, source_target_pairs={{1,0},{0,1},{3,2},{2,3},{5,4},{4,5},{7,6},{6,7},{9,8},{8,9},{11,10... | collective-permute-start | bytes 344072 | tf_op jit(solution)/shard_map/ppermute | solution.py:585
